TPU v7x, 256 devices: a whole 4x4x8 slice. The times are simulated.
256 devices in a mesh: table: 32 (over z, x), dp: 8 (over y, core).
Axes of the slice: x: 4, y: 4, z: 8, core: 2. Of those that a mesh axis runs over, the one named last changes fastest.
Arguments:
- table_rows: bfloat16 [65536, 512], P('table'), may hold values from -6 to 6
- item_shard: int32 [8, 8192, 1], P('dp', 'table'), may hold values from 0 to 31; in each aligned block of 256 rows (0 to 255, 256 to 511, ..., all dimensions but the last counted through in order) at most 16 rows name the same one
- item_slot: int32 [8, 8192], P('dp', 'table'), may hold values from 0 to 2047
- seq_lengths: int32 [8, 32, 4], P('dp', 'table'), may hold values from 1 to 128, 256 in all within a row
- cotangent: bfloat16 [8, 8192, 512], P('dp', 'table'), may hold values from -6 to 6
- w_proj: bfloat16 [512, 2048], replicated, may hold values from -0.25 to 0.25
- w_out: bfloat16 [512, 512], replicated, may hold values from -0.25 to 0.25
- norm_gain: float32 [512], replicated, may hold values from 0.5 to 1.5
Outputs:
- layer_out: bfloat16 [8, 8192, 512], P('dp', 'table')
- table_grad: float32 [65536, 512], P(('table', 'dp'))
- step_proj: bfloat16 [512, 2048], replicated
- step_out: bfloat16 [512, 512], replicated
- step_gain: float32 [512], replicated
Inputs may be any that keep to these rules, and one draw needn't show every extreme that they name: `item_shard`: among the 256 tokens of one pack no table shard is named by more than 16 tokens, a bound that some block reaches. `seq_lengths`: the 4 lengths of one pack sum to 256; each pack has one sequence of length 128.
All inputs are finite; a program needn't handle non-finite values.
Results may differ from a plain program's by a relative error of at most 0.015.
Values may be sent and summed in bfloat16 or wider, within the bound.
No kernel may reach another device: no remote copies, remote signals or barrier semaphores. Data moves between devices by JAX's collectives and lax.ppermute only.
A program may use at most 64 MiB of HBM per device.

v0:
```python
import jax
import jax.numpy as jnp
from jax import lax
from jax.sharding import PartitionSpec as P

HEADS = 4
HEAD_DIM = 128


norm_eps = 1e-05
step_eps = 1e-06


def normalize(values):
    centered = values - jnp.mean(values, axis=-1, keepdims=True)
    variance = jnp.mean(centered * centered, axis=-1, keepdims=True)
    return centered * lax.rsqrt(variance + norm_eps)


def input_norm(inputs, norm_gain):
    return normalize(inputs) * norm_gain


def gate_norm(mixed_rows, gate_up):
    return normalize(mixed_rows) * gate_up


def silu_slope(values):
    sigmoid = jax.nn.sigmoid(values)
    return sigmoid * (1.0 + values * (1.0 - sigmoid))


def segment_ids(lengths, tok_count):
    seq_ends = jnp.cumsum(lengths)
    places = jnp.arange(tok_count, dtype=jnp.int32)
    return jnp.sum((seq_ends[None, :] <= places[:, None]).astype(jnp.int32), axis=1)


def rms_scale(square_sum, entries):
    return lax.rsqrt(square_sum / entries + step_eps)


def body(table_rows, item_shard, item_slot, seq_lengths, cotangent, w_proj, w_out, norm_gain):
    shards = lax.axis_size("table")
    tok_count = item_slot.shape[1]
    model_width = table_rows.shape[1]
    inner_width = w_out.shape[0]
    capacity = 2 * tok_count // shards
    targets = item_shard[0, :, 0]
    onehot = (targets[:, None] == jnp.arange(shards, dtype=jnp.int32)[None, :]).astype(jnp.int32)
    slot_rank = jnp.sum((jnp.cumsum(onehot, axis=0) - 1) * onehot, axis=1)
    placed = targets * capacity + slot_rank
    requests = (
        jnp.full((shards * capacity,), -1, jnp.int32)
        .at[placed]
        .set(item_slot[0])
        .reshape(shards, capacity)
    )
    asked_rows = lax.all_to_all(requests, "table", split_axis=0, concat_axis=0, tiled=True)
    is_valid = asked_rows >= 0
    picked = jnp.take(table_rows, jnp.maximum(asked_rows, 0), axis=0)
    picked = jnp.where(is_valid[..., None], picked, jnp.zeros((), jnp.bfloat16))
    returned, asked_rows = (
        lax.all_to_all(picked, "table", split_axis=0, concat_axis=0, tiled=True),
        asked_rows,
    )
    fetched = returned.reshape(shards * capacity, model_width)[placed]
    segments = segment_ids(seq_lengths[0, 0], tok_count)
    positions = jnp.arange(tok_count, dtype=jnp.int32)
    inputs = fetched.astype(jnp.float32)
    normed = input_norm(inputs, norm_gain).astype(jnp.bfloat16)
    pre_act = jnp.dot(normed, w_proj, preferred_element_type=jnp.float32)
    activated = jax.nn.silu(pre_act).astype(jnp.bfloat16)
    gate_up = activated[:, :inner_width]
    shaped = activated[:, inner_width:].reshape(tok_count, 3, HEADS, HEAD_DIM)
    values_all = shaped[:, 0]
    queries_all = shaped[:, 1]
    keys_all = shaped[:, 2]
    query_block = min(512, tok_count)
    blocks = tok_count // query_block
    key_pos = positions[None]
    key_seg = segments[None]
    key_rows = keys_all[None]
    value_rows = values_all[None]
    query_pos = positions.reshape(blocks, query_block)
    query_seg = segments.reshape(blocks, query_block)
    queries = queries_all.reshape(blocks, query_block, HEADS, HEAD_DIM)
    allowed = (
        (key_seg[:, None, :] == query_seg[:, :, None])
        & (key_pos[:, None, :] <= query_pos[:, :, None])
        & (key_pos[:, None, :] >= 0)
    )
    score_scale = HEAD_DIM ** (-0.5)
    scores = (
        jnp.einsum("bqhd,bkhd->bhqk", queries, key_rows, preferred_element_type=jnp.float32)
        * score_scale
    )
    weights = jnp.where(allowed[:, None], jax.nn.silu(scores), 0.0).astype(jnp.bfloat16)
    mixed_rows = jnp.einsum(
        "bhqk,bkhd->bqhd", weights, value_rows, preferred_element_type=jnp.float32
    ).reshape(tok_count, inner_width)
    gated_float, gate_back = jax.vjp(gate_norm, mixed_rows, gate_up.astype(jnp.float32))
    gated_rows = gated_float.astype(jnp.bfloat16)
    layer_rows = (inputs + jnp.dot(gated_rows, w_out, preferred_element_type=jnp.float32)).astype(
        jnp.bfloat16
    )
    upstream = cotangent[0]
    grad_out_w = lax.dot_general(
        gated_rows, upstream, (((0,), (0,)), ((), ())), preferred_element_type=jnp.float32
    )
    grad_gated = lax.dot_general(
        upstream, w_out, (((1,), (1,)), ((), ())), preferred_element_type=jnp.float32
    )
    grad_mixed_float, grad_up = gate_back(grad_gated)
    grad_mixed = grad_mixed_float.astype(jnp.bfloat16).reshape(blocks, query_block, HEADS, HEAD_DIM)
    grad_weights = jnp.einsum(
        "bqhd,bkhd->bhqk", grad_mixed, value_rows, preferred_element_type=jnp.float32
    )
    grad_value_rows = jnp.einsum(
        "bhqk,bqhd->bkhd", weights, grad_mixed, preferred_element_type=jnp.float32
    )
    grad_scores = (
        jnp.where(allowed[:, None], grad_weights * silu_slope(scores), 0.0) * score_scale
    ).astype(jnp.bfloat16)
    grad_queries = jnp.einsum(
        "bhqk,bkhd->bqhd", grad_scores, key_rows, preferred_element_type=jnp.float32
    )
    grad_key_rows = jnp.einsum(
        "bhqk,bqhd->bkhd", grad_scores, queries, preferred_element_type=jnp.float32
    )
    grad_values = jnp.sum(grad_value_rows, axis=0)
    grad_keys = jnp.sum(grad_key_rows, axis=0)
    grad_acted = jnp.concatenate(
        [
            grad_up,
            grad_values.reshape(tok_count, inner_width),
            grad_queries.reshape(tok_count, inner_width),
            grad_keys.reshape(tok_count, inner_width),
        ],
        axis=1,
    )
    grad_pre = (grad_acted * silu_slope(pre_act)).astype(jnp.bfloat16)
    grad_proj_w = lax.dot_general(
        normed, grad_pre, (((0,), (0,)), ((), ())), preferred_element_type=jnp.float32
    )
    grad_normed = lax.dot_general(
        grad_pre, w_proj, (((1,), (1,)), ((), ())), preferred_element_type=jnp.float32
    )
    normed_again, norm_back = jax.vjp(input_norm, inputs, norm_gain)
    grad_inputs, grad_gain = norm_back(grad_normed)
    row_grads = upstream.astype(jnp.float32) + grad_inputs
    sent_grads = (
        jnp.zeros((shards * capacity, model_width), jnp.float32)
        .at[placed]
        .set(row_grads)
        .reshape(shards, capacity, model_width)
    )
    got_grads = lax.all_to_all(
        sent_grads.astype(jnp.bfloat16), "table", split_axis=0, concat_axis=0, tiled=True
    ).astype(sent_grads.dtype)
    flat_slots = asked_rows.reshape(-1)
    got_flat = jnp.where(flat_slots[:, None] >= 0, got_grads.reshape(-1, model_width), 0.0)
    dense_grads = (
        jnp.zeros((table_rows.shape[0], model_width), jnp.float32)
        .at[jnp.maximum(flat_slots, 0)]
        .add(got_flat)
    )
    table_grad = lax.psum_scatter(
        dense_grads.astype(jnp.bfloat16), "dp", scatter_dimension=0, tiled=True
    ).astype(jnp.float32)
    proj_count = grad_proj_w.size
    out_count = grad_out_w.size
    grad_proj_w, grad_out_w, grad_gain = lax.psum(
        (grad_proj_w, grad_out_w, grad_gain), ("table", "dp")
    )
    step_proj = (grad_proj_w * rms_scale(jnp.sum(grad_proj_w * grad_proj_w), proj_count)).astype(
        jnp.bfloat16
    )
    step_out = (grad_out_w * rms_scale(jnp.sum(grad_out_w * grad_out_w), out_count)).astype(
        jnp.bfloat16
    )
    step_gain = grad_gain * rms_scale(jnp.sum(grad_gain * grad_gain), grad_gain.size)
    return (layer_rows[None], table_grad, step_proj, step_out, step_gain)


def solution(mesh):
    placed = (
        P("table", None),
        P("dp", "table", None),
        P("dp", "table"),
        P("dp", "table", None),
        P("dp", "table", None),
        P(),
        P(),
        P(),
    )
    return jax.shard_map(
        body,
        mesh=mesh,
        in_specs=placed,
        out_specs=(P("dp", "table", None), P(("table", "dp"), None), P(), P(), P()),
        check_vma=False,
    )
```

profile of v0, /device:TPU:1, one launch (start us, length us, event | category | flops | bytes accessed | tf_op | source)
XLA Modules:
  0.0 383.0 jit_solution(2942318096052476566)
XLA Ops:
  11.1 1.6 scatter_custom_fusion
  12.8 20.2 %all_to_all.19 = s32[32,1,16]{2,1,0:T(1,128)S(1)} all-to-all(s32[32,1,16]{2,1,0:T(1,128)S(1)} %bitcast.127), channel_id=1, replica_groups=mesh['table'=32,'dp'=8] {'table'}, dimensions={0} | all-to-all | bytes 4096 | tf_op jit(solution)/shard_map/all_to_all | solution.py:59
  33.4 3.9 %gather_fusion = bf16[512,512]{1,0:T(8,128)(2,1)S(1)} fusion(bf16[2048,512]{1,0:T(8,128)(2,1)} %param.8, s32[1024]{0:T(1024)S(1)} %pad_clamp_fusion.1), kind=kCustom, calls=%fused_computation | custom fusion | bytes 1050624 | tf_op jit(solution)/shard_map/jit(_take)/gather | solution.py:61
  37.3 1.0 select_select_fusion
  38.3 4.0 %all-to-all-start.1 = ((bf16[32,16,512]{2,1,0:T(8,128)(2,1)}), bf16[32,16,512]{2,1,0:T(8,128)(2,1)S(1)}, u32[]{:S(2)}, u32[]{:S(2)}) async-start(bf16[32,16,512]{2,1,0:T(8,128)(2,1)} %select_select_fusion), calls=%async_computation.1 | async-start | bytes 1048576 | tf_op jit(solution)/shard_map/all_to_all | solution.py:64
  42.9 14.0 %all-to-all-done.1 = bf16[32,16,512]{2,1,0:T(8,128)(2,1)S(1)} async-done(((bf16[32,16,512]{2,1,0:T(8,128)(2,1)}), bf16[32,16,512]{2,1,0:T(8,128)(2,1)S(1)}, u32[]{:S(2)}, u32[]{:S(2)}) %all-to-all-start.1) | async-done | bytes 524320 | tf_op jit(solution)/shard_map/all_to_all | solution.py:64
  57.0 1.2 gather_fusion.1
  58.5 2.1 multiply_convert_fusion.1
  62.6 1.7 reshape.353
  64.4 1.1 fusion.59
  65.5 1.2 copy.99
  66.7 2.6 select_convert_fusion
  70.4 1.7 multiply_reduce_fusion.2
  72.1 2.1 fusion.58
  76.3 1.2 fusion.29
  77.4 1.0 copy.98
  78.4 1.0 copy.97
  79.4 2.1 copy.96
  81.5 3.0 fusion
  84.5 2.8 fusion.53
  87.3 1.3 fusion.32
  90.3 2.5 scatter_custom_fusion.1
  93.6 6.3 %all-to-all-start.2 = ((bf16[32,16,512]{2,1,0:T(8,128)(2,1)}), bf16[32,16,512]{2,1,0:T(8,128)(2,1)S(1)}, u32[]{:S(2)}, u32[]{:S(2)}) async-start(bf16[32,16,512]{2,1,0:T(8,128)(2,1)} %bitcast.121), calls=%async_computation.2 | async-start | bytes 1048576 | tf_op jit(solution)/shard_map/all_to_all | solution.py:158
  100.4 15.7 %all-to-all-done.2 = bf16[32,16,512]{2,1,0:T(8,128)(2,1)S(1)} async-done(((bf16[32,16,512]{2,1,0:T(8,128)(2,1)}), bf16[32,16,512]{2,1,0:T(8,128)(2,1)S(1)}, u32[]{:S(2)}, u32[]{:S(2)}) %all-to-all-start.2) | async-done | bytes 524320 | tf_op jit(solution)/shard_map/all_to_all | solution.py:158
  116.1 5.9 %scatter_custom_fusion.2 = f32[2048,512]{1,0:T(8,128)} fusion(s32[512]{0:T(512)S(1)} %reshape.370, f32[]{:T(128)} %constant.71.clone.1, bf16[512,512]{1,0:T(8,128)(2,1)S(1)} %bitcast.126, pred[512]{0:T(512)(128)(4,1)S(1)} %ge.31), kind=kCustom, calls=%fused_computation.9 | custom fusion | flops 786432 | bytes 4720128 | tf_op jit(solution)/shard_map/scatter-add | solution.py:166
  122.1 3.8 %convert_element_type.77 = bf16[2048,512]{1,0:T(8,128)(2,1)} convert(f32[2048,512]{1,0:T(8,128)} %scatter_custom_fusion.2) | non-fusion elementwise | flops 1048576 | bytes 6291456 | tf_op jit(solution)/shard_map/convert_element_type | solution.py:169
  125.9 79.3 %psum.23 = f32[512]{0:T(512)S(1)} all-reduce(f32[512]{0:T(512)S(1)} %get-tuple-element.5), channel_id=1, replica_groups=mesh['table'=32,'dp'=8] {'table','dp'}, use_global_device_ids=true, to_apply=%region_22.23 | all-reduce | flops 512 | bytes 4096 | tf_op jit(solution)/shard_map/psum | solution.py:173
  206.6 1.0 fusion.7
  208.1 154.4 %all-reduce.3.cloned.1.call-done = (f32[512,2048]{1,0:T(8,128)}, f32[512,512]{1,0:T(8,128)}) async-done(((f32[512,2048]{1,0:T(8,128)}, f32[512,512]{1,0:T(8,128)}), (f32[512,2048]{1,0:T(8,128)}, f32[512,512]{1,0:T(8,128)})) %all-reduce.3.cloned.1.call-update) | async-done | bytes 5242896 | tf_op jit(solution)/shard_map/psum | solution.py:173
  362.6 4.0 %multiply_reduce_fusion = f32[]{:T(128)} fusion(f32[512,2048]{1,0:T(8,128)} %get-tuple-element.7), kind=kLoop, calls=%fused_computation.6 | loop fusion | flops 2097151 | bytes 4194308 | tf_op jit(solution)/shard_map/reduce_sum | solution.py:176
  369.7 4.0 %multiply_convert_fusion = bf16[512,2048]{1,0:T(8,128)(2,1)} fusion(f32[512,2048]{1,0:T(8,128)} %get-tuple-element.7, f32[]{:T(128)S(6)} %rsqrt.32), kind=kLoop, calls=%fused_computation.5 | loop fusion | flops 2097152 | bytes 6291460 | tf_op jit(solution)/shard_map/convert_element_type | solution.py:176
  373.7 1.8 convert_element_type.78
  (86 shorter events, 15.6 us)
Async XLA Ops:
  8.0 50.5 %copy-start = (bf16[512,2048]{1,0:T(8,128)(2,1)S(1)}, bf16[512,2048]{1,0:T(8,128)(2,1)}, u32[]{:S(2)}) copy-start(bf16[512,2048]{1,0:T(8,128)(2,1)} %param.13) | copy-start | bytes 6291460
  37.3 5.3 %copy-start.16 = (s32[1,1,4]{2,1,0:T(1,128)S(1)}, s32[1,1,4]{2,1,0:T(1,128)}, u32[]{:S(2)}) copy-start(s32[1,1,4]{2,1,0:T(1,128)} %param.11) | copy-start | bytes 52
  38.3 20.2 %copy-start.15 = (f32[512]{0:T(512)S(1)}, f32[512]{0:T(512)}, u32[]{:S(2)}) copy-start(f32[512]{0:T(512)} %param.15) | copy-start | bytes 6148
  38.3 18.7 %all-to-all-start.1 = ((bf16[32,16,512]{2,1,0:T(8,128)(2,1)}), bf16[32,16,512]{2,1,0:T(8,128)(2,1)S(1)}, u32[]{:S(2)}, u32[]{:S(2)}) async-start(bf16[32,16,512]{2,1,0:T(8,128)(2,1)} %select_select_fusion), calls=%async_computation.1 | async-start | bytes 1048576 | tf_op jit(solution)/shard_map/all_to_all | solution.py:64
  42.3 320.3 %all-reduce.3.cloned.1.call-start = ((), (), s32[]{:S(2)}) async-start(), calls=%async_computation.5 | async-start | bytes 10485760 | tf_op jit(solution)/shard_map/psum | solution.py:173
  60.6 1.0 copy-start.9
  65.5 3.8 copy-start.10
  66.7 2.6 copy-start.13
  69.3 0.8 copy-start.6
  70.4 3.9 %copy-start.14 = (bf16[256,1,4,128]{0,3,2,1:T(8,128)(2,1)S(1)}, bf16[256,1,4,128]{0,3,2,1:T(8,128)(2,1)}, u32[]{:S(2)}) copy-start(bf16[256,1,4,128]{0,3,2,1:T(8,128)(2,1)} %copy-done.13) | copy-start | bytes 786436
  70.4 3.9 %copy-start.17 = (f32[4,256,256]{2,1,0:T(8,128)S(1)}, f32[4,256,256]{2,1,0:T(8,128)}, u32[]{:S(2)}) copy-start(f32[4,256,256]{2,1,0:T(8,128)} %get-tuple-element.23) | copy-start | bytes 3145732
  74.3 1.0 copy-start.12
  74.3 1.2 copy-start.11
  75.2 1.1 copy-start.7
  84.5 2.9 copy-start.2
  84.5 2.9 copy-start.4
  89.5 0.8 copy-start.8
  93.6 22.5 %all-to-all-start.2 = ((bf16[32,16,512]{2,1,0:T(8,128)(2,1)}), bf16[32,16,512]{2,1,0:T(8,128)(2,1)S(1)}, u32[]{:S(2)}, u32[]{:S(2)}) async-start(bf16[32,16,512]{2,1,0:T(8,128)(2,1)} %bitcast.121), calls=%async_computation.2 | async-start | bytes 1048576 | tf_op jit(solution)/shard_map/all_to_all | solution.py:158
  99.9 273.8 %reduce-scatter.2.cloned.1.call-start = ((), (), s32[]{:S(2)}) async-start(), calls=%async_computation.4 | async-start | bytes 2359296 | tf_op jit(solution)/shard_map/reduce_scatter | solution.py:168
  125.9 80.6 %copy-start.3 = (bf16[256,512]{1,0:T(8,128)(2,1)S(1)}, bf16[256,512]{1,0:T(8,128)(2,1)}, u32[]{:S(2)}) copy-start(bf16[256,512]{1,0:T(8,128)(2,1)} %get-tuple-element.11) | copy-start | bytes 786436
  125.9 80.6 %copy-start.5 = (bf16[512,512]{1,0:T(8,128)(2,1)S(1)}, bf16[512,512]{1,0:T(8,128)(2,1)}, u32[]{:S(2)}) copy-start(bf16[512,512]{1,0:T(8,128)(2,1)} %param.14) | copy-start | bytes 1572868
  362.6 4.7 %copy-start.1 = (f32[512,512]{1,0:T(8,128)S(1)}, f32[512,512]{1,0:T(8,128)}, u32[]{:S(2)}) copy-start(f32[512,512]{1,0:T(8,128)} %get-tuple-element.8) | copy-start | bytes 3145732
Sparse Core Ops, SparseCore 0:
  88.8 273.7 all-reduce.2
Sparse Core Ops, SparseCore 1:
  126.0 34.9 reduce-scatter.1
where the time goes:
time: 385 us; the launch traced here: 383 us
  waiting for transfers between devices  184 us (48%)
  blocking collectives  99.5 us (26%)
  other arithmetic  36 us (9%)
  local copies, waits for them, and re-layouts  19.4 us (5%)
  between operations  17.8 us (5%)
  matrix products  15.1 us (4%)
  starting transfers between devices  10.8 us (3%)
    psum x1, waiting for transfers between devices, body(): lax.psum((grad_proj_w, grad_out_w, grad_gain), ('table', 'dp'))  154 us
    psum x1, blocking collectives, body(): lax.psum((grad_proj_w, grad_out_w, grad_gain), ('table', 'dp'))  79.3 us
    all_to_all x1, blocking collectives, body(): lax.all_to_all(requests, 'table', split_axis=0, concat_axis=0, tiled=True)  20.2 us
    all_to_all x1, waiting for transfers between devices, body(): lax.all_to_all(sent_grads.astype(jnp.bfloat16), 'table', split_axis=0, co...  15.7 us
    all_to_all x1, waiting for transfers between devices, body(): lax.all_to_all(picked, 'table', split_axis=0, concat_axis=0, tiled=True)  14 us
  transfers between devices with their start and end apart: 4, of which 3 were waited for; matrix products, arithmetic and copies ran while one was open for 7% of the time, Pallas kernels for 0%

commit v1 on v0

v1 whole, which is shorter than its diff:
```python
import jax
import jax.numpy as jnp
from jax import lax
from jax.experimental import pallas as pl
from jax.experimental.pallas import tpu as pltpu
from jax.sharding import PartitionSpec as P

HEADS = 4
HEAD_DIM = 128
NORM_EPS = 1e-05
STEP_EPS = 1e-06
BOTH = ("table", "dp")
F32 = jnp.float32
BF16 = jnp.bfloat16
LANES = 128
VMEM = pl.BlockSpec(memory_space=pltpu.VMEM)
SMEM = pl.BlockSpec(memory_space=pltpu.SMEM)


def call(kernel, outs, *operands, specs=None, flops=0, transcendentals=0, scratch=()):
    moved = sum(v.size * v.dtype.itemsize for v in operands)
    moved += sum(v.size * v.dtype.itemsize for v in outs)
    return pl.pallas_call(
        kernel,
        out_shape=outs,
        in_specs=specs if specs is not None else [VMEM] * len(operands),
        out_specs=[VMEM] * len(outs),
        scratch_shapes=list(scratch),
        cost_estimate=pl.CostEstimate(
            flops=flops, bytes_accessed=moved, transcendentals=transcendentals
        ),
        compiler_params=pltpu.CompilerParams(vmem_limit_bytes=40 * 1024 * 1024),
    )(*operands)


def shape(dims, dtype):
    return jax.ShapeDtypeStruct(dims, dtype)


def nn(a, b):
    return jnp.dot(a, b, preferred_element_type=F32)


def nt(a, b):
    return lax.dot_general(a, b, (((1,), (1,)), ((), ())), preferred_element_type=F32)


def tn(a, b):
    return lax.dot_general(a, b, (((0,), (0,)), ((), ())), preferred_element_type=F32)


def iota(dims, axis):
    return lax.broadcasted_iota(jnp.int32, dims, axis)


def flag(mask):
    return jnp.where(mask, 1.0, 0.0).astype(BF16)


def request_kernel(shard_ref, slot_ref, request_ref, placed_ref):
    shards, capacity = request_ref.shape
    tokens = slot_ref.shape[1]
    target = shard_ref[...]
    named = target == iota((shards, tokens), 0)
    earlier = flag(iota((tokens, tokens), 0) < iota((tokens, tokens), 1))
    counts = nn(flag(named), earlier)
    rank = jnp.sum(jnp.where(named, counts, 0.0), axis=0, keepdims=True).astype(jnp.int32)
    placed_ref[...] = target * capacity + rank
    wanted = slot_ref[...] + 1
    at_rank = rank == iota((capacity, tokens), 0)
    high = jnp.where(at_rank, wanted // 64, 0).astype(F32).astype(BF16)
    low = jnp.where(at_rank, wanted % 64, 0).astype(F32).astype(BF16)
    picked = nt(flag(named), high) * 64.0 + nt(flag(named), low)
    request_ref[...] = picked.astype(jnp.int32) - 1


def halves(values):
    shifted = values + 1
    high = (shifted // 64).astype(F32).astype(BF16)
    low = (shifted % 64).astype(F32).astype(BF16)
    return high, low


def pick_kernel(asked_ref, table_ref, out_ref):
    shards, capacity = asked_ref.shape
    slots = shards * capacity
    rows = table_ref.shape[0]
    high, low = halves(asked_ref[...])
    owner = flag(iota((slots, shards), 0) // capacity == iota((slots, shards), 1))
    spread = nn(owner, high) * 64.0 + nn(owner, low)
    mine = iota((slots, capacity), 0) % capacity == iota((slots, capacity), 1)
    wanted = jnp.sum(jnp.where(mine, spread, 0.0), axis=1, keepdims=True).astype(jnp.int32) - 1
    for start in range(0, slots, 256):
        hits = flag(wanted[start : start + 256] == iota((256, rows), 1))
        out_ref[pl.ds(start, 256), :] = nn(hits, table_ref[...]).astype(BF16)


def dense_kernel(asked_ref, got_ref, out_ref):
    shards, capacity = asked_ref.shape
    slots = shards * capacity
    rows = out_ref.shape[0]
    high, low = halves(asked_ref[...])
    column = flag(iota((capacity, slots), 0) == iota((capacity, slots), 1) % capacity)
    spread = nn(high, column) * 64.0 + nn(low, column)
    mine = iota((shards, slots), 0) == iota((shards, slots), 1) // capacity
    wanted = jnp.sum(jnp.where(mine, spread, 0.0), axis=0, keepdims=True).astype(jnp.int32) - 1
    got = got_ref[...]
    for start in range(0, rows, 256):
        hits = flag(wanted == iota((256, slots), 0) + start)
        out_ref[pl.ds(start, 256), :] = nn(hits, got).astype(BF16)


def centered_norm(values):
    centered = values - jnp.mean(values, axis=-1, keepdims=True)
    inverse = lax.rsqrt(jnp.mean(centered * centered, axis=-1, keepdims=True) + NORM_EPS)
    return centered * inverse, inverse


def norm_slope(grads, normed, inverse):
    return inverse * (
        grads
        - jnp.mean(grads, axis=-1, keepdims=True)
        - normed * jnp.mean(grads * normed, axis=-1, keepdims=True)
    )


def layer_kernel(
    lengths_ref, returned_ref, placed_ref, upstream_ref, w_proj_ref, w_out_ref, gain_ref,
    layer_ref, sent_ref, grads_ref, slope_ref, acted_ref, grad_pre_ref,
):
    slots = returned_ref.shape[0]
    tokens, width = upstream_ref.shape
    inner = w_out_ref.shape[0]
    placed = placed_ref[...]
    eye = iota((tokens, tokens), 0) == iota((tokens, tokens), 1)
    placed_col = jnp.sum(jnp.where(eye, placed, 0), axis=1, keepdims=True)
    inputs = nn(flag(placed_col == iota((tokens, slots), 1)), returned_ref[...])
    gain = gain_ref[...]
    hat, inverse = centered_norm(inputs)
    normed = (hat * gain).astype(BF16)
    for block in range(4):
        cols = pl.ds(block * inner, inner)
        pre = nn(normed, w_proj_ref[:, cols])
        sig = jax.nn.sigmoid(pre)
        acted_ref[:, cols] = (pre * sig).astype(BF16)
        slope_ref[:, cols] = sig * (1.0 + pre * (1.0 - sig))
    query_pos = iota((tokens, tokens), 0)
    key_pos = iota((tokens, tokens), 1)
    start_of = jnp.zeros((tokens, 1), jnp.int32)
    query_col = iota((tokens, 1), 0)
    end = jnp.int32(0)
    for i in range(lengths_ref.shape[1]):
        end = end + lengths_ref[0, i]
        start_of = jnp.where(query_col >= end, end, start_of)
    allowed = (key_pos <= query_pos) & (key_pos >= start_of)
    scale = HEAD_DIM ** (-0.5)

    def head(block, h):
        return acted_ref[:, pl.ds(block * inner + h * HEAD_DIM, HEAD_DIM)]

    mixed, weights, slopes = [], [], []
    for h in range(HEADS):
        scores = nt(head(2, h), head(3, h)) * scale
        sig = jax.nn.sigmoid(scores)
        weight = jnp.where(allowed, scores * sig, 0.0).astype(BF16)
        slopes.append(jnp.where(allowed, sig * (1.0 + scores * (1.0 - sig)), 0.0))
        weights.append(weight)
        mixed.append(nn(weight, head(1, h)))
    mixed_hat, mixed_inverse = centered_norm(jnp.concatenate(mixed, axis=1))
    gate = acted_ref[:, pl.ds(0, inner)].astype(F32)
    gated = (mixed_hat * gate).astype(BF16)
    layer_ref[...] = (inputs + nn(gated, w_out_ref[...])).astype(BF16)
    upstream = upstream_ref[...]
    grad_gated = nt(upstream, w_out_ref[...])
    grad_mixed = norm_slope(grad_gated * gate, mixed_hat, mixed_inverse).astype(BF16)

    def put(block, h, value):
        cols = pl.ds(block * inner + h * HEAD_DIM, HEAD_DIM)
        grad_pre_ref[:, cols] = (value * slope_ref[:, cols]).astype(BF16)

    grad_pre_ref[:, pl.ds(0, inner)] = (
        grad_gated * mixed_hat * slope_ref[:, pl.ds(0, inner)]
    ).astype(BF16)
    for h in range(HEADS):
        part = grad_mixed[:, h * HEAD_DIM : (h + 1) * HEAD_DIM]
        grad_scores = (nt(part, head(1, h)) * slopes[h] * scale).astype(BF16)
        put(1, h, tn(weights[h], part))
        put(2, h, nn(grad_scores, head(3, h)))
        put(3, h, tn(grad_scores, head(2, h)))
    grad_normed = nt(grad_pre_ref[...], w_proj_ref[...])
    grad_gain = jnp.sum(grad_normed * hat, axis=0, keepdims=True)
    row_grads = (
        upstream.astype(F32) + norm_slope(grad_normed * gain, hat, inverse)
    ).astype(BF16)
    sent_ref[...] = nn(flag(placed == iota((slots, tokens), 0)), row_grads).astype(BF16)

    half = grads_ref.shape[1] - 16
    per_half = half // width
    normed_t = normed.T
    gated_t = gated.T
    blocks = (4 * inner + width) // LANES
    for pair in range(0, blocks, 2):
        start = pair * LANES
        if start < 4 * inner:
            value = nn(normed_t, grad_pre_ref[:, pl.ds(start, 2 * LANES)])
        else:
            value = nn(gated_t, upstream_ref[:, pl.ds(start - 4 * inner, 2 * LANES)])
        for k in range(2):
            side, place = divmod(pair + k, per_half)
            grads_ref[side, pl.ds(place * width, width), :] = value[
                :, k * LANES : (k + 1) * LANES
            ].astype(BF16)
    tail = gain_tail(
        jnp.concatenate(
            [grad_gain[:, k * LANES : (k + 1) * LANES] for k in range(width // LANES)], axis=0
        )
    )
    for side in range(2):
        grads_ref[side, pl.ds(half, 16), :] = tail


def gain_tail(grad_gain):
    high = grad_gain.astype(BF16).astype(F32)
    low = grad_gain - high
    return jnp.concatenate([high, low, jnp.zeros((8, LANES), F32)], axis=0).astype(BF16)


def merge_kernel(in_ref, out_ref):
    parts = in_ref.shape[0]
    rows = in_ref.shape[1] - 16
    pieces, size, _ = out_ref.shape
    chunk = rows // pieces

    def total(start, count):
        value = in_ref[0, pl.ds(start, count), :].astype(F32)
        for i in range(1, parts):
            value = value + in_ref[i, pl.ds(start, count), :].astype(F32)
        return value

    tail = total(rows, 16)
    tail = gain_tail(tail[0:4] + tail[4:8]).astype(F32)
    whole = size == chunk + 16
    for p in range(pieces):
        if whole:
            out_ref[p, pl.ds(0, chunk), :] = total(p * chunk, chunk).astype(BF16)
            out_ref[p, pl.ds(chunk, 16), :] = tail.astype(BF16)
        elif p % 2 == 0:
            two = total(p * chunk, 2 * chunk)
            for k in range(2):
                piece = jnp.concatenate([two[k * chunk : (k + 1) * chunk], tail[0:8]], axis=0)
                out_ref[p + k] = piece.astype(BF16)


def turn_kernel(in_ref, spread_ref, gain_ref):
    total = jnp.sum(in_ref[...].astype(F32), axis=0)
    rows = spread_ref.shape[1]
    mine = total[0:rows].astype(BF16)
    for p in range(spread_ref.shape[0]):
        spread_ref[p] = mine
    gain = total[rows : rows + 4] + total[rows + 4 : rows + 8]
    scale = lax.rsqrt(jnp.sum(gain * gain) / gain.size + STEP_EPS)
    gain_ref[...] = gain * scale


def finish_kernel(grads_ref, proj_ref, out_ref):
    rows = proj_ref.shape[0]
    proj_blocks = proj_ref.shape[1] // LANES
    out_blocks = out_ref.shape[1] // LANES

    def squares(first, count):
        total = jnp.zeros((8, LANES), F32)
        for b in range(first, first + count):
            value = grads_ref[pl.ds(b * rows, rows), :].astype(F32)
            total = total + jnp.sum((value * value).reshape(rows // 8, 8, LANES), axis=0)
        return jnp.sum(total)

    proj_scale = lax.rsqrt(squares(0, proj_blocks) / proj_ref.size + STEP_EPS)
    out_scale = lax.rsqrt(squares(proj_blocks, out_blocks) / out_ref.size + STEP_EPS)
    for b in range(proj_blocks + out_blocks):
        value = grads_ref[pl.ds(b * rows, rows), :].astype(F32)
        if b < proj_blocks:
            proj_ref[:, pl.ds(b * LANES, LANES)] = (value * proj_scale).astype(BF16)
        else:
            cols = pl.ds((b - proj_blocks) * LANES, LANES)
            out_ref[:, cols] = (value * out_scale).astype(BF16)


ZS, XS, YS = 8, 4, 4


def device(z, x, y, c):
    return (z * XS + x) * (2 * YS) + y * 2 + c


CORE_GROUPS = [
    [device(z, x, y, c) for c in range(2)] for z in range(ZS) for x in range(XS) for y in range(YS)
]
FIRST_GROUPS = [
    [device(z, x, y, 0) for x in range(XS)] for z in range(ZS) for y in range(YS)
] + [[device(z, x, y, 1) for y in range(YS)] for z in range(ZS) for x in range(XS)]
SECOND_GROUPS = [
    [device(z, x, y, 0) for y in range(YS)] for z in range(ZS) for x in range(XS)
] + [[device(z, x, y, 1) for x in range(XS)] for z in range(ZS) for y in range(YS)]
LAST_GROUPS = [
    [device(z, x, y, c) for z in range(ZS)]
    for x in range(XS)
    for y in range(YS)
    for c in range(2)
]


def swap(values, groups):
    return lax.all_to_all(
        values, BOTH, split_axis=0, concat_axis=0, tiled=True, axis_index_groups=groups
    )


def spread(values, groups):
    count = len(groups[0])
    return swap(jnp.broadcast_to(values[None], (count, *values.shape)), groups).reshape(
        count * values.shape[0], values.shape[1]
    )


def body(table_rows, item_shard, item_slot, seq_lengths, cotangent, w_proj, w_out, norm_gain):
    shards = lax.axis_size("table")
    tokens = item_slot.shape[1]
    width = table_rows.shape[1]
    inner = w_out.shape[0]
    capacity = 2 * tokens // shards
    slots = shards * capacity
    requests, placed = call(
        request_kernel,
        [shape((shards, capacity), jnp.int32), shape((1, tokens), jnp.int32)],
        item_shard.reshape(1, tokens),
        item_slot,
    )
    asked = lax.all_to_all(requests, "table", split_axis=0, concat_axis=0, tiled=True)
    (picked,) = call(
        pick_kernel,
        [shape((slots, width), BF16)],
        asked,
        table_rows,
        flops=2 * slots * width * table_rows.shape[0],
    )
    returned = lax.all_to_all(
        picked.reshape(shards, capacity, width), "table", split_axis=0, concat_axis=0, tiled=True
    ).reshape(slots, width)
    half = width * (4 * inner + width) // (2 * LANES)
    layer_rows, sent, grads = call(
        layer_kernel,
        [
            shape((tokens, width), BF16),
            shape((slots, width), BF16),
            shape((2, half + 16, LANES), BF16),
        ],
        seq_lengths[0],
        returned,
        placed,
        cotangent[0],
        w_proj,
        w_out,
        norm_gain.reshape(1, width),
        specs=[SMEM] + [VMEM] * 6,
        flops=6 * tokens * width * (4 * inner + width),
        transcendentals=tokens * (4 * inner + HEADS * tokens),
        scratch=[
            pltpu.VMEM((tokens, 4 * inner), F32),
            pltpu.VMEM((tokens, 4 * inner), BF16),
            pltpu.VMEM((tokens, 4 * inner), BF16),
        ],
    )
    got = lax.all_to_all(
        sent.reshape(shards, capacity, width), "table", split_axis=0, concat_axis=0, tiled=True
    ).reshape(slots, width)
    (dense,) = call(
        dense_kernel,
        [shape(table_rows.shape, BF16)],
        asked,
        got,
        flops=2 * slots * width * table_rows.shape[0],
    )
    table_grad = lax.psum_scatter(dense, "dp", scatter_dimension=0, tiled=True).astype(F32)

    grads = swap(grads, CORE_GROUPS)
    (grads,) = call(merge_kernel, [shape((4, half // 4 + 16, LANES), BF16)], grads)
    grads = swap(grads, FIRST_GROUPS)
    (grads,) = call(merge_kernel, [shape((4, half // 16 + 16, LANES), BF16)], grads)
    grads = swap(grads, SECOND_GROUPS)
    (grads,) = call(merge_kernel, [shape((8, half // 128 + 8, LANES), BF16)], grads)
    grads = swap(grads, LAST_GROUPS)
    grads, step_gain = call(
        turn_kernel,
        [shape((8, half // 128, LANES), BF16), shape((width // LANES, LANES), F32)],
        grads,
    )
    grads = swap(grads, LAST_GROUPS).reshape(half // 16, LANES)
    grads = spread(grads, SECOND_GROUPS)
    grads = spread(grads, FIRST_GROUPS)
    grads = spread(grads, CORE_GROUPS)
    step_proj, step_out = call(
        finish_kernel, [shape(w_proj.shape, BF16), shape(w_out.shape, BF16)], grads
    )
    return (layer_rows[None], table_grad, step_proj, step_out, step_gain.reshape(width))


def solution(mesh):
    placed = (
        P("table", None),
        P("dp", "table", None),
        P("dp", "table"),
        P("dp", "table", None),
        P("dp", "table", None),
        P(),
        P(),
        P(),
    )
    return jax.shard_map(
        body,
        mesh=mesh,
        in_specs=placed,
        out_specs=(P("dp", "table", None), P(("table", "dp"), None), P(), P(), P()),
        check_vma=False,
    )
```

time: 385 us -> 184 us (0.48)
  waiting for transfers between devices: 184 us -> 0.02 us
  blocking collectives: 99.5 us -> 150 us
  other arithmetic: 36 us -> 1.8 us
  matrix products: 15.1 us -> 0 us
  local copies, waits for them, and re-layouts: 19.4 us -> 4.66 us
  Pallas kernels: 0 us -> 13.2 us
  starting transfers between devices: 10.8 us -> 0.04 us
    psum x1 -> x0, waiting for transfers between devices: 154 us -> none  [body(): lax.psum((grad_proj_w, grad_out_w, grad_gain), ('table', 'dp'))]
    all_to_all x0 -> x10, blocking collectives: none -> 129 us  [the longest x8 91.1 us: swap(): lax.all_to_all(values, BOTH, split_axis=0, concat_axis=0, tiled=True, axi...]
    psum x1 -> x0, blocking collectives: 79.3 us -> none  [body(): lax.psum((grad_proj_w, grad_out_w, grad_gain), ('table', 'dp'))]
    all_to_all x2 -> x0, waiting for transfers between devices: 29.8 us -> none  [the longest x1 15.7 us: body(): lax.all_to_all(sent_grads.astype(jnp.bfloat16), 'table', split_axis=0, co...]
    dot_general x12 -> x0, matrix products: 15.1 us -> none  [the longest x1 2.84 us: body(): lax.dot_general(normed, grad_pre, (((0,), (0,)), ((), ())), preferred_ele...]
    convert_element_type x7 -> x1, other arithmetic: 15.2 us -> 1.8 us  [body(): lax.psum_scatter(dense, 'dp', scatter_dimension=0, tiled=True).astype(F32)]
    pallas_call x0 -> x9, Pallas kernels: none -> 13.2 us  [call(): pl.pallas_call(kernel, out_shape=outs, in_specs=specs if specs is not Non...]
    all_to_all x2 -> x0, starting transfers between devices: 10.3 us -> none  [the longest x1 6.29 us: body(): lax.all_to_all(sent_grads.astype(jnp.bfloat16), 'table', split_axis=0, co...]
  transfers between devices with their start and end apart: 4 -> 1, of which waited for: 3 -> 0; matrix products, arithmetic and copies ran while one was open for 7% -> 0% of each run, Pallas kernels for 0% -> 2%
where the time goes in v1:
time: 184 us; the launch traced here: 183 us
  blocking collectives  150 us (82%)
  between operations  14.1 us (8%)
  Pallas kernels  13.2 us (7%)
  local copies, waits for them, and re-layouts  4.66 us (3%)
    all_to_all x8, blocking collectives, swap(): lax.all_to_all(values, BOTH, split_axis=0, concat_axis=0, tiled=True, axi...  91.1 us
    all_to_all x1, blocking collectives, body(): lax.all_to_all(sent.reshape(shards, capacity, width), 'table', split_axis...  20.6 us
    all_to_all x1, blocking collectives, body(): lax.all_to_all(requests, 'table', split_axis=0, concat_axis=0, tiled=True)  20.2 us
    all_to_all x1, blocking collectives, body(): lax.all_to_all(picked.reshape(shards, capacity, width), 'table', split_ax...  17.6 us
    pallas_call x9, Pallas kernels, call(): pl.pallas_call(kernel, out_shape=outs, in_specs=specs if specs is not Non...  13.2 us
    unnamed x18, local copies, waits for them, and re-layouts  4.28 us
  transfers between devices with their start and end apart: 1, of which 0 were waited for; matrix products, arithmetic and copies ran while one was open for 0% of the time, Pallas kernels for 2%

profile of v1, /device:TPU:1, one launch (start us, length us, event | category | flops | bytes accessed | tf_op | source)
XLA Modules:
  0.0 183.4 jit_solution(15972971861275197385)
XLA Ops:
  7.2 0.0 reduce-scatter.2.cloned.1.call-start
  7.2 0.0 copy-start.1
  7.2 0.7 copy-done.1
  7.9 0.7 copy-done.2
  8.6 0.3 shard_map.119
  8.9 20.2 %all_to_all.61 = s32[32,1,16]{2,1,0:T(1,128)S(1)} all-to-all(s32[32,1,16]{2,1,0:T(1,128)S(1)} %bitcast.25), channel_id=1, replica_groups=mesh['table'=32,'dp'=8] {'table'}, dimensions={0} | all-to-all | bytes 4096 | tf_op jit(solution)/shard_map/all_to_all | solution.py:338
  29.1 1.6 copy-done.3
  30.7 0.0 copy-start.8
  30.7 1.5 shard_map.120
  32.2 17.6 %all_to_all.62 = bf16[32,16,512]{2,1,0:T(8,128)(2,1)S(1)} all-to-all(bf16[32,16,512]{2,1,0:T(8,128)(2,1)S(1)} %bitcast.22), channel_id=1, replica_groups=mesh['table'=32,'dp'=8] {'table'}, dimensions={0} | all-to-all | bytes 1048576 | tf_op jit(solution)/shard_map/all_to_all | solution.py:346
  49.8 0.0 copy-done.4
  49.9 0.0 copy-done.5
  49.9 6.0 %shard_map.121 = (bf16[256,512]{1,0:T(8,128)(2,1)}, bf16[512,512]{1,0:T(8,128)(2,1)S(1)}, bf16[2,5136,128]{2,1,0:T(8,128)(2,1)S(1)}) custom-call(s32[1,4]{1,0:T(1,128)S(1)} %bitcast.29, bf16[512,512]{1,0:T(8,128)(2,1)S(1)} %bitcast.19, s32[1,256]{1,0:T(1,128)S(1)} %get-tuple-element.15.placed_ref, bf16[256,512]{1,0:T(8,128)(2,1)S(1)} %bitcast.27, ...), custom_call_target="tpu_custom_call" | custom-call | flops 2013265920 | bytes 6827024 | tf_op jit(solution)/shard_map/pallas_call | solution.py:23
  55.9 20.6 %all_to_all.63 = bf16[32,16,512]{2,1,0:T(8,128)(2,1)S(1)} all-to-all(bf16[32,16,512]{2,1,0:T(8,128)(2,1)S(1)} %bitcast.20), channel_id=1, replica_groups=mesh['table'=32,'dp'=8] {'table'}, dimensions={0} | all-to-all | bytes 1048576 | tf_op jit(solution)/shard_map/all_to_all | solution.py:373
  76.5 1.4 shard_map.122
  77.9 1.3 copy-done
  79.2 0.0 reduce-scatter.2.cloned.1.call-update
  79.3 9.8 %all_to_all.64.in_ref = bf16[2,5136,128]{2,1,0:T(8,128)(2,1)S(1)} all-to-all(bf16[2,5136,128]{2,1,0:T(8,128)(2,1)S(1)} %get-tuple-element.18), channel_id=1, replica_groups={{0,1},{2,3},{4,5},{6,7},{8,9},{10,11},{12,13},{14,15},{16,17},{18,19},{..., dimensions={0} | all-to-all | bytes 5259264 | tf_op jit(solution)/shard_map/all_to_all | solution.py:313
  89.1 0.3 shard_map.123
  89.4 19.8 %all_to_all.65.in_ref = bf16[4,1296,128]{2,1,0:T(8,128)(2,1)S(1)} all-to-all(bf16[4,1296,128]{2,1,0:T(8,128)(2,1)S(1)} %shard_map.123), channel_id=1, replica_groups={{0,8,16,24},{2,10,18,26},{4,12,20,28},{6,14,22,30},{32,40,48,56},{34,42..., dimensions={0} | all-to-all | bytes 2654208 | tf_op jit(solution)/shard_map/all_to_all | solution.py:313
  109.2 0.2 shard_map.124
  109.3 10.0 %all_to_all.66.in_ref = bf16[4,336,128]{2,1,0:T(8,128)(2,1)S(1)} all-to-all(bf16[4,336,128]{2,1,0:T(8,128)(2,1)S(1)} %shard_map.124), channel_id=1, replica_groups={{0,2,4,6},{8,10,12,14},{16,18,20,22},{24,26,28,30},{32,34,36,38},{40,42..., dimensions={0} | all-to-all | bytes 688128 | tf_op jit(solution)/shard_map/all_to_all | solution.py:313
  119.3 10.0 %all_to_all.67.in_ref = bf16[8,48,128]{2,1,0:T(8,128)(2,1)S(1)} all-to-all(bf16[8,48,128]{2,1,0:T(8,128)(2,1)S(1)} %shard_map.125), channel_id=1, replica_groups={{0,32,64,96,128,160,192,224},{1,33,65,97,129,161,193,225},{2,34,66,98,1..., dimensions={0} | all-to-all | bytes 196608 | tf_op jit(solution)/shard_map/all_to_all | solution.py:313
  129.3 0.8 shard_map.126
  130.0 10.9 %all_to_all.68 = bf16[8,40,128]{2,1,0:T(8,128)(2,1)S(1)} all-to-all(bf16[8,40,128]{2,1,0:T(8,128)(2,1)S(1)} %get-tuple-element.19), channel_id=1, replica_groups={{0,32,64,96,128,160,192,224},{1,33,65,97,129,161,193,225},{2,34,66,98,1..., dimensions={0} | all-to-all | bytes 163840 | tf_op jit(solution)/shard_map/all_to_all | solution.py:313
  141.0 8.3 %all_to_all.69 = bf16[4,320,128]{2,1,0:T(8,128)(2,1)S(1)} all-to-all(bf16[4,320,128]{2,1,0:T(8,128)(2,1)S(1)} %broadcast_in_dim.26), channel_id=1, replica_groups={{0,2,4,6},{8,10,12,14},{16,18,20,22},{24,26,28,30},{32,34,36,38},{40,42..., dimensions={0} | all-to-all | bytes 655360 | tf_op jit(solution)/shard_map/all_to_all | solution.py:313
  149.2 0.2 broadcast_in_dim.28
  149.4 13.8 %all_to_all.70 = bf16[4,1280,128]{2,1,0:T(8,128)(2,1)S(1)} all-to-all(bf16[4,1280,128]{2,1,0:T(8,128)(2,1)S(1)} %broadcast_in_dim.28), channel_id=1, replica_groups={{0,8,16,24},{2,10,18,26},{4,12,20,28},{6,14,22,30},{32,40,48,56},{34,42..., dimensions={0} | all-to-all | bytes 2621440 | tf_op jit(solution)/shard_map/all_to_all | solution.py:313
  163.2 0.2 broadcast_in_dim.30
  163.3 8.7 %all_to_all.71 = bf16[2,5120,128]{2,1,0:T(8,128)(2,1)S(1)} all-to-all(bf16[2,5120,128]{2,1,0:T(8,128)(2,1)S(1)} %broadcast_in_dim.30), channel_id=1, replica_groups={{0,1},{2,3},{4,5},{6,7},{8,9},{10,11},{12,13},{14,15},{16,17},{18,19},{..., dimensions={0} | all-to-all | bytes 5242880 | tf_op jit(solution)/shard_map/all_to_all | solution.py:313
  172.0 2.8 %shard_map.127 = (bf16[512,2048]{1,0:T(8,128)(2,1)}, bf16[512,512]{1,0:T(8,128)(2,1)}) custom-call(bf16[10240,128]{1,0:T(8,128)(2,1)S(1)} %bitcast.18), custom_call_target="tpu_custom_call" | custom-call | bytes 5242880 | tf_op jit(solution)/shard_map/pallas_call | solution.py:23
  174.8 1.8 convert_element_type.3
  (13 shorter events, 0.1 us)
Async XLA Ops:
  7.2 167.6 %reduce-scatter.2.cloned.1.call-start = ((), (), s32[]{:S(2)}) async-start(), calls=%async_computation.12 | async-start | bytes 2359296 | tf_op jit(solution)/shard_map/reduce_scatter | solution.py:383
  7.2 0.7 copy-start.1
  7.9 0.7 copy-start.2
  29.1 1.6 copy-start.3
  30.7 19.1 %copy-start.4 = (bf16[512,2048]{1,0:T(8,128)(2,1)S(1)}, bf16[512,2048]{1,0:T(8,128)(2,1)}, u32[]{:S(2)}) copy-start(bf16[512,2048]{1,0:T(8,128)(2,1)} %w_proj_ref.1) | copy-start | bytes 6291460
  30.7 19.1 %copy-start.5 = (bf16[512,512]{1,0:T(8,128)(2,1)S(1)}, bf16[512,512]{1,0:T(8,128)(2,1)}, u32[]{:S(2)}) copy-start(bf16[512,512]{1,0:T(8,128)(2,1)} %w_out_ref.1) | copy-start | bytes 1572868
  30.7 19.1 %copy-start.6 = (bf16[1,256,512]{2,1,0:T(8,128)(2,1)S(1)}, bf16[1,256,512]{2,1,0:T(8,128)(2,1)}, u32[]{:S(2)}) copy-start(bf16[1,256,512]{2,1,0:T(8,128)(2,1)} %param.12) | copy-start | bytes 786436
  30.7 19.1 %copy-start.7 = (f32[512]{0:T(512)S(1)}, f32[512]{0:T(512)}, u32[]{:S(2)}) copy-start(f32[512]{0:T(512)} %param.15) | copy-start | bytes 6148
  30.7 19.1 %copy-start.8 = (s32[1,1,4]{2,1,0:T(1,128)S(1)}, s32[1,1,4]{2,1,0:T(1,128)}, u32[]{:S(2)}) copy-start(s32[1,1,4]{2,1,0:T(1,128)} %param.11) | copy-start | bytes 52
  77.9 1.3 copy-start
Sparse Core Ops, SparseCore 0:
  79.4 37.7 reduce-scatter.1

commit v2 on v1

--- a/solution.py
+++ b/solution.py
@@ -95,19 +95,28 @@
         out_ref[pl.ds(start, 256), :] = nn(hits, table_ref[...]).astype(BF16)
 
 
-def dense_kernel(asked_ref, got_ref, out_ref):
+def dense_kernel(asked_ref, got_ref, keep_ref, give_ref):
     shards, capacity = asked_ref.shape
     slots = shards * capacity
-    rows = out_ref.shape[0]
+    ring, rows, _ = keep_ref.shape
     high, low = halves(asked_ref[...])
     column = flag(iota((capacity, slots), 0) == iota((capacity, slots), 1) % capacity)
     spread = nn(high, column) * 64.0 + nn(low, column)
     mine = iota((shards, slots), 0) == iota((shards, slots), 1) // capacity
     wanted = jnp.sum(jnp.where(mine, spread, 0.0), axis=0, keepdims=True).astype(jnp.int32) - 1
     got = got_ref[...]
-    for start in range(0, rows, 256):
-        hits = flag(wanted == iota((256, slots), 0) + start)
-        out_ref[pl.ds(start, 256), :] = nn(hits, got).astype(BF16)
+    rank = lax.axis_index("dp")
+    core, place = lax.rem(rank, 2), lax.div(rank, 2)
+    for out_ref, side in ((give_ref, 1 - core), (keep_ref, core)):
+        for d in range(ring):
+            first = (lax.rem(place + d, ring) * 2 + side) * rows
+            hits = flag(wanted - first == iota((rows, slots), 0))
+            out_ref[d] = nn(hits, got).astype(BF16)
+
+
+def pair_kernel(mine_ref, other_ref, *out_refs):
+    for d, out_ref in enumerate(out_refs):
+        out_ref[...] = (mine_ref[d].astype(F32) + other_ref[d].astype(F32)).astype(BF16)
 
 
 def centered_norm(values):
@@ -126,7 +135,7 @@
 
 def layer_kernel(
     lengths_ref, returned_ref, placed_ref, upstream_ref, w_proj_ref, w_out_ref, gain_ref,
-    layer_ref, sent_ref, grads_ref, slope_ref, acted_ref, grad_pre_ref,
+    layer_ref, sent_ref, keep_ref, give_ref, slope_ref, acted_ref, grad_pre_ref,
 ):
     slots = returned_ref.shape[0]
     tokens, width = upstream_ref.shape
@@ -194,11 +203,22 @@
     ).astype(BF16)
     sent_ref[...] = nn(flag(placed == iota((slots, tokens), 0)), row_grads).astype(BF16)
 
-    half = grads_ref.shape[1] - 16
+    half = keep_ref.shape[0] - 16
     per_half = half // width
+    core = lax.rem(lax.axis_index("dp"), 2)
     normed_t = normed.T
     gated_t = gated.T
     blocks = (4 * inner + width) // LANES
+
+    def store(side, rows, value):
+        @pl.when(core == side)
+        def _():
+            keep_ref[rows, :] = value
+
+        @pl.when(core != side)
+        def _():
+            give_ref[rows, :] = value
+
     for pair in range(0, blocks, 2):
         start = pair * LANES
         if start < 4 * inner:
@@ -207,16 +227,15 @@
             value = nn(gated_t, upstream_ref[:, pl.ds(start - 4 * inner, 2 * LANES)])
         for k in range(2):
             side, place = divmod(pair + k, per_half)
-            grads_ref[side, pl.ds(place * width, width), :] = value[
-                :, k * LANES : (k + 1) * LANES
-            ].astype(BF16)
+            part = value[:, k * LANES : (k + 1) * LANES].astype(BF16)
+            store(side, pl.ds(place * width, width), part)
     tail = gain_tail(
         jnp.concatenate(
             [grad_gain[:, k * LANES : (k + 1) * LANES] for k in range(width // LANES)], axis=0
         )
     )
-    for side in range(2):
-        grads_ref[side, pl.ds(half, 16), :] = tail
+    keep_ref[pl.ds(half, 16), :] = tail
+    give_ref[pl.ds(half, 16), :] = tail
 
 
 def gain_tail(grad_gain):
@@ -225,30 +244,58 @@
     return jnp.concatenate([high, low, jnp.zeros((8, LANES), F32)], axis=0).astype(BF16)
 
 
-def merge_kernel(in_ref, out_ref):
-    parts = in_ref.shape[0]
-    rows = in_ref.shape[1] - 16
+def first_place():
+    rank = lax.axis_index("dp")
+    along_x = lax.rem(lax.axis_index("table"), XS)
+    along_y = lax.div(rank, 2)
+    core = lax.rem(rank, 2)
+    return core, jnp.where(core == 0, along_x, along_y), jnp.where(core == 0, along_y, along_x)
+
+
+def part_sum(refs, start, count):
+    value = refs[0][pl.ds(start, count), :].astype(F32)
+    for ref in refs[1:]:
+        value = value + ref[pl.ds(start, count), :].astype(F32)
+    return value
+
+
+def tail_sum(refs, rows):
+    tail = part_sum(refs, rows, 16)
+    return gain_tail(tail[0:4] + tail[4:8])
+
+
+def turned_merge_kernel(mine_ref, other_ref, *out_refs):
+    refs = (mine_ref, other_ref)
+    chunk = out_refs[0].shape[0] - 16
+    ring = len(out_refs)
+    tail = tail_sum(refs, ring * chunk)
+    _, place, _ = first_place()
+    for d in (1, 2, 3, 0):
+        start = pl.multiple_of(lax.rem(place + d, ring) * chunk, chunk)
+        out_refs[d][pl.ds(0, chunk), :] = part_sum(refs, start, chunk).astype(BF16)
+        out_refs[d][pl.ds(chunk, 16), :] = tail
+
+
+def merge_kernel(*refs):
+    refs, out_ref = refs[:-1], refs[-1]
     pieces, size, _ = out_ref.shape
-    chunk = rows // pieces
-
-    def total(start, count):
-        value = in_ref[0, pl.ds(start, count), :].astype(F32)
-        for i in range(1, parts):
-            value = value + in_ref[i, pl.ds(start, count), :].astype(F32)
-        return value
-
-    tail = total(rows, 16)
-    tail = gain_tail(tail[0:4] + tail[4:8]).astype(F32)
-    whole = size == chunk + 16
+    chunk = size - 16
+    tail = tail_sum(refs, pieces * chunk)
     for p in range(pieces):
-        if whole:
-            out_ref[p, pl.ds(0, chunk), :] = total(p * chunk, chunk).astype(BF16)
-            out_ref[p, pl.ds(chunk, 16), :] = tail.astype(BF16)
-        elif p % 2 == 0:
-            two = total(p * chunk, 2 * chunk)
-            for k in range(2):
-                piece = jnp.concatenate([two[k * chunk : (k + 1) * chunk], tail[0:8]], axis=0)
-                out_ref[p + k] = piece.astype(BF16)
+        out_ref[p, pl.ds(0, chunk), :] = part_sum(refs, p * chunk, chunk).astype(BF16)
+        out_ref[p, pl.ds(chunk, 16), :] = tail
+
+
+def narrow_merge_kernel(in_ref, out_ref):
+    pieces, size, _ = out_ref.shape
+    chunk = size - 8
+    refs = [in_ref.at[i] for i in range(in_ref.shape[0])]
+    tail = tail_sum(refs, pieces * chunk).astype(F32)[0:8]
+    for p in range(0, pieces, 2):
+        two = part_sum(refs, p * chunk, 2 * chunk)
+        for k in range(2):
+            piece = jnp.concatenate([two[k * chunk : (k + 1) * chunk], tail], axis=0)
+            out_ref[p + k] = piece.astype(BF16)
 
 
 def turn_kernel(in_ref, spread_ref, gain_ref):
@@ -262,10 +309,26 @@
     gain_ref[...] = gain * scale
 
 
-def finish_kernel(grads_ref, proj_ref, out_ref):
+def finish_kernel(*refs):
+    pieces, (proj_ref, out_ref, grads_ref, sems) = refs[:-4], refs[-4:]
     rows = proj_ref.shape[0]
     proj_blocks = proj_ref.shape[1] // LANES
     out_blocks = out_ref.shape[1] // LANES
+    ring = len(pieces) // 2
+    chunk = pieces[0].shape[0]
+    core, mine, other = first_place()
+    copies = []
+    for i, piece in enumerate(pieces):
+        side, place = (core, mine) if i < ring else (1 - core, other)
+        spot = side * ring + lax.rem(place + (ring - i % ring), ring)
+        start = pl.multiple_of(spot * chunk, chunk)
+        copies.append(
+            pltpu.make_async_copy(piece, grads_ref.at[pl.ds(start, chunk), :], sems.at[i])
+        )
+    for copy in copies:
+        copy.start()
+    for copy in copies:
+        copy.wait()
 
     def squares(first, count):
         total = jnp.zeros((8, LANES), F32)
@@ -285,6 +348,13 @@
             out_ref[:, cols] = (value * out_scale).astype(BF16)
 
 
+def sum_kernel(*refs):
+    value = refs[0][...].astype(F32)
+    for ref in refs[1:-1]:
+        value = value + ref[...].astype(F32)
+    refs[-1][...] = value
+
+
 ZS, XS, YS = 8, 4, 4
 
 
@@ -292,12 +362,24 @@
     return (z * XS + x) * (2 * YS) + y * 2 + c
 
 
-CORE_GROUPS = [
-    [device(z, x, y, c) for c in range(2)] for z in range(ZS) for x in range(XS) for y in range(YS)
-]
-FIRST_GROUPS = [
-    [device(z, x, y, 0) for x in range(XS)] for z in range(ZS) for y in range(YS)
-] + [[device(z, x, y, 1) for y in range(YS)] for z in range(ZS) for x in range(XS)]
+PLACES = [(z, x, y, c) for z in range(ZS) for x in range(XS) for y in range(YS) for c in range(2)]
+CORE_PERM = [(device(z, x, y, c), device(z, x, y, 1 - c)) for z, x, y, c in PLACES]
+
+
+def first_perm(d):
+    return [
+        (
+            device(z, x, y, c),
+            device(z, (x + d) % XS, y, c) if c == 0 else device(z, x, (y + d) % YS, c),
+        )
+        for z, x, y, c in PLACES
+    ]
+
+
+def y_perm(d):
+    return [(device(z, x, y, c), device(z, x, (y + d) % YS, c)) for z, x, y, c in PLACES]
+
+
 SECOND_GROUPS = [
     [device(z, x, y, 0) for y in range(YS)] for z in range(ZS) for x in range(XS)
 ] + [[device(z, x, y, 1) for x in range(XS)] for z in range(ZS) for y in range(YS)]
@@ -347,12 +429,14 @@
         picked.reshape(shards, capacity, width), "table", split_axis=0, concat_axis=0, tiled=True
     ).reshape(slots, width)
     half = width * (4 * inner + width) // (2 * LANES)
-    layer_rows, sent, grads = call(
+    grad_half = shape((half + 16, LANES), BF16)
+    layer_rows, sent, keep, give = call(
         layer_kernel,
         [
             shape((tokens, width), BF16),
             shape((slots, width), BF16),
-            shape((2, half + 16, LANES), BF16),
+            grad_half,
+            grad_half,
         ],
         seq_lengths[0],
         returned,
@@ -373,21 +457,26 @@
     got = lax.all_to_all(
         sent.reshape(shards, capacity, width), "table", split_axis=0, concat_axis=0, tiled=True
     ).reshape(slots, width)
-    (dense,) = call(
+    rows = table_rows.shape[0] // (2 * YS)
+    quarter = shape((YS, rows, width), BF16)
+    kept, given = call(
         dense_kernel,
-        [shape(table_rows.shape, BF16)],
+        [quarter, quarter],
         asked,
         got,
         flops=2 * slots * width * table_rows.shape[0],
     )
-    table_grad = lax.psum_scatter(dense, "dp", scatter_dimension=0, tiled=True).astype(F32)
-
-    grads = swap(grads, CORE_GROUPS)
-    (grads,) = call(merge_kernel, [shape((4, half // 4 + 16, LANES), BF16)], grads)
-    grads = swap(grads, FIRST_GROUPS)
-    (grads,) = call(merge_kernel, [shape((4, half // 16 + 16, LANES), BF16)], grads)
+    given = lax.ppermute(given, BOTH, CORE_PERM)
+    parts = call(pair_kernel, [shape((rows, width), BF16)] * YS, kept, given)
+    parts = [parts[0]] + [lax.ppermute(parts[d], BOTH, y_perm(d)) for d in (1, 2, 3)]
+    (table_grad,) = call(sum_kernel, [shape((rows, width), F32)], *parts)
+
+    other = lax.ppermute(give, BOTH, CORE_PERM)
+    parts = call(turned_merge_kernel, [shape((half // 4 + 16, LANES), BF16)] * 4, keep, other)
+    parts = [parts[0]] + [lax.ppermute(parts[d], BOTH, first_perm(d)) for d in (1, 2, 3)]
+    (grads,) = call(merge_kernel, [shape((4, half // 16 + 16, LANES), BF16)], *parts)
     grads = swap(grads, SECOND_GROUPS)
-    (grads,) = call(merge_kernel, [shape((8, half // 128 + 8, LANES), BF16)], grads)
+    (grads,) = call(narrow_merge_kernel, [shape((8, half // 128 + 8, LANES), BF16)], grads)
     grads = swap(grads, LAST_GROUPS)
     grads, step_gain = call(
         turn_kernel,
@@ -396,10 +485,15 @@
     )
     grads = swap(grads, LAST_GROUPS).reshape(half // 16, LANES)
     grads = spread(grads, SECOND_GROUPS)
-    grads = spread(grads, FIRST_GROUPS)
-    grads = spread(grads, CORE_GROUPS)
+    mine = [grads] + [lax.ppermute(grads, BOTH, first_perm(d)) for d in (1, 2, 3)]
+    others = [lax.ppermute(piece, BOTH, CORE_PERM) for piece in mine]
     step_proj, step_out = call(
-        finish_kernel, [shape(w_proj.shape, BF16), shape(w_out.shape, BF16)], grads
+        finish_kernel,
+        [shape(w_proj.shape, BF16), shape(w_out.shape, BF16)],
+        *mine,
+        *others,
+        specs=[pl.BlockSpec(memory_space=pl.ANY)] * 8,
+        scratch=[pltpu.VMEM((2 * half, LANES), BF16), pltpu.SemaphoreType.DMA((8,))],
     )
     return (layer_rows[None], table_grad, step_proj, step_out, step_gain.reshape(width))
 

time: 184 us -> 159 us (0.86)
  blocking collectives: 150 us -> 74.8 us
  starting transfers between devices: 0.04 us -> 32.6 us
  waiting for transfers between devices: 0.02 us -> 27.8 us
  between operations: 14.1 us -> 0.93 us
  Pallas kernels: 13.2 us -> 19.6 us
    all_to_all x8 -> x4, blocking collectives: 91.1 us -> 36.9 us  [swap(): lax.all_to_all(values, BOTH, split_axis=0, concat_axis=0, tiled=True, axi...]
    ppermute x0 -> x15, starting transfers between devices: none -> 28.7 us  [the longest x4 10.8 us: body(): others = [lax.ppermute(piece, BOTH, CORE_PERM) for piece in mine]]
    all_to_all x1 -> x0, blocking collectives: 20.6 us -> none  [body(): lax.all_to_all(sent.reshape(shards, capacity, width), 'table', split_axis...]
    ppermute x0 -> x15, waiting for transfers between devices: none -> 16.7 us  [the longest x3 16.7 us: body(): lax.ppermute(parts[d], BOTH, y_perm(d))]
    all_to_all x0 -> x1, waiting for transfers between devices: none -> 11 us  [body(): lax.all_to_all(sent.reshape(shards, capacity, width), 'table', split_axis...]
    pallas_call x9 -> x11, Pallas kernels: 13.2 us -> 19.6 us  [call(): pl.pallas_call(kernel, out_shape=outs, in_specs=specs if specs is not Non...]
    all_to_all x0 -> x1, starting transfers between devices: none -> 3.89 us  [body(): lax.all_to_all(sent.reshape(shards, capacity, width), 'table', split_axis...]
    unnamed x18 -> x16, local copies, waits for them, and re-layouts: 4.28 us -> 2.96 us
  transfers between devices with their start and end apart: 1 -> 16, of which waited for: 0 -> 3; matrix products, arithmetic and copies ran while one was open for 0% -> 0% of each run, Pallas kernels for 2% -> 3%
where the time goes in v2:
time: 159 us
  blocking collectives  74.8 us (47%)
  starting transfers between devices  32.6 us (21%)
  waiting for transfers between devices  27.8 us (17%)
  Pallas kernels  19.6 us (12%)
  local copies, waits for them, and re-layouts  3.01 us (2%)
    all_to_all x4, blocking collectives, swap(): lax.all_to_all(values, BOTH, split_axis=0, concat_axis=0, tiled=True, axi...  36.9 us
    all_to_all x1, blocking collectives, body(): lax.all_to_all(requests, 'table', split_axis=0, concat_axis=0, tiled=True)  20.2 us
    pallas_call x11, Pallas kernels, call(): pl.pallas_call(kernel, out_shape=outs, in_specs=specs if specs is not Non...  19.6 us
    all_to_all x1, blocking collectives, body(): lax.all_to_all(picked.reshape(shards, capacity, width), 'table', split_ax...  17.6 us
    ppermute x3, waiting for transfers between devices, body(): lax.ppermute(parts[d], BOTH, y_perm(d))  16.7 us
    all_to_all x1, waiting for transfers between devices, body(): lax.all_to_all(sent.reshape(shards, capacity, width), 'table', split_axis...  11 us
    ppermute x4, starting transfers between devices, body(): others = [lax.ppermute(piece, BOTH, CORE_PERM) for piece in mine]  10.8 us
    ppermute x3, starting transfers between devices, body(): lax.ppermute(grads, BOTH, first_perm(d))  5.19 us
  transfers between devices with their start and end apart: 16, of which 3 were waited for; matrix products, arithmetic and copies ran while one was open for 0% of the time, Pallas kernels for 3%

profile of v2, /device:TPU:1, one launch (start us, length us, event | category | flops | bytes accessed | tf_op | source)
XLA Modules:
  0.0 158.7 jit_solution(13928019849941834320)
XLA Ops:
  0.6 0.7 copy-done
  1.3 0.7 copy-done.1
  2.3 20.2 %all_to_all.41 = s32[32,1,16]{2,1,0:T(1,128)S(1)} all-to-all(s32[32,1,16]{2,1,0:T(1,128)S(1)} %bitcast.26), channel_id=1, replica_groups=mesh['table'=32,'dp'=8] {'table'}, dimensions={0} | all-to-all | bytes 4096 | tf_op jit(solution)/shard_map/all_to_all | solution.py:420
  22.5 1.6 %copy-done.2 = bf16[2048,512]{1,0:T(8,128)(2,1)S(1)} copy-done((bf16[2048,512]{1,0:T(8,128)(2,1)S(1)}, bf16[2048,512]{1,0:T(8,128)(2,1)}, u32[]{:S(2)}) %copy-start.2) | copy-done | bytes 2097176
  24.2 1.4 shard_map.120
  25.6 17.6 %all_to_all.42 = bf16[32,16,512]{2,1,0:T(8,128)(2,1)S(1)} all-to-all(bf16[32,16,512]{2,1,0:T(8,128)(2,1)S(1)} %bitcast.23), channel_id=1, replica_groups=mesh['table'=32,'dp'=8] {'table'}, dimensions={0} | all-to-all | bytes 1048576 | tf_op jit(solution)/shard_map/all_to_all | solution.py:428
  43.3 9.5 %shard_map.121 = (bf16[256,512]{1,0:T(8,128)(2,1)}, bf16[512,512]{1,0:T(8,128)(2,1)}, bf16[5136,128]{1,0:T(8,128)(2,1)S(1)}, bf16[5136,128]{1,0:T(8,128)(2,1)}) custom-call(s32[1,4]{1,0:T(1,128)S(1)} %bitcast.30, bf16[512,512]{1,0:T(8,128)(2,1)S(1)} %bitcast.22, s32[1,256]{1,0:T(1,128)S(1)} %get-tuple-element.26.placed_ref, bf16[256,512]{1,0:T(8,128)(2,1)S(1)} %bitcast.28, ...), custom_call_target="tpu_custom_call" | custom-call | flops 2013265920 | bytes 6827024 | tf_op jit(solution)/shard_map/pallas_call | solution.py:23
  52.8 4.6 %collective-permute-start.4 = (bf16[5136,128]{1,0:T(8,128)(2,1)}, bf16[5136,128]{1,0:T(8,128)(2,1)S(1)}, u32[]{:S(2)}, u32[]{:S(2)}) collective-permute-start(bf16[5136,128]{1,0:T(8,128)(2,1)} %get-tuple-element.36), channel_id=1, source_target_pairs={{0,1},{1,0},{2,3},{3,2},{4,5},{5,4},{6,7},{7,6},{8,9},{9,8},{10,11... | collective-permute-start | bytes 3944456 | tf_op jit(solution)/shard_map/ppermute | solution.py:474
  57.4 3.9 %all-to-all-start.2 = ((bf16[32,16,512]{2,1,0:T(8,128)(2,1)}), bf16[32,16,512]{2,1,0:T(8,128)(2,1)S(1)}, u32[]{:S(2)}, u32[]{:S(2)}) async-start(bf16[32,16,512]{2,1,0:T(8,128)(2,1)} %bitcast.10), calls=%async_computation.2 | async-start | bytes 1048576 | tf_op jit(solution)/shard_map/all_to_all | solution.py:457
  61.3 1.1 shard_map.125
  62.4 1.3 collective-permute-start.5
  63.7 2.6 %collective-permute-start.6 = (bf16[1296,128]{1,0:T(8,128)(2,1)}, bf16[1296,128]{1,0:T(8,128)(2,1)S(1)}, u32[]{:S(2)}, u32[]{:S(2)}) collective-permute-start(bf16[1296,128]{1,0:T(8,128)(2,1)} %get-tuple-element.39), channel_id=1, source_target_pairs={{0,16},{1,5},{2,18},{3,7},{4,20},{5,1},{6,22},{7,3},{8,24},{9,13},... | collective-permute-start | bytes 995336 | tf_op jit(solution)/shard_map/ppermute | solution.py:476
  66.3 1.1 collective-permute-start.7
  67.3 11.0 %all-to-all-done.2 = bf16[32,16,512]{2,1,0:T(8,128)(2,1)S(1)} async-done(((bf16[32,16,512]{2,1,0:T(8,128)(2,1)}), bf16[32,16,512]{2,1,0:T(8,128)(2,1)S(1)}, u32[]{:S(2)}, u32[]{:S(2)}) %all-to-all-start.2) | async-done | bytes 524320 | tf_op jit(solution)/shard_map/all_to_all | solution.py:457
  78.4 1.4 shard_map.122
  79.8 1.9 %collective-permute-start = (bf16[4,256,512]{2,1,0:T(8,128)(2,1)S(1)}, bf16[4,256,512]{2,1,0:T(8,128)(2,1)S(1)}, u32[]{:S(2)}, u32[]{:S(2)}) collective-permute-start(bf16[4,256,512]{2,1,0:T(8,128)(2,1)S(1)} %get-tuple-element.30), channel_id=1, source_target_pairs={{0,1},{1,0},{2,3},{3,2},{4,5},{5,4},{6,7},{7,6},{8,9},{9,8},{10,11... | collective-permute-start | bytes 3145736 | tf_op jit(solution)/shard_map/ppermute | solution.py:469
  81.8 8.9 %all_to_all.43.in_ref = bf16[4,336,128]{2,1,0:T(8,128)(2,1)S(1)} all-to-all(bf16[4,336,128]{2,1,0:T(8,128)(2,1)S(1)} %shard_map.126), channel_id=1, replica_groups={{0,2,4,6},{8,10,12,14},{16,18,20,22},{24,26,28,30},{32,34,36,38},{40,42..., dimensions={0} | all-to-all | bytes 688128 | tf_op jit(solution)/shard_map/all_to_all | solution.py:395
  90.8 10.0 %all_to_all.44.in_ref = bf16[8,48,128]{2,1,0:T(8,128)(2,1)S(1)} all-to-all(bf16[8,48,128]{2,1,0:T(8,128)(2,1)S(1)} %shard_map.127), channel_id=1, replica_groups={{0,32,64,96,128,160,192,224},{1,33,65,97,129,161,193,225},{2,34,66,98,1..., dimensions={0} | all-to-all | bytes 196608 | tf_op jit(solution)/shard_map/all_to_all | solution.py:395
  100.7 0.8 shard_map.128
  101.5 9.8 %all_to_all.45 = bf16[8,40,128]{2,1,0:T(8,128)(2,1)S(1)} all-to-all(bf16[8,40,128]{2,1,0:T(8,128)(2,1)S(1)} %get-tuple-element.41), channel_id=1, replica_groups={{0,32,64,96,128,160,192,224},{1,33,65,97,129,161,193,225},{2,34,66,98,1..., dimensions={0} | all-to-all | bytes 163840 | tf_op jit(solution)/shard_map/all_to_all | solution.py:395
  111.3 8.3 %all_to_all.46 = bf16[4,320,128]{2,1,0:T(8,128)(2,1)S(1)} all-to-all(bf16[4,320,128]{2,1,0:T(8,128)(2,1)S(1)} %broadcast_in_dim.12), channel_id=1, replica_groups={{0,2,4,6},{8,10,12,14},{16,18,20,22},{24,26,28,30},{32,34,36,38},{40,42..., dimensions={0} | all-to-all | bytes 655360 | tf_op jit(solution)/shard_map/all_to_all | solution.py:395
  119.6 1.4 collective-permute-start.8
  121.0 2.9 %collective-permute-start.9 = (bf16[1280,128]{1,0:T(8,128)(2,1)S(1)}, bf16[1280,128]{1,0:T(8,128)(2,1)S(1)}, u32[]{:S(2)}, u32[]{:S(2)}) collective-permute-start(bf16[1280,128]{1,0:T(8,128)(2,1)S(1)} %bitcast.17), channel_id=1, source_target_pairs={{0,16},{1,5},{2,18},{3,7},{4,20},{5,1},{6,22},{7,3},{8,24},{9,13},... | collective-permute-start | bytes 983048 | tf_op jit(solution)/shard_map/ppermute | solution.py:488
  123.9 0.9 collective-permute-start.10
  125.0 0.6 collective-permute-start.1
  125.6 0.6 collective-permute-start.2
  126.3 9.2 %collective-permute-done.1.refs_1_ = bf16[256,512]{1,0:T(8,128)(2,1)S(1)} collective-permute-done((bf16[256,512]{1,0:T(8,128)(2,1)S(1)}, bf16[256,512]{1,0:T(8,128)(2,1)S(1)}, u32[]{:S(2)}, u32[]{:S(2)}) %collective-permute-start.1) | collective-permute-done | bytes 262176 | tf_op jit(solution)/shard_map/ppermute | solution.py:471
  135.5 10.2 %collective-permute-start.11 = (bf16[1280,128]{1,0:T(8,128)(2,1)S(1)}, bf16[1280,128]{1,0:T(8,128)(2,1)S(1)}, u32[]{:S(2)}, u32[]{:S(2)}) collective-permute-start(bf16[1280,128]{1,0:T(8,128)(2,1)S(1)} %bitcast.19), channel_id=1, source_target_pairs={{0,1},{1,0},{2,3},{3,2},{4,5},{5,4},{6,7},{7,6},{8,9},{9,8},{10,11... | collective-permute-start | bytes 983048 | tf_op jit(solution)/shard_map/ppermute | solution.py:489
  145.7 0.5 collective-permute-start.13
  146.3 7.5 %collective-permute-done.3.refs_3_ = bf16[256,512]{1,0:T(8,128)(2,1)S(1)} collective-permute-done((bf16[256,512]{1,0:T(8,128)(2,1)S(1)}, bf16[256,512]{1,0:T(8,128)(2,1)S(1)}, u32[]{:S(2)}, u32[]{:S(2)}) %collective-permute-start.3) | collective-permute-done | bytes 262176 | tf_op jit(solution)/shard_map/ppermute | solution.py:471
  153.8 0.9 shard_map.124
  154.7 3.8 %shard_map.129 = (bf16[512,2048]{1,0:T(8,128)(2,1)}, bf16[512,512]{1,0:T(8,128)(2,1)}) custom-call(bf16[1280,128]{1,0:T(8,128)(2,1)S(1)} %bitcast.20, bf16[1280,128]{1,0:T(8,128)(2,1)S(1)} %collective-permute-done.8.refs_1_, bf16[1280,128]{1,0:T(8,128)(2,1)S(1)} %collective-permute-done.9.refs_2_, bf16[1280,128]{1,0:T(8,128)(2,1)S(1)} %collective-permute-done.10.refs_3_, ...), custom_call_target="tpu_custom_call" | custom-call | bytes 5242880 | tf_op jit(solution)/shard_map/pallas_call | solution.py:23
  (34 shorter events, 0.9 us)
Async XLA Ops:
  0.6 0.7 copy-start
  1.3 0.7 copy-start.1
  22.5 1.6 %copy-start.2 = (bf16[2048,512]{1,0:T(8,128)(2,1)S(1)}, bf16[2048,512]{1,0:T(8,128)(2,1)}, u32[]{:S(2)}) copy-start(bf16[2048,512]{1,0:T(8,128)(2,1)} %table_ref.1) | copy-start | bytes 6291460
  24.1 19.1 %copy-start.3 = (bf16[512,2048]{1,0:T(8,128)(2,1)S(1)}, bf16[512,2048]{1,0:T(8,128)(2,1)}, u32[]{:S(2)}) copy-start(bf16[512,2048]{1,0:T(8,128)(2,1)} %w_proj_ref.1) | copy-start | bytes 6291460
  24.1 19.1 %copy-start.4 = (bf16[512,512]{1,0:T(8,128)(2,1)S(1)}, bf16[512,512]{1,0:T(8,128)(2,1)}, u32[]{:S(2)}) copy-start(bf16[512,512]{1,0:T(8,128)(2,1)} %w_out_ref.1) | copy-start | bytes 1572868
  24.1 19.1 %copy-start.5 = (bf16[1,256,512]{2,1,0:T(8,128)(2,1)S(1)}, bf16[1,256,512]{2,1,0:T(8,128)(2,1)}, u32[]{:S(2)}) copy-start(bf16[1,256,512]{2,1,0:T(8,128)(2,1)} %param.12) | copy-start | bytes 786436
  24.1 19.1 %copy-start.6 = (f32[512]{0:T(512)S(1)}, f32[512]{0:T(512)}, u32[]{:S(2)}) copy-start(f32[512]{0:T(512)} %param.15) | copy-start | bytes 6148
  24.1 19.1 %copy-start.7 = (s32[1,1,4]{2,1,0:T(1,128)S(1)}, s32[1,1,4]{2,1,0:T(1,128)}, u32[]{:S(2)}) copy-start(s32[1,1,4]{2,1,0:T(1,128)} %param.11) | copy-start | bytes 52
  52.8 8.5 %collective-permute-start.4 = (bf16[5136,128]{1,0:T(8,128)(2,1)}, bf16[5136,128]{1,0:T(8,128)(2,1)S(1)}, u32[]{:S(2)}, u32[]{:S(2)}) collective-permute-start(bf16[5136,128]{1,0:T(8,128)(2,1)} %get-tuple-element.36), channel_id=1, source_target_pairs={{0,1},{1,0},{2,3},{3,2},{4,5},{5,4},{6,7},{7,6},{8,9},{9,8},{10,11... | collective-permute-start | bytes 3944456 | tf_op jit(solution)/shard_map/ppermute | solution.py:474
  57.4 21.0 %all-to-all-start.2 = ((bf16[32,16,512]{2,1,0:T(8,128)(2,1)}), bf16[32,16,512]{2,1,0:T(8,128)(2,1)S(1)}, u32[]{:S(2)}, u32[]{:S(2)}) async-start(bf16[32,16,512]{2,1,0:T(8,128)(2,1)} %bitcast.10), calls=%async_computation.2 | async-start | bytes 1048576 | tf_op jit(solution)/shard_map/all_to_all | solution.py:457
  62.4 19.3 %collective-permute-start.5 = (bf16[1296,128]{1,0:T(8,128)(2,1)}, bf16[1296,128]{1,0:T(8,128)(2,1)S(1)}, u32[]{:S(2)}, u32[]{:S(2)}) collective-permute-start(bf16[1296,128]{1,0:T(8,128)(2,1)} %get-tuple-element.38), channel_id=1, source_target_pairs={{0,8},{1,3},{2,10},{3,5},{4,12},{5,7},{6,14},{7,1},{8,16},{9,11},{... | collective-permute-start | bytes 995336 | tf_op jit(solution)/shard_map/ppermute | solution.py:476
  63.7 18.0 %collective-permute-start.6 = (bf16[1296,128]{1,0:T(8,128)(2,1)}, bf16[1296,128]{1,0:T(8,128)(2,1)S(1)}, u32[]{:S(2)}, u32[]{:S(2)}) collective-permute-start(bf16[1296,128]{1,0:T(8,128)(2,1)} %get-tuple-element.39), channel_id=1, source_target_pairs={{0,16},{1,5},{2,18},{3,7},{4,20},{5,1},{6,22},{7,3},{8,24},{9,13},... | collective-permute-start | bytes 995336 | tf_op jit(solution)/shard_map/ppermute | solution.py:476
  66.3 15.4 %collective-permute-start.7 = (bf16[1296,128]{1,0:T(8,128)(2,1)}, bf16[1296,128]{1,0:T(8,128)(2,1)S(1)}, u32[]{:S(2)}, u32[]{:S(2)}) collective-permute-start(bf16[1296,128]{1,0:T(8,128)(2,1)} %get-tuple-element.40), channel_id=1, source_target_pairs={{0,24},{1,7},{2,26},{3,1},{4,28},{5,3},{6,30},{7,5},{8,0},{9,15},{... | collective-permute-start | bytes 995336 | tf_op jit(solution)/shard_map/ppermute | solution.py:476
  79.8 45.0 %collective-permute-start = (bf16[4,256,512]{2,1,0:T(8,128)(2,1)S(1)}, bf16[4,256,512]{2,1,0:T(8,128)(2,1)S(1)}, u32[]{:S(2)}, u32[]{:S(2)}) collective-permute-start(bf16[4,256,512]{2,1,0:T(8,128)(2,1)S(1)} %get-tuple-element.30), channel_id=1, source_target_pairs={{0,1},{1,0},{2,3},{3,2},{4,5},{5,4},{6,7},{7,6},{8,9},{9,8},{10,11... | collective-permute-start | bytes 3145736 | tf_op jit(solution)/shard_map/ppermute | solution.py:469
  119.6 26.2 %collective-permute-start.8 = (bf16[1280,128]{1,0:T(8,128)(2,1)S(1)}, bf16[1280,128]{1,0:T(8,128)(2,1)S(1)}, u32[]{:S(2)}, u32[]{:S(2)}) collective-permute-start(bf16[1280,128]{1,0:T(8,128)(2,1)S(1)} %bitcast.16), channel_id=1, source_target_pairs={{0,8},{1,3},{2,10},{3,5},{4,12},{5,7},{6,14},{7,1},{8,16},{9,11},{... | collective-permute-start | bytes 983048 | tf_op jit(solution)/shard_map/ppermute | solution.py:488
  121.0 24.8 %collective-permute-start.9 = (bf16[1280,128]{1,0:T(8,128)(2,1)S(1)}, bf16[1280,128]{1,0:T(8,128)(2,1)S(1)}, u32[]{:S(2)}, u32[]{:S(2)}) collective-permute-start(bf16[1280,128]{1,0:T(8,128)(2,1)S(1)} %bitcast.17), channel_id=1, source_target_pairs={{0,16},{1,5},{2,18},{3,7},{4,20},{5,1},{6,22},{7,3},{8,24},{9,13},... | collective-permute-start | bytes 983048 | tf_op jit(solution)/shard_map/ppermute | solution.py:488
  123.9 22.4 %collective-permute-start.10 = (bf16[1280,128]{1,0:T(8,128)(2,1)S(1)}, bf16[1280,128]{1,0:T(8,128)(2,1)S(1)}, u32[]{:S(2)}, u32[]{:S(2)}) collective-permute-start(bf16[1280,128]{1,0:T(8,128)(2,1)S(1)} %bitcast.18), channel_id=1, source_target_pairs={{0,24},{1,7},{2,26},{3,1},{4,28},{5,3},{6,30},{7,5},{8,0},{9,15},{... | collective-permute-start | bytes 983048 | tf_op jit(solution)/shard_map/ppermute | solution.py:488
  125.0 10.5 %collective-permute-start.1 = (bf16[256,512]{1,0:T(8,128)(2,1)S(1)}, bf16[256,512]{1,0:T(8,128)(2,1)S(1)}, u32[]{:S(2)}, u32[]{:S(2)}) collective-permute-start(bf16[256,512]{1,0:T(8,128)(2,1)S(1)} %get-tuple-element.32), channel_id=1, source_target_pairs={{0,2},{1,3},{2,4},{3,5},{4,6},{5,7},{6,0},{7,1},{8,10},{9,11},{10,... | collective-permute-start | bytes 786440 | tf_op jit(solution)/shard_map/ppermute | solution.py:471
  125.6 20.7 %collective-permute-start.2 = (bf16[256,512]{1,0:T(8,128)(2,1)S(1)}, bf16[256,512]{1,0:T(8,128)(2,1)S(1)}, u32[]{:S(2)}, u32[]{:S(2)}) collective-permute-start(bf16[256,512]{1,0:T(8,128)(2,1)S(1)} %get-tuple-element.33), channel_id=1, source_target_pairs={{0,4},{1,5},{2,6},{3,7},{4,0},{5,1},{6,2},{7,3},{8,12},{9,13},{10,... | collective-permute-start | bytes 786440 | tf_op jit(solution)/shard_map/ppermute | solution.py:471
  135.5 19.2 %collective-permute-start.11 = (bf16[1280,128]{1,0:T(8,128)(2,1)S(1)}, bf16[1280,128]{1,0:T(8,128)(2,1)S(1)}, u32[]{:S(2)}, u32[]{:S(2)}) collective-permute-start(bf16[1280,128]{1,0:T(8,128)(2,1)S(1)} %bitcast.19), channel_id=1, source_target_pairs={{0,1},{1,0},{2,3},{3,2},{4,5},{5,4},{6,7},{7,6},{8,9},{9,8},{10,11... | collective-permute-start | bytes 983048 | tf_op jit(solution)/shard_map/ppermute | solution.py:489
  145.7 9.0 %collective-permute-start.12 = (bf16[1280,128]{1,0:T(8,128)(2,1)S(1)}, bf16[1280,128]{1,0:T(8,128)(2,1)S(1)}, u32[]{:S(2)}, u32[]{:S(2)}) collective-permute-start(bf16[1280,128]{1,0:T(8,128)(2,1)S(1)} %collective-permute-done.8.refs_1_), channel_id=1, source_target_pairs={{0,1},{1,0},{2,3},{3,2},{4,5},{5,4},{6,7},{7,6},{8,9},{9,8},{10,11... | collective-permute-start | bytes 983048 | tf_op jit(solution)/shard_map/ppermute | solution.py:489
  145.7 9.0 %collective-permute-start.13 = (bf16[1280,128]{1,0:T(8,128)(2,1)S(1)}, bf16[1280,128]{1,0:T(8,128)(2,1)S(1)}, u32[]{:S(2)}, u32[]{:S(2)}) collective-permute-start(bf16[1280,128]{1,0:T(8,128)(2,1)S(1)} %collective-permute-done.9.refs_2_), channel_id=1, source_target_pairs={{0,1},{1,0},{2,3},{3,2},{4,5},{5,4},{6,7},{7,6},{8,9},{9,8},{10,11... | collective-permute-start | bytes 983048 | tf_op jit(solution)/shard_map/ppermute | solution.py:489
  146.2 8.5 %collective-permute-start.14 = (bf16[1280,128]{1,0:T(8,128)(2,1)S(1)}, bf16[1280,128]{1,0:T(8,128)(2,1)S(1)}, u32[]{:S(2)}, u32[]{:S(2)}) collective-permute-start(bf16[1280,128]{1,0:T(8,128)(2,1)S(1)} %collective-permute-done.10.refs_3_), channel_id=1, source_target_pairs={{0,1},{1,0},{2,3},{3,2},{4,5},{5,4},{6,7},{7,6},{8,9},{9,8},{10,11... | collective-permute-start | bytes 983048 | tf_op jit(solution)/shard_map/ppermute | solution.py:489
  146.3 7.5 %collective-permute-start.3 = (bf16[256,512]{1,0:T(8,128)(2,1)S(1)}, bf16[256,512]{1,0:T(8,128)(2,1)S(1)}, u32[]{:S(2)}, u32[]{:S(2)}) collective-permute-start(bf16[256,512]{1,0:T(8,128)(2,1)S(1)} %get-tuple-element.34), channel_id=1, source_target_pairs={{0,6},{1,7},{2,0},{3,1},{4,2},{5,3},{6,4},{7,5},{8,14},{9,15},{10,... | collective-permute-start | bytes 786440 | tf_op jit(solution)/shard_map/ppermute | solution.py:471

commit v3 on v2

--- a/solution.py
+++ b/solution.py
@@ -1,3 +1,5 @@
+import functools
+
 import jax
 import jax.numpy as jnp
 from jax import lax
@@ -13,19 +15,26 @@
 F32 = jnp.float32
 BF16 = jnp.bfloat16
 LANES = 128
+STRIP = 64
 VMEM = pl.BlockSpec(memory_space=pltpu.VMEM)
 SMEM = pl.BlockSpec(memory_space=pltpu.SMEM)
-
-
-def call(kernel, outs, *operands, specs=None, flops=0, transcendentals=0, scratch=()):
+ANY = pl.BlockSpec(memory_space=pl.ANY)
+HBM = pl.BlockSpec(memory_space=pltpu.HBM)
+
+
+def call(
+    kernel, outs, *operands, specs=None, out_specs=None, flops=0, transcendentals=0, scratch=(),
+    aliases=None,
+):
     moved = sum(v.size * v.dtype.itemsize for v in operands)
     moved += sum(v.size * v.dtype.itemsize for v in outs)
     return pl.pallas_call(
         kernel,
         out_shape=outs,
         in_specs=specs if specs is not None else [VMEM] * len(operands),
-        out_specs=[VMEM] * len(outs),
+        out_specs=out_specs if out_specs is not None else [VMEM] * len(outs),
         scratch_shapes=list(scratch),
+        input_output_aliases=aliases or {},
         cost_estimate=pl.CostEstimate(
             flops=flops, bytes_accessed=moved, transcendentals=transcendentals
         ),
@@ -57,16 +66,17 @@
     return jnp.where(mask, 1.0, 0.0).astype(BF16)
 
 
-def request_kernel(shard_ref, slot_ref, request_ref, placed_ref):
+def request_kernel(rows, item_ref, request_ref, placed_ref):
     shards, capacity = request_ref.shape
-    tokens = slot_ref.shape[1]
-    target = shard_ref[...]
+    tokens = item_ref.shape[1]
+    item = item_ref[...]
+    target = item // rows
     named = target == iota((shards, tokens), 0)
     earlier = flag(iota((tokens, tokens), 0) < iota((tokens, tokens), 1))
     counts = nn(flag(named), earlier)
     rank = jnp.sum(jnp.where(named, counts, 0.0), axis=0, keepdims=True).astype(jnp.int32)
     placed_ref[...] = target * capacity + rank
-    wanted = slot_ref[...] + 1
+    wanted = item - target * rows + 1
     at_rank = rank == iota((capacity, tokens), 0)
     high = jnp.where(at_rank, wanted // 64, 0).astype(F32).astype(BF16)
     low = jnp.where(at_rank, wanted % 64, 0).astype(F32).astype(BF16)
@@ -95,28 +105,31 @@
         out_ref[pl.ds(start, 256), :] = nn(hits, table_ref[...]).astype(BF16)
 
 
-def dense_kernel(asked_ref, got_ref, keep_ref, give_ref):
+def wanted_row(asked_ref):
     shards, capacity = asked_ref.shape
     slots = shards * capacity
-    ring, rows, _ = keep_ref.shape
     high, low = halves(asked_ref[...])
     column = flag(iota((capacity, slots), 0) == iota((capacity, slots), 1) % capacity)
     spread = nn(high, column) * 64.0 + nn(low, column)
     mine = iota((shards, slots), 0) == iota((shards, slots), 1) // capacity
-    wanted = jnp.sum(jnp.where(mine, spread, 0.0), axis=0, keepdims=True).astype(jnp.int32) - 1
-    got = got_ref[...]
+    return jnp.sum(jnp.where(mine, spread, 0.0), axis=0, keepdims=True).astype(jnp.int32) - 1
+
+
+def dense_kernel(asked_ref, asked_other_ref, got_ref, got_other_ref, after_ref, *out_refs):
+    ring, (rows, _) = len(out_refs), out_refs[0].shape
+    wanted = jnp.concatenate([wanted_row(asked_ref), wanted_row(asked_other_ref)], axis=1)
+    got = jnp.concatenate([got_ref[...], got_other_ref[...]], axis=0)
     rank = lax.axis_index("dp")
     core, place = lax.rem(rank, 2), lax.div(rank, 2)
-    for out_ref, side in ((give_ref, 1 - core), (keep_ref, core)):
-        for d in range(ring):
-            first = (lax.rem(place + d, ring) * 2 + side) * rows
-            hits = flag(wanted - first == iota((rows, slots), 0))
-            out_ref[d] = nn(hits, got).astype(BF16)
-
-
-def pair_kernel(mine_ref, other_ref, *out_refs):
-    for d, out_ref in enumerate(out_refs):
-        out_ref[...] = (mine_ref[d].astype(F32) + other_ref[d].astype(F32)).astype(BF16)
+    places = iota((rows, wanted.shape[1]), 0)
+    for d in (2, 3, 1, 0):
+        ahead = lax.rem(jnp.where(core == 0, place + d, place + ring - d), ring)
+        hits = flag(wanted - (ahead * 2 + core) * rows == places)
+        out_refs[d][...] = nn(hits, got).astype(BF16)
+
+
+def sigmoid(values):
+    return 0.5 * jnp.tanh(0.5 * values) + 0.5
 
 
 def centered_norm(values):
@@ -136,6 +149,7 @@
 def layer_kernel(
     lengths_ref, returned_ref, placed_ref, upstream_ref, w_proj_ref, w_out_ref, gain_ref,
     layer_ref, sent_ref, keep_ref, give_ref, slope_ref, acted_ref, grad_pre_ref,
+    left_ref,
 ):
     slots = returned_ref.shape[0]
     tokens, width = upstream_ref.shape
@@ -150,7 +164,7 @@
     for block in range(4):
         cols = pl.ds(block * inner, inner)
         pre = nn(normed, w_proj_ref[:, cols])
-        sig = jax.nn.sigmoid(pre)
+        sig = sigmoid(pre)
         acted_ref[:, cols] = (pre * sig).astype(BF16)
         slope_ref[:, cols] = sig * (1.0 + pre * (1.0 - sig))
     query_pos = iota((tokens, tokens), 0)
@@ -170,7 +184,7 @@
     mixed, weights, slopes = [], [], []
     for h in range(HEADS):
         scores = nt(head(2, h), head(3, h)) * scale
-        sig = jax.nn.sigmoid(scores)
+        sig = sigmoid(scores)
         weight = jnp.where(allowed, scores * sig, 0.0).astype(BF16)
         slopes.append(jnp.where(allowed, sig * (1.0 + scores * (1.0 - sig)), 0.0))
         weights.append(weight)
@@ -204,31 +218,27 @@
     sent_ref[...] = nn(flag(placed == iota((slots, tokens), 0)), row_grads).astype(BF16)
 
     half = keep_ref.shape[0] - 16
-    per_half = half // width
     core = lax.rem(lax.axis_index("dp"), 2)
-    normed_t = normed.T
-    gated_t = gated.T
+    rows = width // 2
+    left_ref[0] = normed.T
+    left_ref[1] = gated.T
     blocks = (4 * inner + width) // LANES
-
-    def store(side, rows, value):
-        @pl.when(core == side)
-        def _():
-            keep_ref[rows, :] = value
-
-        @pl.when(core != side)
-        def _():
-            give_ref[rows, :] = value
-
-    for pair in range(0, blocks, 2):
-        start = pair * LANES
-        if start < 4 * inner:
-            value = nn(normed_t, grad_pre_ref[:, pl.ds(start, 2 * LANES)])
-        else:
-            value = nn(gated_t, upstream_ref[:, pl.ds(start - 4 * inner, 2 * LANES)])
-        for k in range(2):
-            side, place = divmod(pair + k, per_half)
-            part = value[:, k * LANES : (k + 1) * LANES].astype(BF16)
-            store(side, pl.ds(place * width, width), part)
+    for out_ref, side in ((give_ref, 1 - core), (keep_ref, core)):
+        first = pl.multiple_of(side * rows, rows)
+        left = left_ref[0, pl.ds(first, rows), :]
+        value = nn(left, grad_pre_ref[...])
+        for b in range(4 * inner // LANES):
+            for p in range(4):
+                out_ref[pl.ds((p * blocks + b) * STRIP, STRIP), :] = value[
+                    p * STRIP : (p + 1) * STRIP, b * LANES : (b + 1) * LANES
+                ].astype(BF16)
+        value = nn(left_ref[1, pl.ds(first, rows), :], upstream)
+        for b in range(width // LANES):
+            for p in range(4):
+                at = (p * blocks + b + 4 * inner // LANES) * STRIP
+                out_ref[pl.ds(at, STRIP), :] = value[
+                    p * STRIP : (p + 1) * STRIP, b * LANES : (b + 1) * LANES
+                ].astype(BF16)
     tail = gain_tail(
         jnp.concatenate(
             [grad_gain[:, k * LANES : (k + 1) * LANES] for k in range(width // LANES)], axis=0
@@ -276,20 +286,10 @@
         out_refs[d][pl.ds(chunk, 16), :] = tail
 
 
-def merge_kernel(*refs):
+def narrow_merge_kernel(*refs):
     refs, out_ref = refs[:-1], refs[-1]
     pieces, size, _ = out_ref.shape
-    chunk = size - 16
-    tail = tail_sum(refs, pieces * chunk)
-    for p in range(pieces):
-        out_ref[p, pl.ds(0, chunk), :] = part_sum(refs, p * chunk, chunk).astype(BF16)
-        out_ref[p, pl.ds(chunk, 16), :] = tail
-
-
-def narrow_merge_kernel(in_ref, out_ref):
-    pieces, size, _ = out_ref.shape
     chunk = size - 8
-    refs = [in_ref.at[i] for i in range(in_ref.shape[0])]
     tail = tail_sum(refs, pieces * chunk).astype(F32)[0:8]
     for p in range(0, pieces, 2):
         two = part_sum(refs, p * chunk, 2 * chunk)
@@ -298,7 +298,8 @@
             out_ref[p + k] = piece.astype(BF16)
 
 
-def turn_kernel(in_ref, spread_ref, gain_ref):
+def turn_kernel(in_ref, near_ref, passed_ref, sum_ref, spread_ref, gain_ref):
+    sum_ref[...] = (near_ref[...].astype(F32) + passed_ref[...].astype(F32)).astype(BF16)
     total = jnp.sum(in_ref[...].astype(F32), axis=0)
     rows = spread_ref.shape[1]
     mine = total[0:rows].astype(BF16)
@@ -310,49 +311,55 @@
 
 
 def finish_kernel(*refs):
-    pieces, (proj_ref, out_ref, grads_ref, sems) = refs[:-4], refs[-4:]
-    rows = proj_ref.shape[0]
-    proj_blocks = proj_ref.shape[1] // LANES
-    out_blocks = out_ref.shape[1] // LANES
+    own_ref, near_ref, far_ref = refs[:3]
+    pieces = refs[3:-6]
+    table_ref, proj_ref, out_ref, sum_ref, stage_ref, sems = refs[-6:]
+    sum_ref[...] = (
+        own_ref[...].astype(F32) + near_ref[...].astype(F32) + far_ref[...].astype(F32)
+    )
+    copies = [pltpu.make_async_copy(sum_ref, table_ref, sems.at[len(pieces), 0])]
+    copies[0].start()
+    split = proj_ref.shape[1]
+    blocks = stage_ref.shape[2] // LANES
     ring = len(pieces) // 2
-    chunk = pieces[0].shape[0]
     core, mine, other = first_place()
-    copies = []
+
+    def strip(piece, b):
+        return piece[pl.ds(b * STRIP, STRIP), :].astype(F32)
+
+    proj_sum = jnp.zeros((8, LANES), F32)
+    out_sum = jnp.zeros((8, LANES), F32)
+    for piece in pieces:
+        for b in range(blocks):
+            value = strip(piece, b)
+            part = jnp.sum((value * value).reshape(STRIP // 8, 8, LANES), axis=0)
+            if b * LANES < split:
+                proj_sum = proj_sum + part
+            else:
+                out_sum = out_sum + part
+    proj_scale = lax.rsqrt(jnp.sum(proj_sum) / proj_ref.size + STEP_EPS)
+    out_scale = lax.rsqrt(jnp.sum(out_sum) / out_ref.size + STEP_EPS)
     for i, piece in enumerate(pieces):
+        for b in range(blocks):
+            scale = proj_scale if b * LANES < split else out_scale
+            stage_ref[i, :, pl.ds(b * LANES, LANES)] = (strip(piece, b) * scale).astype(BF16)
         side, place = (core, mine) if i < ring else (1 - core, other)
         spot = side * ring + lax.rem(place + (ring - i % ring), ring)
-        start = pl.multiple_of(spot * chunk, chunk)
-        copies.append(
-            pltpu.make_async_copy(piece, grads_ref.at[pl.ds(start, chunk), :], sems.at[i])
-        )
-    for copy in copies:
-        copy.start()
+        rows = pl.ds(pl.multiple_of(spot * STRIP, STRIP), STRIP)
+        for k, (first, count, ref) in enumerate(
+            ((0, split, proj_ref), (split, out_ref.shape[1], out_ref))
+        ):
+            copy = pltpu.make_async_copy(
+                stage_ref.at[i, :, pl.ds(first, count)], ref.at[rows, :], sems.at[i, k]
+            )
+            copy.start()
+            copies.append(copy)
     for copy in copies:
         copy.wait()
 
-    def squares(first, count):
-        total = jnp.zeros((8, LANES), F32)
-        for b in range(first, first + count):
-            value = grads_ref[pl.ds(b * rows, rows), :].astype(F32)
-            total = total + jnp.sum((value * value).reshape(rows // 8, 8, LANES), axis=0)
-        return jnp.sum(total)
-
-    proj_scale = lax.rsqrt(squares(0, proj_blocks) / proj_ref.size + STEP_EPS)
-    out_scale = lax.rsqrt(squares(proj_blocks, out_blocks) / out_ref.size + STEP_EPS)
-    for b in range(proj_blocks + out_blocks):
-        value = grads_ref[pl.ds(b * rows, rows), :].astype(F32)
-        if b < proj_blocks:
-            proj_ref[:, pl.ds(b * LANES, LANES)] = (value * proj_scale).astype(BF16)
-        else:
-            cols = pl.ds((b - proj_blocks) * LANES, LANES)
-            out_ref[:, cols] = (value * out_scale).astype(BF16)
-
-
-def sum_kernel(*refs):
-    value = refs[0][...].astype(F32)
-    for ref in refs[1:-1]:
-        value = value + ref[...].astype(F32)
-    refs[-1][...] = value
+
+def hold_kernel(value_ref, near_ref, far_ref, out_ref):
+    pass
 
 
 ZS, XS, YS = 8, 4, 4
@@ -376,31 +383,21 @@
     ]
 
 
-def y_perm(d):
-    return [(device(z, x, y, c), device(z, x, (y + d) % YS, c)) for z, x, y, c in PLACES]
+def ring_perm(step):
+    return [
+        (device(z, x, y, c), device(z, x, (y + (step if c == 0 else -step)) % YS, c))
+        for z, x, y, c in PLACES
+    ]
 
 
 SECOND_GROUPS = [
-    [device(z, x, y, 0) for y in range(YS)] for z in range(ZS) for x in range(XS)
-] + [[device(z, x, y, 1) for x in range(XS)] for z in range(ZS) for y in range(YS)]
-LAST_GROUPS = [
-    [device(z, x, y, c) for z in range(ZS)]
-    for x in range(XS)
-    for y in range(YS)
-    for c in range(2)
-]
+    [device(z, x, y, 0) for y in range(YS) for z in range(ZS)] for x in range(XS)
+] + [[device(z, x, y, 1) for x in range(XS) for z in range(ZS)] for y in range(YS)]
 
 
 def swap(values, groups):
     return lax.all_to_all(
         values, BOTH, split_axis=0, concat_axis=0, tiled=True, axis_index_groups=groups
-    )
-
-
-def spread(values, groups):
-    count = len(groups[0])
-    return swap(jnp.broadcast_to(values[None], (count, *values.shape)), groups).reshape(
-        count * values.shape[0], values.shape[1]
     )
 
 
@@ -412,10 +409,10 @@
     capacity = 2 * tokens // shards
     slots = shards * capacity
     requests, placed = call(
-        request_kernel,
+        functools.partial(request_kernel, table_rows.shape[0]),
         [shape((shards, capacity), jnp.int32), shape((1, tokens), jnp.int32)],
-        item_shard.reshape(1, tokens),
-        item_slot,
+        item_shard.reshape(1, tokens) * table_rows.shape[0] + item_slot,
+        flops=4 * slots * width * table_rows.shape[0],
     )
     asked = lax.all_to_all(requests, "table", split_axis=0, concat_axis=0, tiled=True)
     (picked,) = call(
@@ -452,48 +449,70 @@
             pltpu.VMEM((tokens, 4 * inner), F32),
             pltpu.VMEM((tokens, 4 * inner), BF16),
             pltpu.VMEM((tokens, 4 * inner), BF16),
+            pltpu.VMEM((2, width, tokens), BF16),
         ],
     )
     got = lax.all_to_all(
         sent.reshape(shards, capacity, width), "table", split_axis=0, concat_axis=0, tiled=True
     ).reshape(slots, width)
     rows = table_rows.shape[0] // (2 * YS)
-    quarter = shape((YS, rows, width), BF16)
-    kept, given = call(
-        dense_kernel,
-        [quarter, quarter],
-        asked,
-        got,
-        flops=2 * slots * width * table_rows.shape[0],
-    )
-    given = lax.ppermute(given, BOTH, CORE_PERM)
-    parts = call(pair_kernel, [shape((rows, width), BF16)] * YS, kept, given)
-    parts = [parts[0]] + [lax.ppermute(parts[d], BOTH, y_perm(d)) for d in (1, 2, 3)]
-    (table_grad,) = call(sum_kernel, [shape((rows, width), F32)], *parts)
-
     other = lax.ppermute(give, BOTH, CORE_PERM)
     parts = call(turned_merge_kernel, [shape((half // 4 + 16, LANES), BF16)] * 4, keep, other)
     parts = [parts[0]] + [lax.ppermute(parts[d], BOTH, first_perm(d)) for d in (1, 2, 3)]
-    (grads,) = call(merge_kernel, [shape((4, half // 16 + 16, LANES), BF16)], *parts)
+    (grads,) = call(narrow_merge_kernel, [shape((32, half // 128 + 8, LANES), BF16)], *parts)
+    own, near, two, far = call(
+        dense_kernel,
+        [shape((rows, width), BF16)] * YS,
+        asked,
+        lax.ppermute(asked, BOTH, CORE_PERM),
+        got,
+        lax.ppermute(got, BOTH, CORE_PERM),
+        grads,
+        specs=[VMEM] * 4 + [ANY],
+        flops=2 * slots * width * table_rows.shape[0],
+    )
+    passed = lax.ppermute(two, BOTH, ring_perm(1))
+    far = lax.ppermute(far, BOTH, ring_perm(-1))
     grads = swap(grads, SECOND_GROUPS)
-    (grads,) = call(narrow_merge_kernel, [shape((8, half // 128 + 8, LANES), BF16)], grads)
-    grads = swap(grads, LAST_GROUPS)
-    grads, step_gain = call(
+    near, grads, step_gain = call(
         turn_kernel,
-        [shape((8, half // 128, LANES), BF16), shape((width // LANES, LANES), F32)],
+        [
+            shape((rows, width), BF16),
+            shape((32, half // 128, LANES), BF16),
+            shape((width // LANES, LANES), F32),
+        ],
         grads,
-    )
-    grads = swap(grads, LAST_GROUPS).reshape(half // 16, LANES)
-    grads = spread(grads, SECOND_GROUPS)
+        near,
+        passed,
+    )
+    near = lax.ppermute(near, BOTH, ring_perm(1))
+    grads = swap(grads, SECOND_GROUPS).reshape(half // 4, LANES)
+    (grads,) = call(
+        hold_kernel,
+        [shape(grads.shape, BF16)],
+        grads,
+        near,
+        far,
+        specs=[ANY] * 3,
+        out_specs=[ANY],
+        aliases={0: 0},
+    )
     mine = [grads] + [lax.ppermute(grads, BOTH, first_perm(d)) for d in (1, 2, 3)]
     others = [lax.ppermute(piece, BOTH, CORE_PERM) for piece in mine]
-    step_proj, step_out = call(
+    table_grad, step_proj, step_out = call(
         finish_kernel,
-        [shape(w_proj.shape, BF16), shape(w_out.shape, BF16)],
+        [shape((rows, width), F32), shape(w_proj.shape, BF16), shape(w_out.shape, BF16)],
+        own,
+        near,
+        far,
         *mine,
         *others,
-        specs=[pl.BlockSpec(memory_space=pl.ANY)] * 8,
-        scratch=[pltpu.VMEM((2 * half, LANES), BF16), pltpu.SemaphoreType.DMA((8,))],
+        out_specs=[HBM, HBM, HBM],
+        scratch=[
+            pltpu.VMEM((rows, width), F32),
+            pltpu.VMEM((8, STRIP, 4 * inner + width), BF16),
+            pltpu.SemaphoreType.DMA((9, 2)),
+        ],
     )
     return (layer_rows[None], table_grad, step_proj, step_out, step_gain.reshape(width))
 

time: 159 us -> 138 us (0.87)
  blocking collectives: 74.8 us -> 38 us
  starting transfers between devices: 32.6 us -> 54.3 us
  Pallas kernels: 19.6 us -> 15.3 us
  local copies, waits for them, and re-layouts: 3.01 us -> 0.82 us
    all_to_all x4 -> x0, blocking collectives: 36.9 us -> none  [swap(): lax.all_to_all(values, BOTH, split_axis=0, concat_axis=0, tiled=True, axi...]
    all_to_all x0 -> x2, starting transfers between devices: none -> 12.1 us  [swap(): lax.all_to_all(values, BOTH, split_axis=0, concat_axis=0, tiled=True, axi...]
    ppermute x4 -> x5, starting transfers between devices: 3.16 us -> 12.6 us  [the longest x1 4.88 us: body(): lax.ppermute(asked, BOTH, CORE_PERM)]
    ppermute x4 -> x5, waiting for transfers between devices: 16.7 us -> 12.3 us  [the longest x1 4.24 us: body(): passed = lax.ppermute(two, BOTH, ring_perm(1))]
    pallas_call x11 -> x9, Pallas kernels: 19.6 us -> 15.3 us  [call(): pl.pallas_call(kernel, out_shape=outs, in_specs=specs if specs is not Non...]
    ppermute x3, waiting for transfers between devices: 0.01 us -> 2.54 us  [body(): lax.ppermute(grads, BOTH, first_perm(d))]
    unnamed x16 -> x14, local copies, waits for them, and re-layouts: 2.96 us -> 0.82 us
  transfers between devices with their start and end apart: 16 -> 19, of which waited for: 3 -> 8; matrix products, arithmetic and copies ran while one was open for 0% -> 0% of each run, Pallas kernels for 3% -> 2%
where the time goes in v3:
time: 138 us; the launch traced here: 137 us
  starting transfers between devices  54.3 us (39%)
  blocking collectives  38 us (28%)
  waiting for transfers between devices  27.3 us (20%)
  Pallas kernels  15.3 us (11%)
    all_to_all x1, blocking collectives, body(): lax.all_to_all(requests, 'table', split_axis=0, concat_axis=0, tiled=True)  20.4 us
    all_to_all x1, blocking collectives, body(): lax.all_to_all(picked.reshape(shards, capacity, width), 'table', split_ax...  17.6 us
    pallas_call x9, Pallas kernels, call(): pl.pallas_call(kernel, out_shape=outs, in_specs=specs if specs is not Non...  15.3 us
    ppermute x4, starting transfers between devices, body(): others = [lax.ppermute(piece, BOTH, CORE_PERM) for piece in mine]  12.2 us
    all_to_all x2, starting transfers between devices, swap(): lax.all_to_all(values, BOTH, split_axis=0, concat_axis=0, tiled=True, axi...  12.1 us
    all_to_all x1, waiting for transfers between devices, body(): lax.all_to_all(sent.reshape(shards, capacity, width), 'table', split_axis...  11 us
    ppermute x3, starting transfers between devices, body(): lax.ppermute(parts[d], BOTH, first_perm(d))  5 us
    ppermute x1, starting transfers between devices, body(): lax.ppermute(asked, BOTH, CORE_PERM)  4.88 us
  transfers between devices with their start and end apart: 19, of which 8 were waited for; matrix products, arithmetic and copies ran while one was open for 0% of the time, Pallas kernels for 2%

profile of v3, /device:TPU:1, one launch (start us, length us, event | category | flops | bytes accessed | tf_op | source)
XLA Modules:
  0.0 137.3 jit_solution(2342625365075936556)
XLA Ops:
  1.6 20.4 %all_to_all.31 = s32[32,1,16]{2,1,0:T(1,128)S(1)} all-to-all(s32[32,1,16]{2,1,0:T(1,128)S(1)} %bitcast.25), channel_id=1, replica_groups=mesh['table'=32,'dp'=8] {'table'}, dimensions={0} | all-to-all | bytes 4096 | tf_op jit(solution)/shard_map/all_to_all | solution.py:417
  22.1 1.4 %shard_map.120 = bf16[512,512]{1,0:T(8,128)(2,1)S(1)} custom-call(s32[32,16]{1,0:T(8,128)S(1)} %bitcast.22, bf16[2048,512]{1,0:T(8,128)(2,1)S(1)} %copy-done.1), custom_call_target="tpu_custom_call" | custom-call | flops 1073741824 | bytes 2623488 | tf_op jit(solution)/shard_map/pallas_call | solution.py:31
  23.5 17.6 %all_to_all.32 = bf16[32,16,512]{2,1,0:T(8,128)(2,1)S(1)} all-to-all(bf16[32,16,512]{2,1,0:T(8,128)(2,1)S(1)} %bitcast.21), channel_id=1, replica_groups=mesh['table'=32,'dp'=8] {'table'}, dimensions={0} | all-to-all | bytes 1048576 | tf_op jit(solution)/shard_map/all_to_all | solution.py:425
  41.2 6.7 %shard_map.121 = (bf16[256,512]{1,0:T(8,128)(2,1)}, bf16[512,512]{1,0:T(8,128)(2,1)S(1)}, bf16[5136,128]{1,0:T(8,128)(2,1)S(1)}, bf16[5136,128]{1,0:T(8,128)(2,1)}) custom-call(s32[1,4]{1,0:T(1,128)S(1)} %bitcast.28, bf16[512,512]{1,0:T(8,128)(2,1)S(1)} %bitcast.20, s32[1,256]{1,0:T(1,128)S(1)} %get-tuple-element.26.placed_ref, ...), custom_call_target="tpu_custom_call" | custom-call | flops 2013265920 | bytes 6827024 | tf_op jit(solution)/shard_map/pallas_call | solution.py:31
  48.7 4.5 %collective-permute-start.2 = (bf16[5136,128]{1,0:T(8,128)(2,1)}, bf16[5136,128]{1,0:T(8,128)(2,1)S(1)}, u32[]{:S(2)}, u32[]{:S(2)}) collective-permute-start(bf16[5136,128]{1,0:T(8,128)(2,1)} %get-tuple-element.30), channel_id=1, source_target_pairs={{0,1},{1,0},{2,3},{3,2},{4,5},{5,4},{6,7},{7,6},{8,9},{9,8},{10,11... | collective-permute-start | bytes 3944456 | tf_op jit(solution)/shard_map/ppermute | solution.py:459
  53.2 3.9 %all-to-all-start.2 = ((bf16[32,16,512]{2,1,0:T(8,128)(2,1)}), bf16[32,16,512]{2,1,0:T(8,128)(2,1)S(1)}, u32[]{:S(2)}, u32[]{:S(2)}) async-start(bf16[32,16,512]{2,1,0:T(8,128)(2,1)} %bitcast.19), calls=%async_computation.2 | async-start | bytes 1048576 | tf_op jit(solution)/shard_map/all_to_all | solution.py:455
  57.1 1.1 shard_map.122
  58.2 1.3 collective-permute-start.3
  59.5 2.6 %collective-permute-start.4 = (bf16[1296,128]{1,0:T(8,128)(2,1)}, bf16[1296,128]{1,0:T(8,128)(2,1)S(1)}, u32[]{:S(2)}, u32[]{:S(2)}) collective-permute-start(bf16[1296,128]{1,0:T(8,128)(2,1)} %get-tuple-element.33), channel_id=1, source_target_pairs={{0,16},{1,5},{2,18},{3,7},{4,20},{5,1},{6,22},{7,3},{8,24},{9,13},... | collective-permute-start | bytes 995336 | tf_op jit(solution)/shard_map/ppermute | solution.py:461
  62.1 1.1 collective-permute-start.5
  63.2 11.0 %all-to-all-done.2 = bf16[32,16,512]{2,1,0:T(8,128)(2,1)S(1)} async-done(((bf16[32,16,512]{2,1,0:T(8,128)(2,1)}), bf16[32,16,512]{2,1,0:T(8,128)(2,1)S(1)}, u32[]{:S(2)}, u32[]{:S(2)}) %all-to-all-start.2) | async-done | bytes 524320 | tf_op jit(solution)/shard_map/all_to_all | solution.py:455
  74.2 1.8 %collective-permute-start.1 = (bf16[512,512]{1,0:T(8,128)(2,1)S(1)}, bf16[512,512]{1,0:T(8,128)(2,1)S(1)}, u32[]{:S(2)}, u32[]{:S(2)}) collective-permute-start(bf16[512,512]{1,0:T(8,128)(2,1)S(1)} %bitcast.17), channel_id=1, source_target_pairs={{0,1},{1,0},{2,3},{3,2},{4,5},{5,4},{6,7},{7,6},{8,9},{9,8},{10,11... | collective-permute-start | bytes 1572872 | tf_op jit(solution)/shard_map/ppermute | solution.py:469
  76.0 0.9 shard_map.123.after_ref
  76.9 4.2 %all-to-all-start.3 = ((bf16[32,48,128]{2,1,0:T(8,128)(2,1)}), bf16[32,48,128]{2,1,0:T(8,128)(2,1)S(1)}, u32[]{:S(2)}, u32[]{:S(2)}) async-start(bf16[32,48,128]{2,1,0:T(8,128)(2,1)} %shard_map.123.after_ref), calls=%async_computation.3 | async-start | bytes 786432 | tf_op jit(solution)/shard_map/all_to_all | solution.py:399
  81.1 4.9 %collective-permute-start = (s32[32,16]{1,0:T(8,128)S(1)}, s32[32,16]{1,0:T(8,128)S(1)}, u32[]{:S(2)}, u32[]{:S(2)}) collective-permute-start(s32[32,16]{1,0:T(8,128)S(1)} %bitcast.23), channel_id=1, source_target_pairs={{0,1},{1,0},{2,3},{3,2},{4,5},{5,4},{6,7},{7,6},{8,9},{9,8},{10,11... | collective-permute-start | bytes 6152 | tf_op jit(solution)/shard_map/ppermute | solution.py:467
  86.0 0.8 collective-permute-done.asked_other_ref
  86.8 1.4 %shard_map.124 = (bf16[256,512]{1,0:T(8,128)(2,1)S(1)}, bf16[256,512]{1,0:T(8,128)(2,1)S(1)}, bf16[256,512]{1,0:T(8,128)(2,1)S(1)}, bf16[256,512]{1,0:T(8,128)(2,1)S(1)}) custom-call(s32[32,16]{1,0:T(8,128)S(1)} %bitcast.24, s32[32,16]{1,0:T(8,128)S(1)} %collective-permute-done.asked_other_ref, bf16[512,512]{1,0:T(8,128)(2,1)S(1)} %bitcast.18, ...), custom_call_target="tpu_custom_call" | custom-call | flops 1073741824 | bytes 2494464 | tf_op jit(solution)/shard_map/pallas_call | solution.py:31
  88.2 2.8 %collective-permute-start.6 = (bf16[256,512]{1,0:T(8,128)(2,1)S(1)}, bf16[256,512]{1,0:T(8,128)(2,1)S(1)}, u32[]{:S(2)}, u32[]{:S(2)}) collective-permute-start(bf16[256,512]{1,0:T(8,128)(2,1)S(1)} %get-tuple-element.37), channel_id=1, source_target_pairs={{0,2},{1,7},{2,4},{3,1},{4,6},{5,3},{6,0},{7,5},{8,10},{9,15},{10,... | collective-permute-start | bytes 786440 | tf_op jit(solution)/shard_map/ppermute | solution.py:474
  91.1 4.2 %collective-permute-done.6.passed_ref = bf16[256,512]{1,0:T(8,128)(2,1)S(1)} collective-permute-done((bf16[256,512]{1,0:T(8,128)(2,1)S(1)}, bf16[256,512]{1,0:T(8,128)(2,1)S(1)}, u32[]{:S(2)}, u32[]{:S(2)}) %collective-permute-start.6) | collective-permute-done | bytes 262176 | tf_op jit(solution)/shard_map/ppermute | solution.py:474
  95.3 0.9 shard_map.125
  96.2 7.9 %all-to-all-start.4 = ((bf16[32,40,128]{2,1,0:T(8,128)(2,1)}), bf16[32,40,128]{2,1,0:T(8,128)(2,1)S(1)}, u32[]{:S(2)}, u32[]{:S(2)}) async-start(bf16[32,40,128]{2,1,0:T(8,128)(2,1)} %get-tuple-element.40), calls=%async_computation.4 | async-start | bytes 655360 | tf_op jit(solution)/shard_map/all_to_all | solution.py:399
  104.2 1.4 %collective-permute-start.8 = (bf16[256,512]{1,0:T(8,128)(2,1)S(1)}, bf16[256,512]{1,0:T(8,128)(2,1)S(1)}, u32[]{:S(2)}, u32[]{:S(2)}) collective-permute-start(bf16[256,512]{1,0:T(8,128)(2,1)S(1)} %get-tuple-element.39), channel_id=1, source_target_pairs={{0,6},{1,3},{2,0},{3,5},{4,2},{5,7},{6,4},{7,1},{8,14},{9,11},{10,... | collective-permute-start | bytes 786440 | tf_op jit(solution)/shard_map/ppermute | solution.py:475
  105.6 1.6 %collective-permute-start.7 = (bf16[256,512]{1,0:T(8,128)(2,1)S(1)}, bf16[256,512]{1,0:T(8,128)(2,1)S(1)}, u32[]{:S(2)}, u32[]{:S(2)}) collective-permute-start(bf16[256,512]{1,0:T(8,128)(2,1)S(1)} %get-tuple-element.38), channel_id=1, source_target_pairs={{0,2},{1,7},{2,4},{3,1},{4,6},{5,3},{6,0},{7,5},{8,10},{9,15},{10,... | collective-permute-start | bytes 786440 | tf_op jit(solution)/shard_map/ppermute | solution.py:488
  107.2 4.2 %collective-permute-done.8.far_ref.refs_2_ = bf16[256,512]{1,0:T(8,128)(2,1)S(1)} collective-permute-done((bf16[256,512]{1,0:T(8,128)(2,1)S(1)}, bf16[256,512]{1,0:T(8,128)(2,1)S(1)}, u32[]{:S(2)}, u32[]{:S(2)}) %collective-permute-start.8) | collective-permute-done | bytes 262176 | tf_op jit(solution)/shard_map/ppermute | solution.py:475
  111.4 3.0 %collective-permute-done.7.near_ref.refs_1_ = bf16[256,512]{1,0:T(8,128)(2,1)S(1)} collective-permute-done((bf16[256,512]{1,0:T(8,128)(2,1)S(1)}, bf16[256,512]{1,0:T(8,128)(2,1)S(1)}, u32[]{:S(2)}, u32[]{:S(2)}) %collective-permute-start.7) | collective-permute-done | bytes 262176 | tf_op jit(solution)/shard_map/ppermute | solution.py:488
  114.6 3.5 %collective-permute-start.11 = (bf16[1280,128]{1,0:T(8,128)(2,1)S(1)}, bf16[1280,128]{1,0:T(8,128)(2,1)S(1)}, u32[]{:S(2)}, u32[]{:S(2)}) collective-permute-start(bf16[1280,128]{1,0:T(8,128)(2,1)S(1)} %shard_map.126.refs_3_), channel_id=1, source_target_pairs={{0,24},{1,7},{2,26},{3,1},{4,28},{5,3},{6,30},{7,5},{8,0},{9,15},{... | collective-permute-start | bytes 983048 | tf_op jit(solution)/shard_map/ppermute | solution.py:500
  118.7 4.4 %collective-permute-start.12 = (bf16[1280,128]{1,0:T(8,128)(2,1)S(1)}, bf16[1280,128]{1,0:T(8,128)(2,1)S(1)}, u32[]{:S(2)}, u32[]{:S(2)}) collective-permute-start(bf16[1280,128]{1,0:T(8,128)(2,1)S(1)} %shard_map.126.refs_3_), channel_id=1, source_target_pairs={{0,1},{1,0},{2,3},{3,2},{4,5},{5,4},{6,7},{7,6},{8,9},{9,8},{10,11... | collective-permute-start | bytes 983048 | tf_op jit(solution)/shard_map/ppermute | solution.py:501
  123.1 2.5 %collective-permute-done.11.refs_6_ = bf16[1280,128]{1,0:T(8,128)(2,1)S(1)} collective-permute-done((bf16[1280,128]{1,0:T(8,128)(2,1)S(1)}, bf16[1280,128]{1,0:T(8,128)(2,1)S(1)}, u32[]{:S(2)}, u32[]{:S(2)}) %collective-permute-start.11) | collective-permute-done | bytes 327712 | tf_op jit(solution)/shard_map/ppermute | solution.py:500
  125.6 3.8 %collective-permute-start.15 = (bf16[1280,128]{1,0:T(8,128)(2,1)S(1)}, bf16[1280,128]{1,0:T(8,128)(2,1)S(1)}, u32[]{:S(2)}, u32[]{:S(2)}) collective-permute-start(bf16[1280,128]{1,0:T(8,128)(2,1)S(1)} %collective-permute-done.11.refs_6_), channel_id=1, source_target_pairs={{0,1},{1,0},{2,3},{3,2},{4,5},{5,4},{6,7},{7,6},{8,9},{9,8},{10,11... | collective-permute-start | bytes 983048 | tf_op jit(solution)/shard_map/ppermute | solution.py:501
  130.0 3.4 %collective-permute-start.13 = (bf16[1280,128]{1,0:T(8,128)(2,1)S(1)}, bf16[1280,128]{1,0:T(8,128)(2,1)S(1)}, u32[]{:S(2)}, u32[]{:S(2)}) collective-permute-start(bf16[1280,128]{1,0:T(8,128)(2,1)S(1)} %collective-permute-done.9.refs_4_), channel_id=1, source_target_pairs={{0,1},{1,0},{2,3},{3,2},{4,5},{5,4},{6,7},{7,6},{8,9},{9,8},{10,11... | collective-permute-start | bytes 983048 | tf_op jit(solution)/shard_map/ppermute | solution.py:501
  133.4 1.2 collective-permute-done.13.refs_8_
  134.6 2.5 %shard_map.127 = (f32[256,512]{1,0:T(8,128)}, bf16[512,2048]{1,0:T(8,128)(2,1)}, bf16[512,512]{1,0:T(8,128)(2,1)}) custom-call(bf16[256,512]{1,0:T(8,128)(2,1)S(1)} %get-tuple-element.35.refs_0_, bf16[256,512]{1,0:T(8,128)(2,1)S(1)} %collective-permute-done.7.near_ref.refs_1_, bf16[256,512]{1,0:T(8,128)(2,1)S(1)} %collective-permute-done.8.far_ref.refs_2_, ...), custom_call_target="tpu_custom_call" | custom-call | bytes 6553600 | tf_op jit(solution)/shard_map/pallas_call | solution.py:31
  (32 shorter events, 3.2 us)
Async XLA Ops:
  1.3 20.7 %copy-start.1 = (bf16[2048,512]{1,0:T(8,128)(2,1)S(1)}, bf16[2048,512]{1,0:T(8,128)(2,1)}, u32[]{:S(2)}) copy-start(bf16[2048,512]{1,0:T(8,128)(2,1)} %table_ref.1) | copy-start | bytes 6291460
  22.0 19.1 %copy-start.2 = (bf16[512,2048]{1,0:T(8,128)(2,1)S(1)}, bf16[512,2048]{1,0:T(8,128)(2,1)}, u32[]{:S(2)}) copy-start(bf16[512,2048]{1,0:T(8,128)(2,1)} %w_proj_ref.1) | copy-start | bytes 6291460
  22.0 19.1 %copy-start.3 = (bf16[512,512]{1,0:T(8,128)(2,1)S(1)}, bf16[512,512]{1,0:T(8,128)(2,1)}, u32[]{:S(2)}) copy-start(bf16[512,512]{1,0:T(8,128)(2,1)} %w_out_ref.1) | copy-start | bytes 1572868
  22.0 19.1 %copy-start.4 = (bf16[1,256,512]{2,1,0:T(8,128)(2,1)S(1)}, bf16[1,256,512]{2,1,0:T(8,128)(2,1)}, u32[]{:S(2)}) copy-start(bf16[1,256,512]{2,1,0:T(8,128)(2,1)} %param.12) | copy-start | bytes 786436
  22.0 19.1 %copy-start.5 = (f32[512]{0:T(512)S(1)}, f32[512]{0:T(512)}, u32[]{:S(2)}) copy-start(f32[512]{0:T(512)} %param.15) | copy-start | bytes 6148
  22.0 19.1 %copy-start.6 = (s32[1,1,4]{2,1,0:T(1,128)S(1)}, s32[1,1,4]{2,1,0:T(1,128)}, u32[]{:S(2)}) copy-start(s32[1,1,4]{2,1,0:T(1,128)} %param.11) | copy-start | bytes 52
  47.9 0.8 copy-start
  48.7 8.5 %collective-permute-start.2 = (bf16[5136,128]{1,0:T(8,128)(2,1)}, bf16[5136,128]{1,0:T(8,128)(2,1)S(1)}, u32[]{:S(2)}, u32[]{:S(2)}) collective-permute-start(bf16[5136,128]{1,0:T(8,128)(2,1)} %get-tuple-element.30), channel_id=1, source_target_pairs={{0,1},{1,0},{2,3},{3,2},{4,5},{5,4},{6,7},{7,6},{8,9},{9,8},{10,11... | collective-permute-start | bytes 3944456 | tf_op jit(solution)/shard_map/ppermute | solution.py:459
  53.2 21.0 %all-to-all-start.2 = ((bf16[32,16,512]{2,1,0:T(8,128)(2,1)}), bf16[32,16,512]{2,1,0:T(8,128)(2,1)S(1)}, u32[]{:S(2)}, u32[]{:S(2)}) async-start(bf16[32,16,512]{2,1,0:T(8,128)(2,1)} %bitcast.19), calls=%async_computation.2 | async-start | bytes 1048576 | tf_op jit(solution)/shard_map/all_to_all | solution.py:455
  58.2 17.8 %collective-permute-start.3 = (bf16[1296,128]{1,0:T(8,128)(2,1)}, bf16[1296,128]{1,0:T(8,128)(2,1)S(1)}, u32[]{:S(2)}, u32[]{:S(2)}) collective-permute-start(bf16[1296,128]{1,0:T(8,128)(2,1)} %get-tuple-element.32), channel_id=1, source_target_pairs={{0,8},{1,3},{2,10},{3,5},{4,12},{5,7},{6,14},{7,1},{8,16},{9,11},{... | collective-permute-start | bytes 995336 | tf_op jit(solution)/shard_map/ppermute | solution.py:461
  59.5 16.5 %collective-permute-start.4 = (bf16[1296,128]{1,0:T(8,128)(2,1)}, bf16[1296,128]{1,0:T(8,128)(2,1)S(1)}, u32[]{:S(2)}, u32[]{:S(2)}) collective-permute-start(bf16[1296,128]{1,0:T(8,128)(2,1)} %get-tuple-element.33), channel_id=1, source_target_pairs={{0,16},{1,5},{2,18},{3,7},{4,20},{5,1},{6,22},{7,3},{8,24},{9,13},... | collective-permute-start | bytes 995336 | tf_op jit(solution)/shard_map/ppermute | solution.py:461
  62.1 13.9 %collective-permute-start.5 = (bf16[1296,128]{1,0:T(8,128)(2,1)}, bf16[1296,128]{1,0:T(8,128)(2,1)S(1)}, u32[]{:S(2)}, u32[]{:S(2)}) collective-permute-start(bf16[1296,128]{1,0:T(8,128)(2,1)} %get-tuple-element.34), channel_id=1, source_target_pairs={{0,24},{1,7},{2,26},{3,1},{4,28},{5,3},{6,30},{7,5},{8,0},{9,15},{... | collective-permute-start | bytes 995336 | tf_op jit(solution)/shard_map/ppermute | solution.py:461
  74.2 12.6 %collective-permute-start.1 = (bf16[512,512]{1,0:T(8,128)(2,1)S(1)}, bf16[512,512]{1,0:T(8,128)(2,1)S(1)}, u32[]{:S(2)}, u32[]{:S(2)}) collective-permute-start(bf16[512,512]{1,0:T(8,128)(2,1)S(1)} %bitcast.17), channel_id=1, source_target_pairs={{0,1},{1,0},{2,3},{3,2},{4,5},{5,4},{6,7},{7,6},{8,9},{9,8},{10,11... | collective-permute-start | bytes 1572872 | tf_op jit(solution)/shard_map/ppermute | solution.py:469
  76.9 18.4 %all-to-all-start.3 = ((bf16[32,48,128]{2,1,0:T(8,128)(2,1)}), bf16[32,48,128]{2,1,0:T(8,128)(2,1)S(1)}, u32[]{:S(2)}, u32[]{:S(2)}) async-start(bf16[32,48,128]{2,1,0:T(8,128)(2,1)} %shard_map.123.after_ref), calls=%async_computation.3 | async-start | bytes 786432 | tf_op jit(solution)/shard_map/all_to_all | solution.py:399
  81.1 5.7 %collective-permute-start = (s32[32,16]{1,0:T(8,128)S(1)}, s32[32,16]{1,0:T(8,128)S(1)}, u32[]{:S(2)}, u32[]{:S(2)}) collective-permute-start(s32[32,16]{1,0:T(8,128)S(1)} %bitcast.23), channel_id=1, source_target_pairs={{0,1},{1,0},{2,3},{3,2},{4,5},{5,4},{6,7},{7,6},{8,9},{9,8},{10,11... | collective-permute-start | bytes 6152 | tf_op jit(solution)/shard_map/ppermute | solution.py:467
  88.2 7.1 %collective-permute-start.6 = (bf16[256,512]{1,0:T(8,128)(2,1)S(1)}, bf16[256,512]{1,0:T(8,128)(2,1)S(1)}, u32[]{:S(2)}, u32[]{:S(2)}) collective-permute-start(bf16[256,512]{1,0:T(8,128)(2,1)S(1)} %get-tuple-element.37), channel_id=1, source_target_pairs={{0,2},{1,7},{2,4},{3,1},{4,6},{5,3},{6,0},{7,5},{8,10},{9,15},{10,... | collective-permute-start | bytes 786440 | tf_op jit(solution)/shard_map/ppermute | solution.py:474
  96.2 18.3 %all-to-all-start.4 = ((bf16[32,40,128]{2,1,0:T(8,128)(2,1)}), bf16[32,40,128]{2,1,0:T(8,128)(2,1)S(1)}, u32[]{:S(2)}, u32[]{:S(2)}) async-start(bf16[32,40,128]{2,1,0:T(8,128)(2,1)} %get-tuple-element.40), calls=%async_computation.4 | async-start | bytes 655360 | tf_op jit(solution)/shard_map/all_to_all | solution.py:399
  104.2 7.2 %collective-permute-start.8 = (bf16[256,512]{1,0:T(8,128)(2,1)S(1)}, bf16[256,512]{1,0:T(8,128)(2,1)S(1)}, u32[]{:S(2)}, u32[]{:S(2)}) collective-permute-start(bf16[256,512]{1,0:T(8,128)(2,1)S(1)} %get-tuple-element.39), channel_id=1, source_target_pairs={{0,6},{1,3},{2,0},{3,5},{4,2},{5,7},{6,4},{7,1},{8,14},{9,11},{10,... | collective-permute-start | bytes 786440 | tf_op jit(solution)/shard_map/ppermute | solution.py:475
  105.6 8.8 %collective-permute-start.7 = (bf16[256,512]{1,0:T(8,128)(2,1)S(1)}, bf16[256,512]{1,0:T(8,128)(2,1)S(1)}, u32[]{:S(2)}, u32[]{:S(2)}) collective-permute-start(bf16[256,512]{1,0:T(8,128)(2,1)S(1)} %get-tuple-element.38), channel_id=1, source_target_pairs={{0,2},{1,7},{2,4},{3,1},{4,6},{5,3},{6,0},{7,5},{8,10},{9,15},{10,... | collective-permute-start | bytes 786440 | tf_op jit(solution)/shard_map/ppermute | solution.py:488
  114.6 11.0 %collective-permute-start.11 = (bf16[1280,128]{1,0:T(8,128)(2,1)S(1)}, bf16[1280,128]{1,0:T(8,128)(2,1)S(1)}, u32[]{:S(2)}, u32[]{:S(2)}) collective-permute-start(bf16[1280,128]{1,0:T(8,128)(2,1)S(1)} %shard_map.126.refs_3_), channel_id=1, source_target_pairs={{0,24},{1,7},{2,26},{3,1},{4,28},{5,3},{6,30},{7,5},{8,0},{9,15},{... | collective-permute-start | bytes 983048 | tf_op jit(solution)/shard_map/ppermute | solution.py:500
  118.1 11.3 %collective-permute-start.10 = (bf16[1280,128]{1,0:T(8,128)(2,1)S(1)}, bf16[1280,128]{1,0:T(8,128)(2,1)S(1)}, u32[]{:S(2)}, u32[]{:S(2)}) collective-permute-start(bf16[1280,128]{1,0:T(8,128)(2,1)S(1)} %shard_map.126.refs_3_), channel_id=1, source_target_pairs={{0,16},{1,5},{2,18},{3,7},{4,20},{5,1},{6,22},{7,3},{8,24},{9,13},... | collective-permute-start | bytes 983048 | tf_op jit(solution)/shard_map/ppermute | solution.py:500
  118.1 11.9 %collective-permute-start.9 = (bf16[1280,128]{1,0:T(8,128)(2,1)S(1)}, bf16[1280,128]{1,0:T(8,128)(2,1)S(1)}, u32[]{:S(2)}, u32[]{:S(2)}) collective-permute-start(bf16[1280,128]{1,0:T(8,128)(2,1)S(1)} %shard_map.126.refs_3_), channel_id=1, source_target_pairs={{0,8},{1,3},{2,10},{3,5},{4,12},{5,7},{6,14},{7,1},{8,16},{9,11},{... | collective-permute-start | bytes 983048 | tf_op jit(solution)/shard_map/ppermute | solution.py:500
  118.7 14.7 %collective-permute-start.12 = (bf16[1280,128]{1,0:T(8,128)(2,1)S(1)}, bf16[1280,128]{1,0:T(8,128)(2,1)S(1)}, u32[]{:S(2)}, u32[]{:S(2)}) collective-permute-start(bf16[1280,128]{1,0:T(8,128)(2,1)S(1)} %shard_map.126.refs_3_), channel_id=1, source_target_pairs={{0,1},{1,0},{2,3},{3,2},{4,5},{5,4},{6,7},{7,6},{8,9},{9,8},{10,11... | collective-permute-start | bytes 983048 | tf_op jit(solution)/shard_map/ppermute | solution.py:501
  125.6 7.8 %collective-permute-start.15 = (bf16[1280,128]{1,0:T(8,128)(2,1)S(1)}, bf16[1280,128]{1,0:T(8,128)(2,1)S(1)}, u32[]{:S(2)}, u32[]{:S(2)}) collective-permute-start(bf16[1280,128]{1,0:T(8,128)(2,1)S(1)} %collective-permute-done.11.refs_6_), channel_id=1, source_target_pairs={{0,1},{1,0},{2,3},{3,2},{4,5},{5,4},{6,7},{7,6},{8,9},{9,8},{10,11... | collective-permute-start | bytes 983048 | tf_op jit(solution)/shard_map/ppermute | solution.py:501
  129.4 4.0 %collective-permute-start.14 = (bf16[1280,128]{1,0:T(8,128)(2,1)S(1)}, bf16[1280,128]{1,0:T(8,128)(2,1)S(1)}, u32[]{:S(2)}, u32[]{:S(2)}) collective-permute-start(bf16[1280,128]{1,0:T(8,128)(2,1)S(1)} %collective-permute-done.10.refs_5_), channel_id=1, source_target_pairs={{0,1},{1,0},{2,3},{3,2},{4,5},{5,4},{6,7},{7,6},{8,9},{9,8},{10,11... | collective-permute-start | bytes 983048 | tf_op jit(solution)/shard_map/ppermute | solution.py:501
  130.0 4.7 %collective-permute-start.13 = (bf16[1280,128]{1,0:T(8,128)(2,1)S(1)}, bf16[1280,128]{1,0:T(8,128)(2,1)S(1)}, u32[]{:S(2)}, u32[]{:S(2)}) collective-permute-start(bf16[1280,128]{1,0:T(8,128)(2,1)S(1)} %collective-permute-done.9.refs_4_), channel_id=1, source_target_pairs={{0,1},{1,0},{2,3},{3,2},{4,5},{5,4},{6,7},{7,6},{8,9},{9,8},{10,11... | collective-permute-start | bytes 983048 | tf_op jit(solution)/shard_map/ppermute | solution.py:501

commit v4 on v3

--- a/solution.py
+++ b/solution.py
@@ -148,8 +148,7 @@
 
 def layer_kernel(
     lengths_ref, returned_ref, placed_ref, upstream_ref, w_proj_ref, w_out_ref, gain_ref,
-    layer_ref, sent_ref, keep_ref, give_ref, slope_ref, acted_ref, grad_pre_ref,
-    left_ref,
+    layer_ref, sent_ref, grad_pre_ref, left_ref, tail_ref, slope_ref, acted_ref,
 ):
     slots = returned_ref.shape[0]
     tokens, width = upstream_ref.shape
@@ -217,13 +216,24 @@
     ).astype(BF16)
     sent_ref[...] = nn(flag(placed == iota((slots, tokens), 0)), row_grads).astype(BF16)
 
+    left_ref[0] = normed.T
+    left_ref[1] = gated.T
+    tail_ref[...] = gain_tail(
+        jnp.concatenate(
+            [grad_gain[:, k * LANES : (k + 1) * LANES] for k in range(width // LANES)], axis=0
+        )
+    )
+
+
+def weights_kernel(left_ref, grad_pre_ref, upstream_ref, tail_ref, keep_ref, give_ref):
+    width = upstream_ref.shape[1]
+    inner = grad_pre_ref.shape[1] // 4
     half = keep_ref.shape[0] - 16
     core = lax.rem(lax.axis_index("dp"), 2)
     rows = width // 2
-    left_ref[0] = normed.T
-    left_ref[1] = gated.T
     blocks = (4 * inner + width) // LANES
     for out_ref, side in ((give_ref, 1 - core), (keep_ref, core)):
+        out_ref[pl.ds(half, 16), :] = tail_ref[...]
         first = pl.multiple_of(side * rows, rows)
         left = left_ref[0, pl.ds(first, rows), :]
         value = nn(left, grad_pre_ref[...])
@@ -232,20 +242,13 @@
                 out_ref[pl.ds((p * blocks + b) * STRIP, STRIP), :] = value[
                     p * STRIP : (p + 1) * STRIP, b * LANES : (b + 1) * LANES
                 ].astype(BF16)
-        value = nn(left_ref[1, pl.ds(first, rows), :], upstream)
+        value = nn(left_ref[1, pl.ds(first, rows), :], upstream_ref[...])
         for b in range(width // LANES):
             for p in range(4):
                 at = (p * blocks + b + 4 * inner // LANES) * STRIP
                 out_ref[pl.ds(at, STRIP), :] = value[
                     p * STRIP : (p + 1) * STRIP, b * LANES : (b + 1) * LANES
                 ].astype(BF16)
-    tail = gain_tail(
-        jnp.concatenate(
-            [grad_gain[:, k * LANES : (k + 1) * LANES] for k in range(width // LANES)], axis=0
-        )
-    )
-    keep_ref[pl.ds(half, 16), :] = tail
-    give_ref[pl.ds(half, 16), :] = tail
 
 
 def gain_tail(grad_gain):
@@ -298,8 +301,11 @@
             out_ref[p + k] = piece.astype(BF16)
 
 
-def turn_kernel(in_ref, near_ref, passed_ref, sum_ref, spread_ref, gain_ref):
+def add_kernel(near_ref, passed_ref, after_ref, sum_ref):
     sum_ref[...] = (near_ref[...].astype(F32) + passed_ref[...].astype(F32)).astype(BF16)
+
+
+def turn_kernel(in_ref, after_ref, spread_ref, gain_ref):
     total = jnp.sum(in_ref[...].astype(F32), axis=0)
     rows = spread_ref.shape[1]
     mine = total[0:rows].astype(BF16)
@@ -427,13 +433,14 @@
     ).reshape(slots, width)
     half = width * (4 * inner + width) // (2 * LANES)
     grad_half = shape((half + 16, LANES), BF16)
-    layer_rows, sent, keep, give = call(
+    layer_rows, sent, grad_pre, left, tail = call(
         layer_kernel,
         [
             shape((tokens, width), BF16),
             shape((slots, width), BF16),
-            grad_half,
-            grad_half,
+            shape((tokens, 4 * inner), BF16),
+            shape((2, width, tokens), BF16),
+            shape((16, LANES), BF16),
         ],
         seq_lengths[0],
         returned,
@@ -443,14 +450,21 @@
         w_out,
         norm_gain.reshape(1, width),
         specs=[SMEM] + [VMEM] * 6,
-        flops=6 * tokens * width * (4 * inner + width),
+        flops=4 * tokens * width * (4 * inner + width),
         transcendentals=tokens * (4 * inner + HEADS * tokens),
         scratch=[
             pltpu.VMEM((tokens, 4 * inner), F32),
             pltpu.VMEM((tokens, 4 * inner), BF16),
-            pltpu.VMEM((tokens, 4 * inner), BF16),
-            pltpu.VMEM((2, width, tokens), BF16),
         ],
+    )
+    keep, give = call(
+        weights_kernel,
+        [grad_half, grad_half],
+        left,
+        grad_pre,
+        cotangent[0],
+        tail,
+        flops=2 * tokens * width * (4 * inner + width),
     )
     got = lax.all_to_all(
         sent.reshape(shards, capacity, width), "table", split_axis=0, concat_axis=0, tiled=True
@@ -474,30 +488,45 @@
     passed = lax.ppermute(two, BOTH, ring_perm(1))
     far = lax.ppermute(far, BOTH, ring_perm(-1))
     grads = swap(grads, SECOND_GROUPS)
-    near, grads, step_gain = call(
+    grads, step_gain = call(
         turn_kernel,
-        [
-            shape((rows, width), BF16),
-            shape((32, half // 128, LANES), BF16),
-            shape((width // LANES, LANES), F32),
-        ],
+        [shape((32, half // 128, LANES), BF16), shape((width // LANES, LANES), F32)],
         grads,
         near,
+        specs=[VMEM, ANY],
+    )
+    (near,) = call(
+        add_kernel,
+        [shape((rows, width), BF16)],
+        near,
         passed,
-    )
-    near = lax.ppermute(near, BOTH, ring_perm(1))
+        grads,
+        specs=[VMEM, VMEM, ANY],
+    )
+    near_sum = near
+    near = lax.ppermute(near_sum, BOTH, ring_perm(1))
     grads = swap(grads, SECOND_GROUPS).reshape(half // 4, LANES)
     (grads,) = call(
         hold_kernel,
         [shape(grads.shape, BF16)],
         grads,
+        near_sum,
+        far,
+        specs=[ANY] * 3,
+        out_specs=[ANY],
+        aliases={0: 0},
+    )
+    mine = [grads] + [lax.ppermute(grads, BOTH, first_perm(d)) for d in (1, 2, 3)]
+    (mine[1],) = call(
+        hold_kernel,
+        [shape(grads.shape, BF16)],
+        mine[1],
         near,
         far,
         specs=[ANY] * 3,
         out_specs=[ANY],
         aliases={0: 0},
     )
-    mine = [grads] + [lax.ppermute(grads, BOTH, first_perm(d)) for d in (1, 2, 3)]
     others = [lax.ppermute(piece, BOTH, CORE_PERM) for piece in mine]
     table_grad, step_proj, step_out = call(
         finish_kernel,

time: 138 us -> 132 us (0.957)
  waiting for transfers between devices: 27.3 us -> 22.3 us
    all_to_all x1, waiting for transfers between devices: 11 us -> 3.38 us  [body(): lax.all_to_all(sent.reshape(shards, capacity, width), 'table', split_axis...]
    ppermute x3, waiting for transfers between devices: 0.01 us -> 7.28 us  [body(): lax.ppermute(parts[d], BOTH, first_perm(d))]
    ppermute x1, starting transfers between devices: 4.88 us -> 0.28 us  [body(): lax.ppermute(asked, BOTH, CORE_PERM)]
    ppermute x1, starting transfers between devices: 1.81 us -> 5.55 us  [body(): lax.ppermute(got, BOTH, CORE_PERM)]
    ppermute x1, waiting for transfers between devices: 3 us -> 0.01 us  [body(): near = lax.ppermute(near_sum, BOTH, ring_perm(1))]
    ppermute x3, waiting for transfers between devices: 2.54 us -> 0.01 us  [body(): lax.ppermute(grads, BOTH, first_perm(d))]
    all_to_all x2, waiting for transfers between devices: 0.2 us -> 2.68 us  [swap(): lax.all_to_all(values, BOTH, split_axis=0, concat_axis=0, tiled=True, axi...]
    ppermute x4, starting transfers between devices: 12.2 us -> 14.6 us  [body(): others = [lax.ppermute(piece, BOTH, CORE_PERM) for piece in mine]]
  transfers between devices with their start and end apart: 19 -> 19, of which waited for: 8 -> 9; matrix products, arithmetic and copies ran while one was open for 0% -> 0% of each run, Pallas kernels for 2% -> 2%
where the time goes in v4:
time: 132 us
  starting transfers between devices  54.5 us (41%)
  blocking collectives  38 us (29%)
  waiting for transfers between devices  22.3 us (17%)
  Pallas kernels  15.1 us (11%)
    all_to_all x1, blocking collectives, body(): lax.all_to_all(requests, 'table', split_axis=0, concat_axis=0, tiled=True)  20.4 us
    all_to_all x1, blocking collectives, body(): lax.all_to_all(picked.reshape(shards, capacity, width), 'table', split_ax...  17.6 us
    pallas_call x12, Pallas kernels, call(): pl.pallas_call(kernel, out_shape=outs, in_specs=specs if specs is not Non...  15.1 us
    ppermute x4, starting transfers between devices, body(): others = [lax.ppermute(piece, BOTH, CORE_PERM) for piece in mine]  14.6 us
    all_to_all x2, starting transfers between devices, swap(): lax.all_to_all(values, BOTH, split_axis=0, concat_axis=0, tiled=True, axi...  12.4 us
    ppermute x3, waiting for transfers between devices, body(): lax.ppermute(parts[d], BOTH, first_perm(d))  7.28 us
    ppermute x1, starting transfers between devices, body(): lax.ppermute(got, BOTH, CORE_PERM)  5.55 us
    ppermute x3, starting transfers between devices, body(): lax.ppermute(parts[d], BOTH, first_perm(d))  5.07 us
  transfers between devices with their start and end apart: 19, of which 9 were waited for; matrix products, arithmetic and copies ran while one was open for 0% of the time, Pallas kernels for 2%

profile of v4, /device:TPU:1, one launch (start us, length us, event | category | flops | bytes accessed | tf_op | source)
XLA Modules:
  0.0 131.5 jit_solution(15513799271491055274)
XLA Ops:
  1.6 20.4 %all_to_all.31 = s32[32,1,16]{2,1,0:T(1,128)S(1)} all-to-all(s32[32,1,16]{2,1,0:T(1,128)S(1)} %bitcast.25), channel_id=1, replica_groups=mesh['table'=32,'dp'=8] {'table'}, dimensions={0} | all-to-all | bytes 4096 | tf_op jit(solution)/shard_map/all_to_all | solution.py:423
  22.1 1.4 %shard_map.120 = bf16[512,512]{1,0:T(8,128)(2,1)S(1)} custom-call(s32[32,16]{1,0:T(8,128)S(1)} %bitcast.22, bf16[2048,512]{1,0:T(8,128)(2,1)S(1)} %copy-done.1), custom_call_target="tpu_custom_call" | custom-call | flops 1073741824 | bytes 2623488 | tf_op jit(solution)/shard_map/pallas_call | solution.py:31
  23.5 17.6 %all_to_all.32 = bf16[32,16,512]{2,1,0:T(8,128)(2,1)S(1)} all-to-all(bf16[32,16,512]{2,1,0:T(8,128)(2,1)S(1)} %bitcast.21), channel_id=1, replica_groups=mesh['table'=32,'dp'=8] {'table'}, dimensions={0} | all-to-all | bytes 1048576 | tf_op jit(solution)/shard_map/all_to_all | solution.py:431
  41.2 5.4 %shard_map.121 = (bf16[256,512]{1,0:T(8,128)(2,1)}, bf16[512,512]{1,0:T(8,128)(2,1)S(1)}, bf16[256,2048]{1,0:T(8,128)(2,1)S(1)}, bf16[2,512,256]{2,1,0:T(8,128)(2,1)S(1)}, bf16[16,128]{1,0:T(8,128)(2,1)S(1)}) custom-call(s32[1,4]{1,0:T(1,128)S(1)} %bitcast.29, bf16[512,512]{1,0:T(8,128)(2,1)S(1)} %bitcast.20, s32[1,256]{1,0:T(1,128)S(1)} %get-tuple-element.28.placed_ref, ...), custom_call_target="tpu_custom_call" | custom-call | flops 1342177280 | bytes 5774352 | tf_op jit(solution)/shard_map/pallas_call | solution.py:31
  46.6 1.8 %shard_map.122 = (bf16[5136,128]{1,0:T(8,128)(2,1)S(1)}, bf16[5136,128]{1,0:T(8,128)(2,1)}) custom-call(bf16[2,512,256]{2,1,0:T(8,128)(2,1)S(1)} %get-tuple-element.31.left_ref, bf16[256,2048]{1,0:T(8,128)(2,1)S(1)} %get-tuple-element.32.grad_pre_ref, bf16[256,512]{1,0:T(8,128)(2,1)S(1)} %bitcast.27, bf16[16,128]{1,0:T(8,128)(2,1)S(1)} %get-tuple-element.33.tail_ref), custom_call_target="tpu_custom_call" | custom-call | flops 671088640 | bytes 4468736 | tf_op jit(solution)/shard_map/pallas_call | solution.py:31
  48.4 4.5 %collective-permute-start.2 = (bf16[5136,128]{1,0:T(8,128)(2,1)}, bf16[5136,128]{1,0:T(8,128)(2,1)S(1)}, u32[]{:S(2)}, u32[]{:S(2)}) collective-permute-start(bf16[5136,128]{1,0:T(8,128)(2,1)} %get-tuple-element.35), channel_id=1, source_target_pairs={{0,1},{1,0},{2,3},{3,2},{4,5},{5,4},{6,7},{7,6},{8,9},{9,8},{10,11... | collective-permute-start | bytes 3944456 | tf_op jit(solution)/shard_map/ppermute | solution.py:473
  53.0 3.9 %all-to-all-start.2 = ((bf16[32,16,512]{2,1,0:T(8,128)(2,1)}), bf16[32,16,512]{2,1,0:T(8,128)(2,1)S(1)}, u32[]{:S(2)}, u32[]{:S(2)}) async-start(bf16[32,16,512]{2,1,0:T(8,128)(2,1)} %bitcast.19), calls=%async_computation.2 | async-start | bytes 1048576 | tf_op jit(solution)/shard_map/all_to_all | solution.py:469
  57.3 1.4 %collective-permute-start.3 = (bf16[1296,128]{1,0:T(8,128)(2,1)S(1)}, bf16[1296,128]{1,0:T(8,128)(2,1)S(1)}, u32[]{:S(2)}, u32[]{:S(2)}) collective-permute-start(bf16[1296,128]{1,0:T(8,128)(2,1)S(1)} %get-tuple-element.37), channel_id=1, source_target_pairs={{0,8},{1,3},{2,10},{3,5},{4,12},{5,7},{6,14},{7,1},{8,16},{9,11},{... | collective-permute-start | bytes 995336 | tf_op jit(solution)/shard_map/ppermute | solution.py:475
  58.6 2.6 %collective-permute-start.4 = (bf16[1296,128]{1,0:T(8,128)(2,1)S(1)}, bf16[1296,128]{1,0:T(8,128)(2,1)S(1)}, u32[]{:S(2)}, u32[]{:S(2)}) collective-permute-start(bf16[1296,128]{1,0:T(8,128)(2,1)S(1)} %get-tuple-element.38), channel_id=1, source_target_pairs={{0,16},{1,5},{2,18},{3,7},{4,20},{5,1},{6,22},{7,3},{8,24},{9,13},... | collective-permute-start | bytes 995336 | tf_op jit(solution)/shard_map/ppermute | solution.py:475
  61.3 1.1 collective-permute-start.5
  62.4 2.6 %collective-permute-done.3.refs_1_ = bf16[1296,128]{1,0:T(8,128)(2,1)S(1)} collective-permute-done((bf16[1296,128]{1,0:T(8,128)(2,1)S(1)}, bf16[1296,128]{1,0:T(8,128)(2,1)S(1)}, u32[]{:S(2)}, u32[]{:S(2)}) %collective-permute-start.3) | collective-permute-done | bytes 331808 | tf_op jit(solution)/shard_map/ppermute | solution.py:475
  64.9 4.7 %collective-permute-done.4.refs_2_ = bf16[1296,128]{1,0:T(8,128)(2,1)S(1)} collective-permute-done((bf16[1296,128]{1,0:T(8,128)(2,1)S(1)}, bf16[1296,128]{1,0:T(8,128)(2,1)S(1)}, u32[]{:S(2)}, u32[]{:S(2)}) %collective-permute-start.4) | collective-permute-done | bytes 331808 | tf_op jit(solution)/shard_map/ppermute | solution.py:475
  69.6 0.9 shard_map.124.after_ref
  70.6 3.4 %all-to-all-done.2 = bf16[32,16,512]{2,1,0:T(8,128)(2,1)S(1)} async-done(((bf16[32,16,512]{2,1,0:T(8,128)(2,1)}), bf16[32,16,512]{2,1,0:T(8,128)(2,1)S(1)}, u32[]{:S(2)}, u32[]{:S(2)}) %all-to-all-start.2) | async-done | bytes 524320 | tf_op jit(solution)/shard_map/all_to_all | solution.py:469
  73.9 5.6 %all-to-all-start.3 = ((bf16[32,48,128]{2,1,0:T(8,128)(2,1)}), bf16[32,48,128]{2,1,0:T(8,128)(2,1)S(1)}, u32[]{:S(2)}, u32[]{:S(2)}) async-start(bf16[32,48,128]{2,1,0:T(8,128)(2,1)} %shard_map.124.after_ref), calls=%async_computation.3 | async-start | bytes 786432 | tf_op jit(solution)/shard_map/all_to_all | solution.py:405
  79.5 5.5 %collective-permute-start.1 = (bf16[512,512]{1,0:T(8,128)(2,1)S(1)}, bf16[512,512]{1,0:T(8,128)(2,1)S(1)}, u32[]{:S(2)}, u32[]{:S(2)}) collective-permute-start(bf16[512,512]{1,0:T(8,128)(2,1)S(1)} %bitcast.17), channel_id=1, source_target_pairs={{0,1},{1,0},{2,3},{3,2},{4,5},{5,4},{6,7},{7,6},{8,9},{9,8},{10,11... | collective-permute-start | bytes 1572872 | tf_op jit(solution)/shard_map/ppermute | solution.py:483
  85.4 1.3 collective-permute-done.asked_other_ref
  86.7 1.4 %shard_map.125 = (bf16[256,512]{1,0:T(8,128)(2,1)S(1)}, bf16[256,512]{1,0:T(8,128)(2,1)S(1)}, bf16[256,512]{1,0:T(8,128)(2,1)S(1)}, bf16[256,512]{1,0:T(8,128)(2,1)S(1)}) custom-call(s32[32,16]{1,0:T(8,128)S(1)} %bitcast.24, s32[32,16]{1,0:T(8,128)S(1)} %collective-permute-done.asked_other_ref, bf16[512,512]{1,0:T(8,128)(2,1)S(1)} %bitcast.18, ...), custom_call_target="tpu_custom_call" | custom-call | flops 1073741824 | bytes 2494464 | tf_op jit(solution)/shard_map/pallas_call | solution.py:31
  88.0 1.7 %all-to-all-done.3.in_ref = bf16[32,48,128]{2,1,0:T(8,128)(2,1)S(1)} async-done(((bf16[32,48,128]{2,1,0:T(8,128)(2,1)}), bf16[32,48,128]{2,1,0:T(8,128)(2,1)S(1)}, u32[]{:S(2)}, u32[]{:S(2)}) %all-to-all-start.3) | async-done | bytes 393248 | tf_op jit(solution)/shard_map/all_to_all | solution.py:405
  90.6 6.8 %all-to-all-start.4 = ((bf16[32,40,128]{2,1,0:T(8,128)(2,1)}), bf16[32,40,128]{2,1,0:T(8,128)(2,1)S(1)}, u32[]{:S(2)}, u32[]{:S(2)}) async-start(bf16[32,40,128]{2,1,0:T(8,128)(2,1)} %get-tuple-element.43.after_ref), calls=%async_computation.4 | async-start | bytes 655360 | tf_op jit(solution)/shard_map/all_to_all | solution.py:405
  97.4 2.6 %collective-permute-start.6 = (bf16[256,512]{1,0:T(8,128)(2,1)S(1)}, bf16[256,512]{1,0:T(8,128)(2,1)S(1)}, u32[]{:S(2)}, u32[]{:S(2)}) collective-permute-start(bf16[256,512]{1,0:T(8,128)(2,1)S(1)} %get-tuple-element.42), channel_id=1, source_target_pairs={{0,2},{1,7},{2,4},{3,1},{4,6},{5,3},{6,0},{7,5},{8,10},{9,15},{10,... | collective-permute-start | bytes 786440 | tf_op jit(solution)/shard_map/ppermute | solution.py:488
  99.9 3.3 %collective-permute-done.6.passed_ref = bf16[256,512]{1,0:T(8,128)(2,1)S(1)} collective-permute-done((bf16[256,512]{1,0:T(8,128)(2,1)S(1)}, bf16[256,512]{1,0:T(8,128)(2,1)S(1)}, u32[]{:S(2)}, u32[]{:S(2)}) %collective-permute-start.6) | collective-permute-done | bytes 262176 | tf_op jit(solution)/shard_map/ppermute | solution.py:488
  103.3 3.1 %collective-permute-done.8.far_ref.refs_2_ = bf16[256,512]{1,0:T(8,128)(2,1)S(1)} collective-permute-done((bf16[256,512]{1,0:T(8,128)(2,1)S(1)}, bf16[256,512]{1,0:T(8,128)(2,1)S(1)}, u32[]{:S(2)}, u32[]{:S(2)}) %collective-permute-start.8) | collective-permute-done | bytes 262176 | tf_op jit(solution)/shard_map/ppermute | solution.py:489
  106.4 0.9 all-to-all-done.4
  107.3 2.5 %collective-permute-start.11 = (bf16[1280,128]{1,0:T(8,128)(2,1)S(1)}, bf16[1280,128]{1,0:T(8,128)(2,1)S(1)}, u32[]{:S(2)}, u32[]{:S(2)}) collective-permute-start(bf16[1280,128]{1,0:T(8,128)(2,1)S(1)} %shard_map.128.refs_3_), channel_id=1, source_target_pairs={{0,24},{1,7},{2,26},{3,1},{4,28},{5,3},{6,30},{7,5},{8,0},{9,15},{... | collective-permute-start | bytes 983048 | tf_op jit(solution)/shard_map/ppermute | solution.py:519
  110.9 2.1 %collective-permute-start.7 = (bf16[256,512]{1,0:T(8,128)(2,1)S(1)}, bf16[256,512]{1,0:T(8,128)(2,1)S(1)}, u32[]{:S(2)}, u32[]{:S(2)}) collective-permute-start(bf16[256,512]{1,0:T(8,128)(2,1)S(1)} %shard_map.127.near_ref), channel_id=1, source_target_pairs={{0,2},{1,7},{2,4},{3,1},{4,6},{5,3},{6,0},{7,5},{8,10},{9,15},{10,... | collective-permute-start | bytes 786440 | tf_op jit(solution)/shard_map/ppermute | solution.py:507
  113.0 5.9 %collective-permute-start.12 = (bf16[1280,128]{1,0:T(8,128)(2,1)S(1)}, bf16[1280,128]{1,0:T(8,128)(2,1)S(1)}, u32[]{:S(2)}, u32[]{:S(2)}) collective-permute-start(bf16[1280,128]{1,0:T(8,128)(2,1)S(1)} %shard_map.128.refs_3_), channel_id=1, source_target_pairs={{0,1},{1,0},{2,3},{3,2},{4,5},{5,4},{6,7},{7,6},{8,9},{9,8},{10,11... | collective-permute-start | bytes 983048 | tf_op jit(solution)/shard_map/ppermute | solution.py:530
  118.9 2.1 %collective-permute-start.15 = (bf16[1280,128]{1,0:T(8,128)(2,1)S(1)}, bf16[1280,128]{1,0:T(8,128)(2,1)S(1)}, u32[]{:S(2)}, u32[]{:S(2)}) collective-permute-start(bf16[1280,128]{1,0:T(8,128)(2,1)S(1)} %collective-permute-done.11.refs_6_), channel_id=1, source_target_pairs={{0,1},{1,0},{2,3},{3,2},{4,5},{5,4},{6,7},{7,6},{8,9},{9,8},{10,11... | collective-permute-start | bytes 983048 | tf_op jit(solution)/shard_map/ppermute | solution.py:530
  120.9 3.2 %collective-permute-start.14 = (bf16[1280,128]{1,0:T(8,128)(2,1)S(1)}, bf16[1280,128]{1,0:T(8,128)(2,1)S(1)}, u32[]{:S(2)}, u32[]{:S(2)}) collective-permute-start(bf16[1280,128]{1,0:T(8,128)(2,1)S(1)} %collective-permute-done.10.refs_5_), channel_id=1, source_target_pairs={{0,1},{1,0},{2,3},{3,2},{4,5},{5,4},{6,7},{7,6},{8,9},{9,8},{10,11... | collective-permute-start | bytes 983048 | tf_op jit(solution)/shard_map/ppermute | solution.py:530
  124.2 3.4 %collective-permute-start.13 = (bf16[1280,128]{1,0:T(8,128)(2,1)S(1)}, bf16[1280,128]{1,0:T(8,128)(2,1)S(1)}, u32[]{:S(2)}, u32[]{:S(2)}) collective-permute-start(bf16[1280,128]{1,0:T(8,128)(2,1)S(1)} %shard_map.129.refs_4_), channel_id=1, source_target_pairs={{0,1},{1,0},{2,3},{3,2},{4,5},{5,4},{6,7},{7,6},{8,9},{9,8},{10,11... | collective-permute-start | bytes 983048 | tf_op jit(solution)/shard_map/ppermute | solution.py:530
  127.6 1.2 collective-permute-done.13.refs_8_
  128.8 2.5 %shard_map.130 = (f32[256,512]{1,0:T(8,128)}, bf16[512,2048]{1,0:T(8,128)(2,1)}, bf16[512,512]{1,0:T(8,128)(2,1)}) custom-call(bf16[256,512]{1,0:T(8,128)(2,1)S(1)} %get-tuple-element.40.refs_0_, bf16[256,512]{1,0:T(8,128)(2,1)S(1)} %collective-permute-done.7.near_ref.refs_1_, bf16[256,512]{1,0:T(8,128)(2,1)S(1)} %collective-permute-done.8.far_ref.refs_2_, ...), custom_call_target="tpu_custom_call" | custom-call | bytes 6553600 | tf_op jit(solution)/shard_map/pallas_call | solution.py:31
  (35 shorter events, 3.7 us)
Async XLA Ops:
  1.3 20.7 %copy-start.1 = (bf16[2048,512]{1,0:T(8,128)(2,1)S(1)}, bf16[2048,512]{1,0:T(8,128)(2,1)}, u32[]{:S(2)}) copy-start(bf16[2048,512]{1,0:T(8,128)(2,1)} %table_ref.1) | copy-start | bytes 6291460
  22.0 19.1 %copy-start.2 = (bf16[512,2048]{1,0:T(8,128)(2,1)S(1)}, bf16[512,2048]{1,0:T(8,128)(2,1)}, u32[]{:S(2)}) copy-start(bf16[512,2048]{1,0:T(8,128)(2,1)} %w_proj_ref.1) | copy-start | bytes 6291460
  22.0 19.1 %copy-start.3 = (bf16[512,512]{1,0:T(8,128)(2,1)S(1)}, bf16[512,512]{1,0:T(8,128)(2,1)}, u32[]{:S(2)}) copy-start(bf16[512,512]{1,0:T(8,128)(2,1)} %w_out_ref.1) | copy-start | bytes 1572868
  22.0 19.1 %copy-start.4 = (bf16[1,256,512]{2,1,0:T(8,128)(2,1)S(1)}, bf16[1,256,512]{2,1,0:T(8,128)(2,1)}, u32[]{:S(2)}) copy-start(bf16[1,256,512]{2,1,0:T(8,128)(2,1)} %param.12) | copy-start | bytes 786436
  22.0 19.1 %copy-start.5 = (f32[512]{0:T(512)S(1)}, f32[512]{0:T(512)}, u32[]{:S(2)}) copy-start(f32[512]{0:T(512)} %param.15) | copy-start | bytes 6148
  22.0 19.1 %copy-start.6 = (s32[1,1,4]{2,1,0:T(1,128)S(1)}, s32[1,1,4]{2,1,0:T(1,128)}, u32[]{:S(2)}) copy-start(s32[1,1,4]{2,1,0:T(1,128)} %param.11) | copy-start | bytes 52
  46.6 6.4 %copy-start = (bf16[512,512]{1,0:T(8,128)(2,1)}, bf16[512,512]{1,0:T(8,128)(2,1)S(1)}, u32[]{:S(2)}) copy-start(bf16[512,512]{1,0:T(8,128)(2,1)S(1)} %get-tuple-element.30) | copy-start | bytes 1572868
  48.4 8.5 %collective-permute-start.2 = (bf16[5136,128]{1,0:T(8,128)(2,1)}, bf16[5136,128]{1,0:T(8,128)(2,1)S(1)}, u32[]{:S(2)}, u32[]{:S(2)}) collective-permute-start(bf16[5136,128]{1,0:T(8,128)(2,1)} %get-tuple-element.35), channel_id=1, source_target_pairs={{0,1},{1,0},{2,3},{3,2},{4,5},{5,4},{6,7},{7,6},{8,9},{9,8},{10,11... | collective-permute-start | bytes 3944456 | tf_op jit(solution)/shard_map/ppermute | solution.py:473
  53.0 21.0 %all-to-all-start.2 = ((bf16[32,16,512]{2,1,0:T(8,128)(2,1)}), bf16[32,16,512]{2,1,0:T(8,128)(2,1)S(1)}, u32[]{:S(2)}, u32[]{:S(2)}) async-start(bf16[32,16,512]{2,1,0:T(8,128)(2,1)} %bitcast.19), calls=%async_computation.2 | async-start | bytes 1048576 | tf_op jit(solution)/shard_map/all_to_all | solution.py:469
  57.3 7.6 %collective-permute-start.3 = (bf16[1296,128]{1,0:T(8,128)(2,1)S(1)}, bf16[1296,128]{1,0:T(8,128)(2,1)S(1)}, u32[]{:S(2)}, u32[]{:S(2)}) collective-permute-start(bf16[1296,128]{1,0:T(8,128)(2,1)S(1)} %get-tuple-element.37), channel_id=1, source_target_pairs={{0,8},{1,3},{2,10},{3,5},{4,12},{5,7},{6,14},{7,1},{8,16},{9,11},{... | collective-permute-start | bytes 995336 | tf_op jit(solution)/shard_map/ppermute | solution.py:475
  58.6 11.0 %collective-permute-start.4 = (bf16[1296,128]{1,0:T(8,128)(2,1)S(1)}, bf16[1296,128]{1,0:T(8,128)(2,1)S(1)}, u32[]{:S(2)}, u32[]{:S(2)}) collective-permute-start(bf16[1296,128]{1,0:T(8,128)(2,1)S(1)} %get-tuple-element.38), channel_id=1, source_target_pairs={{0,16},{1,5},{2,18},{3,7},{4,20},{5,1},{6,22},{7,3},{8,24},{9,13},... | collective-permute-start | bytes 995336 | tf_op jit(solution)/shard_map/ppermute | solution.py:475
  61.3 8.4 %collective-permute-start.5 = (bf16[1296,128]{1,0:T(8,128)(2,1)S(1)}, bf16[1296,128]{1,0:T(8,128)(2,1)S(1)}, u32[]{:S(2)}, u32[]{:S(2)}) collective-permute-start(bf16[1296,128]{1,0:T(8,128)(2,1)S(1)} %get-tuple-element.39), channel_id=1, source_target_pairs={{0,24},{1,7},{2,26},{3,1},{4,28},{5,3},{6,30},{7,5},{8,0},{9,15},{... | collective-permute-start | bytes 995336 | tf_op jit(solution)/shard_map/ppermute | solution.py:475
  73.9 15.8 %all-to-all-start.3 = ((bf16[32,48,128]{2,1,0:T(8,128)(2,1)}), bf16[32,48,128]{2,1,0:T(8,128)(2,1)S(1)}, u32[]{:S(2)}, u32[]{:S(2)}) async-start(bf16[32,48,128]{2,1,0:T(8,128)(2,1)} %shard_map.124.after_ref), calls=%async_computation.3 | async-start | bytes 786432 | tf_op jit(solution)/shard_map/all_to_all | solution.py:405
  79.5 7.1 %collective-permute-start.1 = (bf16[512,512]{1,0:T(8,128)(2,1)S(1)}, bf16[512,512]{1,0:T(8,128)(2,1)S(1)}, u32[]{:S(2)}, u32[]{:S(2)}) collective-permute-start(bf16[512,512]{1,0:T(8,128)(2,1)S(1)} %bitcast.17), channel_id=1, source_target_pairs={{0,1},{1,0},{2,3},{3,2},{4,5},{5,4},{6,7},{7,6},{8,9},{9,8},{10,11... | collective-permute-start | bytes 1572872 | tf_op jit(solution)/shard_map/ppermute | solution.py:483
  85.1 1.6 %collective-permute-start = (s32[32,16]{1,0:T(8,128)S(1)}, s32[32,16]{1,0:T(8,128)S(1)}, u32[]{:S(2)}, u32[]{:S(2)}) collective-permute-start(s32[32,16]{1,0:T(8,128)S(1)} %bitcast.23), channel_id=1, source_target_pairs={{0,1},{1,0},{2,3},{3,2},{4,5},{5,4},{6,7},{7,6},{8,9},{9,8},{10,11... | collective-permute-start | bytes 6152 | tf_op jit(solution)/shard_map/ppermute | solution.py:481
  90.6 16.7 %all-to-all-start.4 = ((bf16[32,40,128]{2,1,0:T(8,128)(2,1)}), bf16[32,40,128]{2,1,0:T(8,128)(2,1)S(1)}, u32[]{:S(2)}, u32[]{:S(2)}) async-start(bf16[32,40,128]{2,1,0:T(8,128)(2,1)} %get-tuple-element.43.after_ref), calls=%async_computation.4 | async-start | bytes 655360 | tf_op jit(solution)/shard_map/all_to_all | solution.py:405
  97.4 5.9 %collective-permute-start.6 = (bf16[256,512]{1,0:T(8,128)(2,1)S(1)}, bf16[256,512]{1,0:T(8,128)(2,1)S(1)}, u32[]{:S(2)}, u32[]{:S(2)}) collective-permute-start(bf16[256,512]{1,0:T(8,128)(2,1)S(1)} %get-tuple-element.42), channel_id=1, source_target_pairs={{0,2},{1,7},{2,4},{3,1},{4,6},{5,3},{6,0},{7,5},{8,10},{9,15},{10,... | collective-permute-start | bytes 786440 | tf_op jit(solution)/shard_map/ppermute | solution.py:488
  99.9 6.4 %collective-permute-start.8 = (bf16[256,512]{1,0:T(8,128)(2,1)S(1)}, bf16[256,512]{1,0:T(8,128)(2,1)S(1)}, u32[]{:S(2)}, u32[]{:S(2)}) collective-permute-start(bf16[256,512]{1,0:T(8,128)(2,1)S(1)} %get-tuple-element.44), channel_id=1, source_target_pairs={{0,6},{1,3},{2,0},{3,5},{4,2},{5,7},{6,4},{7,1},{8,14},{9,11},{10,... | collective-permute-start | bytes 786440 | tf_op jit(solution)/shard_map/ppermute | solution.py:489
  107.3 11.5 %collective-permute-start.11 = (bf16[1280,128]{1,0:T(8,128)(2,1)S(1)}, bf16[1280,128]{1,0:T(8,128)(2,1)S(1)}, u32[]{:S(2)}, u32[]{:S(2)}) collective-permute-start(bf16[1280,128]{1,0:T(8,128)(2,1)S(1)} %shard_map.128.refs_3_), channel_id=1, source_target_pairs={{0,24},{1,7},{2,26},{3,1},{4,28},{5,3},{6,30},{7,5},{8,0},{9,15},{... | collective-permute-start | bytes 983048 | tf_op jit(solution)/shard_map/ppermute | solution.py:519
  109.8 11.2 %collective-permute-start.10 = (bf16[1280,128]{1,0:T(8,128)(2,1)S(1)}, bf16[1280,128]{1,0:T(8,128)(2,1)S(1)}, u32[]{:S(2)}, u32[]{:S(2)}) collective-permute-start(bf16[1280,128]{1,0:T(8,128)(2,1)S(1)} %shard_map.128.refs_3_), channel_id=1, source_target_pairs={{0,16},{1,5},{2,18},{3,7},{4,20},{5,1},{6,22},{7,3},{8,24},{9,13},... | collective-permute-start | bytes 983048 | tf_op jit(solution)/shard_map/ppermute | solution.py:519
  110.3 13.9 %collective-permute-start.9 = (bf16[1280,128]{1,0:T(8,128)(2,1)S(1)}, bf16[1280,128]{1,0:T(8,128)(2,1)S(1)}, u32[]{:S(2)}, u32[]{:S(2)}) collective-permute-start(bf16[1280,128]{1,0:T(8,128)(2,1)S(1)} %shard_map.128.refs_3_), channel_id=1, source_target_pairs={{0,8},{1,3},{2,10},{3,5},{4,12},{5,7},{6,14},{7,1},{8,16},{9,11},{... | collective-permute-start | bytes 983048 | tf_op jit(solution)/shard_map/ppermute | solution.py:519
  110.9 13.3 %collective-permute-start.7 = (bf16[256,512]{1,0:T(8,128)(2,1)S(1)}, bf16[256,512]{1,0:T(8,128)(2,1)S(1)}, u32[]{:S(2)}, u32[]{:S(2)}) collective-permute-start(bf16[256,512]{1,0:T(8,128)(2,1)S(1)} %shard_map.127.near_ref), channel_id=1, source_target_pairs={{0,2},{1,7},{2,4},{3,1},{4,6},{5,3},{6,0},{7,5},{8,10},{9,15},{10,... | collective-permute-start | bytes 786440 | tf_op jit(solution)/shard_map/ppermute | solution.py:507
  113.0 14.6 %collective-permute-start.12 = (bf16[1280,128]{1,0:T(8,128)(2,1)S(1)}, bf16[1280,128]{1,0:T(8,128)(2,1)S(1)}, u32[]{:S(2)}, u32[]{:S(2)}) collective-permute-start(bf16[1280,128]{1,0:T(8,128)(2,1)S(1)} %shard_map.128.refs_3_), channel_id=1, source_target_pairs={{0,1},{1,0},{2,3},{3,2},{4,5},{5,4},{6,7},{7,6},{8,9},{9,8},{10,11... | collective-permute-start | bytes 983048 | tf_op jit(solution)/shard_map/ppermute | solution.py:530
  118.9 8.7 %collective-permute-start.15 = (bf16[1280,128]{1,0:T(8,128)(2,1)S(1)}, bf16[1280,128]{1,0:T(8,128)(2,1)S(1)}, u32[]{:S(2)}, u32[]{:S(2)}) collective-permute-start(bf16[1280,128]{1,0:T(8,128)(2,1)S(1)} %collective-permute-done.11.refs_6_), channel_id=1, source_target_pairs={{0,1},{1,0},{2,3},{3,2},{4,5},{5,4},{6,7},{7,6},{8,9},{9,8},{10,11... | collective-permute-start | bytes 983048 | tf_op jit(solution)/shard_map/ppermute | solution.py:530
  120.9 6.6 %collective-permute-start.14 = (bf16[1280,128]{1,0:T(8,128)(2,1)S(1)}, bf16[1280,128]{1,0:T(8,128)(2,1)S(1)}, u32[]{:S(2)}, u32[]{:S(2)}) collective-permute-start(bf16[1280,128]{1,0:T(8,128)(2,1)S(1)} %collective-permute-done.10.refs_5_), channel_id=1, source_target_pairs={{0,1},{1,0},{2,3},{3,2},{4,5},{5,4},{6,7},{7,6},{8,9},{9,8},{10,11... | collective-permute-start | bytes 983048 | tf_op jit(solution)/shard_map/ppermute | solution.py:530
  124.2 4.7 %collective-permute-start.13 = (bf16[1280,128]{1,0:T(8,128)(2,1)S(1)}, bf16[1280,128]{1,0:T(8,128)(2,1)S(1)}, u32[]{:S(2)}, u32[]{:S(2)}) collective-permute-start(bf16[1280,128]{1,0:T(8,128)(2,1)S(1)} %shard_map.129.refs_4_), channel_id=1, source_target_pairs={{0,1},{1,0},{2,3},{3,2},{4,5},{5,4},{6,7},{7,6},{8,9},{9,8},{10,11... | collective-permute-start | bytes 983048 | tf_op jit(solution)/shard_map/ppermute | solution.py:530

commit v5 on v4

--- a/solution.py
+++ b/solution.py
@@ -364,7 +364,7 @@
         copy.wait()
 
 
-def hold_kernel(value_ref, near_ref, far_ref, out_ref):
+def hold_kernel(*refs):
     pass
 
 
@@ -511,8 +511,7 @@
         [shape(grads.shape, BF16)],
         grads,
         near_sum,
-        far,
-        specs=[ANY] * 3,
+        specs=[ANY] * 2,
         out_specs=[ANY],
         aliases={0: 0},
     )

time: 132 us -> 132 us (level)
  starting transfers between devices: 54.5 us -> 43.8 us
  waiting for transfers between devices: 22.3 us -> 32.9 us
    ppermute x4, starting transfers between devices: 14.6 us -> 3.32 us  [body(): others = [lax.ppermute(piece, BOTH, CORE_PERM) for piece in mine]]
    ppermute x1, waiting for transfers between devices: 3.05 us -> 10.7 us  [body(): far = lax.ppermute(far, BOTH, ring_perm(-1))]
    all_to_all x2, waiting for transfers between devices: 2.68 us -> 5.73 us  [swap(): lax.all_to_all(values, BOTH, split_axis=0, concat_axis=0, tiled=True, axi...]
    ppermute x1, starting transfers between devices: 0.01 us -> 1.55 us  [body(): far = lax.ppermute(far, BOTH, ring_perm(-1))]
where the time goes in v5:
time: 132 us
  starting transfers between devices  43.8 us (33%)
  blocking collectives  38 us (29%)
  waiting for transfers between devices  32.9 us (25%)
  Pallas kernels  15.1 us (11%)
    all_to_all x1, blocking collectives, body(): lax.all_to_all(requests, 'table', split_axis=0, concat_axis=0, tiled=True)  20.4 us
    all_to_all x1, blocking collectives, body(): lax.all_to_all(picked.reshape(shards, capacity, width), 'table', split_ax...  17.6 us
    pallas_call x12, Pallas kernels, call(): pl.pallas_call(kernel, out_shape=outs, in_specs=specs if specs is not Non...  15.1 us
    all_to_all x2, starting transfers between devices, swap(): lax.all_to_all(values, BOTH, split_axis=0, concat_axis=0, tiled=True, axi...  12.4 us
    ppermute x1, waiting for transfers between devices, body(): far = lax.ppermute(far, BOTH, ring_perm(-1))  10.7 us
    ppermute x3, waiting for transfers between devices, body(): lax.ppermute(parts[d], BOTH, first_perm(d))  7.28 us
    all_to_all x2, waiting for transfers between devices, swap(): lax.all_to_all(values, BOTH, split_axis=0, concat_axis=0, tiled=True, axi...  5.73 us
    ppermute x1, starting transfers between devices, body(): lax.ppermute(got, BOTH, CORE_PERM)  5.55 us
  transfers between devices with their start and end apart: 19, of which 9 were waited for; matrix products, arithmetic and copies ran while one was open for 0% of the time, Pallas kernels for 2%

profile of v5, /device:TPU:1, one launch (start us, length us, event | category | flops | bytes accessed | tf_op | source)
XLA Modules:
  0.0 131.5 jit_solution(9987692336726585946)
XLA Ops:
  0.6 0.7 bitcast_add_fusion.item_ref
  1.6 20.4 %all_to_all.31 = s32[32,1,16]{2,1,0:T(1,128)S(1)} all-to-all(s32[32,1,16]{2,1,0:T(1,128)S(1)} %bitcast.25), channel_id=1, replica_groups=mesh['table'=32,'dp'=8] {'table'}, dimensions={0} | all-to-all | bytes 4096 | tf_op jit(solution)/shard_map/all_to_all | solution.py:423
  22.1 1.4 %shard_map.120 = bf16[512,512]{1,0:T(8,128)(2,1)S(1)} custom-call(s32[32,16]{1,0:T(8,128)S(1)} %bitcast.22, bf16[2048,512]{1,0:T(8,128)(2,1)S(1)} %copy-done.1), custom_call_target="tpu_custom_call" | custom-call | flops 1073741824 | bytes 2623488 | tf_op jit(solution)/shard_map/pallas_call | solution.py:31
  23.5 17.6 %all_to_all.32 = bf16[32,16,512]{2,1,0:T(8,128)(2,1)S(1)} all-to-all(bf16[32,16,512]{2,1,0:T(8,128)(2,1)S(1)} %bitcast.21), channel_id=1, replica_groups=mesh['table'=32,'dp'=8] {'table'}, dimensions={0} | all-to-all | bytes 1048576 | tf_op jit(solution)/shard_map/all_to_all | solution.py:431
  41.2 5.4 %shard_map.121 = (bf16[256,512]{1,0:T(8,128)(2,1)}, bf16[512,512]{1,0:T(8,128)(2,1)S(1)}, bf16[256,2048]{1,0:T(8,128)(2,1)S(1)}, bf16[2,512,256]{2,1,0:T(8,128)(2,1)S(1)}, bf16[16,128]{1,0:T(8,128)(2,1)S(1)}) custom-call(s32[1,4]{1,0:T(1,128)S(1)} %bitcast.29, bf16[512,512]{1,0:T(8,128)(2,1)S(1)} %bitcast.20, s32[1,256]{1,0:T(1,128)S(1)} %get-tuple-element.28.placed_ref, ...), custom_call_target="tpu_custom_call" | custom-call | flops 1342177280 | bytes 5774352 | tf_op jit(solution)/shard_map/pallas_call | solution.py:31
  46.6 1.8 %shard_map.122 = (bf16[5136,128]{1,0:T(8,128)(2,1)S(1)}, bf16[5136,128]{1,0:T(8,128)(2,1)}) custom-call(bf16[2,512,256]{2,1,0:T(8,128)(2,1)S(1)} %get-tuple-element.31.left_ref, bf16[256,2048]{1,0:T(8,128)(2,1)S(1)} %get-tuple-element.32.grad_pre_ref, bf16[256,512]{1,0:T(8,128)(2,1)S(1)} %bitcast.27, bf16[16,128]{1,0:T(8,128)(2,1)S(1)} %get-tuple-element.33.tail_ref), custom_call_target="tpu_custom_call" | custom-call | flops 671088640 | bytes 4468736 | tf_op jit(solution)/shard_map/pallas_call | solution.py:31
  48.4 4.5 %collective-permute-start.2 = (bf16[5136,128]{1,0:T(8,128)(2,1)}, bf16[5136,128]{1,0:T(8,128)(2,1)S(1)}, u32[]{:S(2)}, u32[]{:S(2)}) collective-permute-start(bf16[5136,128]{1,0:T(8,128)(2,1)} %get-tuple-element.35), channel_id=1, source_target_pairs={{0,1},{1,0},{2,3},{3,2},{4,5},{5,4},{6,7},{7,6},{8,9},{9,8},{10,11... | collective-permute-start | bytes 3944456 | tf_op jit(solution)/shard_map/ppermute | solution.py:473
  53.0 3.9 %all-to-all-start.2 = ((bf16[32,16,512]{2,1,0:T(8,128)(2,1)}), bf16[32,16,512]{2,1,0:T(8,128)(2,1)S(1)}, u32[]{:S(2)}, u32[]{:S(2)}) async-start(bf16[32,16,512]{2,1,0:T(8,128)(2,1)} %bitcast.19), calls=%async_computation.2 | async-start | bytes 1048576 | tf_op jit(solution)/shard_map/all_to_all | solution.py:469
  57.3 1.4 %collective-permute-start.3 = (bf16[1296,128]{1,0:T(8,128)(2,1)S(1)}, bf16[1296,128]{1,0:T(8,128)(2,1)S(1)}, u32[]{:S(2)}, u32[]{:S(2)}) collective-permute-start(bf16[1296,128]{1,0:T(8,128)(2,1)S(1)} %get-tuple-element.37), channel_id=1, source_target_pairs={{0,8},{1,3},{2,10},{3,5},{4,12},{5,7},{6,14},{7,1},{8,16},{9,11},{... | collective-permute-start | bytes 995336 | tf_op jit(solution)/shard_map/ppermute | solution.py:475
  58.6 2.6 %collective-permute-start.4 = (bf16[1296,128]{1,0:T(8,128)(2,1)S(1)}, bf16[1296,128]{1,0:T(8,128)(2,1)S(1)}, u32[]{:S(2)}, u32[]{:S(2)}) collective-permute-start(bf16[1296,128]{1,0:T(8,128)(2,1)S(1)} %get-tuple-element.38), channel_id=1, source_target_pairs={{0,16},{1,5},{2,18},{3,7},{4,20},{5,1},{6,22},{7,3},{8,24},{9,13},... | collective-permute-start | bytes 995336 | tf_op jit(solution)/shard_map/ppermute | solution.py:475
  61.3 1.1 collective-permute-start.5
  62.4 2.6 %collective-permute-done.3.refs_1_ = bf16[1296,128]{1,0:T(8,128)(2,1)S(1)} collective-permute-done((bf16[1296,128]{1,0:T(8,128)(2,1)S(1)}, bf16[1296,128]{1,0:T(8,128)(2,1)S(1)}, u32[]{:S(2)}, u32[]{:S(2)}) %collective-permute-start.3) | collective-permute-done | bytes 331808 | tf_op jit(solution)/shard_map/ppermute | solution.py:475
  64.9 4.7 %collective-permute-done.4.refs_2_ = bf16[1296,128]{1,0:T(8,128)(2,1)S(1)} collective-permute-done((bf16[1296,128]{1,0:T(8,128)(2,1)S(1)}, bf16[1296,128]{1,0:T(8,128)(2,1)S(1)}, u32[]{:S(2)}, u32[]{:S(2)}) %collective-permute-start.4) | collective-permute-done | bytes 331808 | tf_op jit(solution)/shard_map/ppermute | solution.py:475
  69.6 0.9 shard_map.124.after_ref
  70.6 3.4 %all-to-all-done.2 = bf16[32,16,512]{2,1,0:T(8,128)(2,1)S(1)} async-done(((bf16[32,16,512]{2,1,0:T(8,128)(2,1)}), bf16[32,16,512]{2,1,0:T(8,128)(2,1)S(1)}, u32[]{:S(2)}, u32[]{:S(2)}) %all-to-all-start.2) | async-done | bytes 524320 | tf_op jit(solution)/shard_map/all_to_all | solution.py:469
  73.9 5.6 %all-to-all-start.3 = ((bf16[32,48,128]{2,1,0:T(8,128)(2,1)}), bf16[32,48,128]{2,1,0:T(8,128)(2,1)S(1)}, u32[]{:S(2)}, u32[]{:S(2)}) async-start(bf16[32,48,128]{2,1,0:T(8,128)(2,1)} %shard_map.124.after_ref), calls=%async_computation.3 | async-start | bytes 786432 | tf_op jit(solution)/shard_map/all_to_all | solution.py:405
  79.5 5.5 %collective-permute-start.1 = (bf16[512,512]{1,0:T(8,128)(2,1)S(1)}, bf16[512,512]{1,0:T(8,128)(2,1)S(1)}, u32[]{:S(2)}, u32[]{:S(2)}) collective-permute-start(bf16[512,512]{1,0:T(8,128)(2,1)S(1)} %bitcast.17), channel_id=1, source_target_pairs={{0,1},{1,0},{2,3},{3,2},{4,5},{5,4},{6,7},{7,6},{8,9},{9,8},{10,11... | collective-permute-start | bytes 1572872 | tf_op jit(solution)/shard_map/ppermute | solution.py:483
  85.4 1.3 collective-permute-done.asked_other_ref
  86.7 1.4 %shard_map.125 = (bf16[256,512]{1,0:T(8,128)(2,1)S(1)}, bf16[256,512]{1,0:T(8,128)(2,1)S(1)}, bf16[256,512]{1,0:T(8,128)(2,1)S(1)}, bf16[256,512]{1,0:T(8,128)(2,1)S(1)}) custom-call(s32[32,16]{1,0:T(8,128)S(1)} %bitcast.24, s32[32,16]{1,0:T(8,128)S(1)} %collective-permute-done.asked_other_ref, bf16[512,512]{1,0:T(8,128)(2,1)S(1)} %bitcast.18, ...), custom_call_target="tpu_custom_call" | custom-call | flops 1073741824 | bytes 2494464 | tf_op jit(solution)/shard_map/pallas_call | solution.py:31
  88.0 1.7 %all-to-all-done.3.in_ref = bf16[32,48,128]{2,1,0:T(8,128)(2,1)S(1)} async-done(((bf16[32,48,128]{2,1,0:T(8,128)(2,1)}), bf16[32,48,128]{2,1,0:T(8,128)(2,1)S(1)}, u32[]{:S(2)}, u32[]{:S(2)}) %all-to-all-start.3) | async-done | bytes 393248 | tf_op jit(solution)/shard_map/all_to_all | solution.py:405
  89.8 0.8 shard_map.126
  90.6 6.8 %all-to-all-start.4 = ((bf16[32,40,128]{2,1,0:T(8,128)(2,1)}), bf16[32,40,128]{2,1,0:T(8,128)(2,1)S(1)}, u32[]{:S(2)}, u32[]{:S(2)}) async-start(bf16[32,40,128]{2,1,0:T(8,128)(2,1)} %get-tuple-element.43.after_ref), calls=%async_computation.4 | async-start | bytes 655360 | tf_op jit(solution)/shard_map/all_to_all | solution.py:405
  97.4 2.6 %collective-permute-start.6 = (bf16[256,512]{1,0:T(8,128)(2,1)S(1)}, bf16[256,512]{1,0:T(8,128)(2,1)S(1)}, u32[]{:S(2)}, u32[]{:S(2)}) collective-permute-start(bf16[256,512]{1,0:T(8,128)(2,1)S(1)} %get-tuple-element.42), channel_id=1, source_target_pairs={{0,2},{1,7},{2,4},{3,1},{4,6},{5,3},{6,0},{7,5},{8,10},{9,15},{10,... | collective-permute-start | bytes 786440 | tf_op jit(solution)/shard_map/ppermute | solution.py:488
  99.9 3.3 %collective-permute-done.6.passed_ref = bf16[256,512]{1,0:T(8,128)(2,1)S(1)} collective-permute-done((bf16[256,512]{1,0:T(8,128)(2,1)S(1)}, bf16[256,512]{1,0:T(8,128)(2,1)S(1)}, u32[]{:S(2)}, u32[]{:S(2)}) %collective-permute-start.6) | collective-permute-done | bytes 262176 | tf_op jit(solution)/shard_map/ppermute | solution.py:488
  103.3 4.0 %all-to-all-done.4 = bf16[32,40,128]{2,1,0:T(8,128)(2,1)S(1)} async-done(((bf16[32,40,128]{2,1,0:T(8,128)(2,1)}), bf16[32,40,128]{2,1,0:T(8,128)(2,1)S(1)}, u32[]{:S(2)}, u32[]{:S(2)}) %all-to-all-start.4) | async-done | bytes 327712 | tf_op jit(solution)/shard_map/all_to_all | solution.py:405
  107.3 2.5 %collective-permute-start.11 = (bf16[1280,128]{1,0:T(8,128)(2,1)S(1)}, bf16[1280,128]{1,0:T(8,128)(2,1)S(1)}, u32[]{:S(2)}, u32[]{:S(2)}) collective-permute-start(bf16[1280,128]{1,0:T(8,128)(2,1)S(1)} %shard_map.128.refs_3_), channel_id=1, source_target_pairs={{0,24},{1,7},{2,26},{3,1},{4,28},{5,3},{6,30},{7,5},{8,0},{9,15},{... | collective-permute-start | bytes 983048 | tf_op jit(solution)/shard_map/ppermute | solution.py:518
  110.9 1.5 %collective-permute-start.8 = (bf16[256,512]{1,0:T(8,128)(2,1)S(1)}, bf16[256,512]{1,0:T(8,128)(2,1)S(1)}, u32[]{:S(2)}, u32[]{:S(2)}) collective-permute-start(bf16[256,512]{1,0:T(8,128)(2,1)S(1)} %get-tuple-element.44), channel_id=1, source_target_pairs={{0,6},{1,3},{2,0},{3,5},{4,2},{5,7},{6,4},{7,1},{8,14},{9,11},{10,... | collective-permute-start | bytes 786440 | tf_op jit(solution)/shard_map/ppermute | solution.py:489
  112.4 1.1 collective-permute-start.7
  113.6 10.7 %collective-permute-done.8.refs_2_ = bf16[256,512]{1,0:T(8,128)(2,1)S(1)} collective-permute-done((bf16[256,512]{1,0:T(8,128)(2,1)S(1)}, bf16[256,512]{1,0:T(8,128)(2,1)S(1)}, u32[]{:S(2)}, u32[]{:S(2)}) %collective-permute-start.8) | collective-permute-done | bytes 262176 | tf_op jit(solution)/shard_map/ppermute | solution.py:489
  124.9 2.7 %collective-permute-start.13 = (bf16[1280,128]{1,0:T(8,128)(2,1)S(1)}, bf16[1280,128]{1,0:T(8,128)(2,1)S(1)}, u32[]{:S(2)}, u32[]{:S(2)}) collective-permute-start(bf16[1280,128]{1,0:T(8,128)(2,1)S(1)} %shard_map.129.refs_4_), channel_id=1, source_target_pairs={{0,1},{1,0},{2,3},{3,2},{4,5},{5,4},{6,7},{7,6},{8,9},{9,8},{10,11... | collective-permute-start | bytes 983048 | tf_op jit(solution)/shard_map/ppermute | solution.py:529
  127.6 1.2 collective-permute-done.13.refs_8_
  128.8 2.5 %shard_map.130 = (f32[256,512]{1,0:T(8,128)}, bf16[512,2048]{1,0:T(8,128)(2,1)}, bf16[512,512]{1,0:T(8,128)(2,1)}) custom-call(bf16[256,512]{1,0:T(8,128)(2,1)S(1)} %get-tuple-element.40.refs_0_, bf16[256,512]{1,0:T(8,128)(2,1)S(1)} %collective-permute-done.7.refs_1_, bf16[256,512]{1,0:T(8,128)(2,1)S(1)} %collective-permute-done.8.refs_2_, ...), custom_call_target="tpu_custom_call" | custom-call | bytes 6553600 | tf_op jit(solution)/shard_map/pallas_call | solution.py:31
  (35 shorter events, 2.8 us)
Async XLA Ops:
  1.3 20.7 %copy-start.1 = (bf16[2048,512]{1,0:T(8,128)(2,1)S(1)}, bf16[2048,512]{1,0:T(8,128)(2,1)}, u32[]{:S(2)}) copy-start(bf16[2048,512]{1,0:T(8,128)(2,1)} %table_ref.1) | copy-start | bytes 6291460
  22.0 19.1 %copy-start.2 = (bf16[512,2048]{1,0:T(8,128)(2,1)S(1)}, bf16[512,2048]{1,0:T(8,128)(2,1)}, u32[]{:S(2)}) copy-start(bf16[512,2048]{1,0:T(8,128)(2,1)} %w_proj_ref.1) | copy-start | bytes 6291460
  22.0 19.1 %copy-start.3 = (bf16[512,512]{1,0:T(8,128)(2,1)S(1)}, bf16[512,512]{1,0:T(8,128)(2,1)}, u32[]{:S(2)}) copy-start(bf16[512,512]{1,0:T(8,128)(2,1)} %w_out_ref.1) | copy-start | bytes 1572868
  22.0 19.1 %copy-start.4 = (bf16[1,256,512]{2,1,0:T(8,128)(2,1)S(1)}, bf16[1,256,512]{2,1,0:T(8,128)(2,1)}, u32[]{:S(2)}) copy-start(bf16[1,256,512]{2,1,0:T(8,128)(2,1)} %param.12) | copy-start | bytes 786436
  22.0 19.1 %copy-start.5 = (f32[512]{0:T(512)S(1)}, f32[512]{0:T(512)}, u32[]{:S(2)}) copy-start(f32[512]{0:T(512)} %param.15) | copy-start | bytes 6148
  22.0 19.1 %copy-start.6 = (s32[1,1,4]{2,1,0:T(1,128)S(1)}, s32[1,1,4]{2,1,0:T(1,128)}, u32[]{:S(2)}) copy-start(s32[1,1,4]{2,1,0:T(1,128)} %param.11) | copy-start | bytes 52
  46.6 6.4 %copy-start = (bf16[512,512]{1,0:T(8,128)(2,1)}, bf16[512,512]{1,0:T(8,128)(2,1)S(1)}, u32[]{:S(2)}) copy-start(bf16[512,512]{1,0:T(8,128)(2,1)S(1)} %get-tuple-element.30) | copy-start | bytes 1572868
  48.4 8.5 %collective-permute-start.2 = (bf16[5136,128]{1,0:T(8,128)(2,1)}, bf16[5136,128]{1,0:T(8,128)(2,1)S(1)}, u32[]{:S(2)}, u32[]{:S(2)}) collective-permute-start(bf16[5136,128]{1,0:T(8,128)(2,1)} %get-tuple-element.35), channel_id=1, source_target_pairs={{0,1},{1,0},{2,3},{3,2},{4,5},{5,4},{6,7},{7,6},{8,9},{9,8},{10,11... | collective-permute-start | bytes 3944456 | tf_op jit(solution)/shard_map/ppermute | solution.py:473
  53.0 21.0 %all-to-all-start.2 = ((bf16[32,16,512]{2,1,0:T(8,128)(2,1)}), bf16[32,16,512]{2,1,0:T(8,128)(2,1)S(1)}, u32[]{:S(2)}, u32[]{:S(2)}) async-start(bf16[32,16,512]{2,1,0:T(8,128)(2,1)} %bitcast.19), calls=%async_computation.2 | async-start | bytes 1048576 | tf_op jit(solution)/shard_map/all_to_all | solution.py:469
  57.3 7.6 %collective-permute-start.3 = (bf16[1296,128]{1,0:T(8,128)(2,1)S(1)}, bf16[1296,128]{1,0:T(8,128)(2,1)S(1)}, u32[]{:S(2)}, u32[]{:S(2)}) collective-permute-start(bf16[1296,128]{1,0:T(8,128)(2,1)S(1)} %get-tuple-element.37), channel_id=1, source_target_pairs={{0,8},{1,3},{2,10},{3,5},{4,12},{5,7},{6,14},{7,1},{8,16},{9,11},{... | collective-permute-start | bytes 995336 | tf_op jit(solution)/shard_map/ppermute | solution.py:475
  58.6 11.0 %collective-permute-start.4 = (bf16[1296,128]{1,0:T(8,128)(2,1)S(1)}, bf16[1296,128]{1,0:T(8,128)(2,1)S(1)}, u32[]{:S(2)}, u32[]{:S(2)}) collective-permute-start(bf16[1296,128]{1,0:T(8,128)(2,1)S(1)} %get-tuple-element.38), channel_id=1, source_target_pairs={{0,16},{1,5},{2,18},{3,7},{4,20},{5,1},{6,22},{7,3},{8,24},{9,13},... | collective-permute-start | bytes 995336 | tf_op jit(solution)/shard_map/ppermute | solution.py:475
  61.3 8.4 %collective-permute-start.5 = (bf16[1296,128]{1,0:T(8,128)(2,1)S(1)}, bf16[1296,128]{1,0:T(8,128)(2,1)S(1)}, u32[]{:S(2)}, u32[]{:S(2)}) collective-permute-start(bf16[1296,128]{1,0:T(8,128)(2,1)S(1)} %get-tuple-element.39), channel_id=1, source_target_pairs={{0,24},{1,7},{2,26},{3,1},{4,28},{5,3},{6,30},{7,5},{8,0},{9,15},{... | collective-permute-start | bytes 995336 | tf_op jit(solution)/shard_map/ppermute | solution.py:475
  73.9 15.8 %all-to-all-start.3 = ((bf16[32,48,128]{2,1,0:T(8,128)(2,1)}), bf16[32,48,128]{2,1,0:T(8,128)(2,1)S(1)}, u32[]{:S(2)}, u32[]{:S(2)}) async-start(bf16[32,48,128]{2,1,0:T(8,128)(2,1)} %shard_map.124.after_ref), calls=%async_computation.3 | async-start | bytes 786432 | tf_op jit(solution)/shard_map/all_to_all | solution.py:405
  79.5 7.1 %collective-permute-start.1 = (bf16[512,512]{1,0:T(8,128)(2,1)S(1)}, bf16[512,512]{1,0:T(8,128)(2,1)S(1)}, u32[]{:S(2)}, u32[]{:S(2)}) collective-permute-start(bf16[512,512]{1,0:T(8,128)(2,1)S(1)} %bitcast.17), channel_id=1, source_target_pairs={{0,1},{1,0},{2,3},{3,2},{4,5},{5,4},{6,7},{7,6},{8,9},{9,8},{10,11... | collective-permute-start | bytes 1572872 | tf_op jit(solution)/shard_map/ppermute | solution.py:483
  85.1 1.6 %collective-permute-start = (s32[32,16]{1,0:T(8,128)S(1)}, s32[32,16]{1,0:T(8,128)S(1)}, u32[]{:S(2)}, u32[]{:S(2)}) collective-permute-start(s32[32,16]{1,0:T(8,128)S(1)} %bitcast.23), channel_id=1, source_target_pairs={{0,1},{1,0},{2,3},{3,2},{4,5},{5,4},{6,7},{7,6},{8,9},{9,8},{10,11... | collective-permute-start | bytes 6152 | tf_op jit(solution)/shard_map/ppermute | solution.py:481
  90.6 16.7 %all-to-all-start.4 = ((bf16[32,40,128]{2,1,0:T(8,128)(2,1)}), bf16[32,40,128]{2,1,0:T(8,128)(2,1)S(1)}, u32[]{:S(2)}, u32[]{:S(2)}) async-start(bf16[32,40,128]{2,1,0:T(8,128)(2,1)} %get-tuple-element.43.after_ref), calls=%async_computation.4 | async-start | bytes 655360 | tf_op jit(solution)/shard_map/all_to_all | solution.py:405
  97.4 5.9 %collective-permute-start.6 = (bf16[256,512]{1,0:T(8,128)(2,1)S(1)}, bf16[256,512]{1,0:T(8,128)(2,1)S(1)}, u32[]{:S(2)}, u32[]{:S(2)}) collective-permute-start(bf16[256,512]{1,0:T(8,128)(2,1)S(1)} %get-tuple-element.42), channel_id=1, source_target_pairs={{0,2},{1,7},{2,4},{3,1},{4,6},{5,3},{6,0},{7,5},{8,10},{9,15},{10,... | collective-permute-start | bytes 786440 | tf_op jit(solution)/shard_map/ppermute | solution.py:488
  107.3 16.9 %collective-permute-start.11 = (bf16[1280,128]{1,0:T(8,128)(2,1)S(1)}, bf16[1280,128]{1,0:T(8,128)(2,1)S(1)}, u32[]{:S(2)}, u32[]{:S(2)}) collective-permute-start(bf16[1280,128]{1,0:T(8,128)(2,1)S(1)} %shard_map.128.refs_3_), channel_id=1, source_target_pairs={{0,24},{1,7},{2,26},{3,1},{4,28},{5,3},{6,30},{7,5},{8,0},{9,15},{... | collective-permute-start | bytes 983048 | tf_op jit(solution)/shard_map/ppermute | solution.py:518
  109.8 15.0 %collective-permute-start.10 = (bf16[1280,128]{1,0:T(8,128)(2,1)S(1)}, bf16[1280,128]{1,0:T(8,128)(2,1)S(1)}, u32[]{:S(2)}, u32[]{:S(2)}) collective-permute-start(bf16[1280,128]{1,0:T(8,128)(2,1)S(1)} %shard_map.128.refs_3_), channel_id=1, source_target_pairs={{0,16},{1,5},{2,18},{3,7},{4,20},{5,1},{6,22},{7,3},{8,24},{9,13},... | collective-permute-start | bytes 983048 | tf_op jit(solution)/shard_map/ppermute | solution.py:518
  110.3 14.6 %collective-permute-start.9 = (bf16[1280,128]{1,0:T(8,128)(2,1)S(1)}, bf16[1280,128]{1,0:T(8,128)(2,1)S(1)}, u32[]{:S(2)}, u32[]{:S(2)}) collective-permute-start(bf16[1280,128]{1,0:T(8,128)(2,1)S(1)} %shard_map.128.refs_3_), channel_id=1, source_target_pairs={{0,8},{1,3},{2,10},{3,5},{4,12},{5,7},{6,14},{7,1},{8,16},{9,11},{... | collective-permute-start | bytes 983048 | tf_op jit(solution)/shard_map/ppermute | solution.py:518
  110.9 13.3 %collective-permute-start.8 = (bf16[256,512]{1,0:T(8,128)(2,1)S(1)}, bf16[256,512]{1,0:T(8,128)(2,1)S(1)}, u32[]{:S(2)}, u32[]{:S(2)}) collective-permute-start(bf16[256,512]{1,0:T(8,128)(2,1)S(1)} %get-tuple-element.44), channel_id=1, source_target_pairs={{0,6},{1,3},{2,0},{3,5},{4,2},{5,7},{6,4},{7,1},{8,14},{9,11},{10,... | collective-permute-start | bytes 786440 | tf_op jit(solution)/shard_map/ppermute | solution.py:489
  112.4 12.4 %collective-permute-start.7 = (bf16[256,512]{1,0:T(8,128)(2,1)S(1)}, bf16[256,512]{1,0:T(8,128)(2,1)S(1)}, u32[]{:S(2)}, u32[]{:S(2)}) collective-permute-start(bf16[256,512]{1,0:T(8,128)(2,1)S(1)} %shard_map.127.refs_1_), channel_id=1, source_target_pairs={{0,2},{1,7},{2,4},{3,1},{4,6},{5,3},{6,0},{7,5},{8,10},{9,15},{10,... | collective-permute-start | bytes 786440 | tf_op jit(solution)/shard_map/ppermute | solution.py:507
  124.2 3.3 %collective-permute-start.12 = (bf16[1280,128]{1,0:T(8,128)(2,1)S(1)}, bf16[1280,128]{1,0:T(8,128)(2,1)S(1)}, u32[]{:S(2)}, u32[]{:S(2)}) collective-permute-start(bf16[1280,128]{1,0:T(8,128)(2,1)S(1)} %shard_map.128.refs_3_), channel_id=1, source_target_pairs={{0,1},{1,0},{2,3},{3,2},{4,5},{5,4},{6,7},{7,6},{8,9},{9,8},{10,11... | collective-permute-start | bytes 983048 | tf_op jit(solution)/shard_map/ppermute | solution.py:529
  124.2 3.3 %collective-permute-start.15 = (bf16[1280,128]{1,0:T(8,128)(2,1)S(1)}, bf16[1280,128]{1,0:T(8,128)(2,1)S(1)}, u32[]{:S(2)}, u32[]{:S(2)}) collective-permute-start(bf16[1280,128]{1,0:T(8,128)(2,1)S(1)} %collective-permute-done.11.refs_6_), channel_id=1, source_target_pairs={{0,1},{1,0},{2,3},{3,2},{4,5},{5,4},{6,7},{7,6},{8,9},{9,8},{10,11... | collective-permute-start | bytes 983048 | tf_op jit(solution)/shard_map/ppermute | solution.py:529
  124.8 2.8 %collective-permute-start.14 = (bf16[1280,128]{1,0:T(8,128)(2,1)S(1)}, bf16[1280,128]{1,0:T(8,128)(2,1)S(1)}, u32[]{:S(2)}, u32[]{:S(2)}) collective-permute-start(bf16[1280,128]{1,0:T(8,128)(2,1)S(1)} %collective-permute-done.10.refs_5_), channel_id=1, source_target_pairs={{0,1},{1,0},{2,3},{3,2},{4,5},{5,4},{6,7},{7,6},{8,9},{9,8},{10,11... | collective-permute-start | bytes 983048 | tf_op jit(solution)/shard_map/ppermute | solution.py:529
  124.9 4.0 %collective-permute-start.13 = (bf16[1280,128]{1,0:T(8,128)(2,1)S(1)}, bf16[1280,128]{1,0:T(8,128)(2,1)S(1)}, u32[]{:S(2)}, u32[]{:S(2)}) collective-permute-start(bf16[1280,128]{1,0:T(8,128)(2,1)S(1)} %shard_map.129.refs_4_), channel_id=1, source_target_pairs={{0,1},{1,0},{2,3},{3,2},{4,5},{5,4},{6,7},{7,6},{8,9},{9,8},{10,11... | collective-permute-start | bytes 983048 | tf_op jit(solution)/shard_map/ppermute | solution.py:529
